TPU v7x, 32 devices: a whole 2x2x4 slice. The times are simulated.
32 devices in a mesh: dp: 4 (over x, core), row: 4 (over z), col: 2 (over y).
Axes of the slice: x: 2, y: 2, z: 4, core: 2. Of those that a mesh axis runs over, the one named last changes fastest.
Arguments:
- token_ids: int32 [4, 1024], P('dp'), may hold values from 0 to 50303
- target_ids: int32 [4, 1024], P('dp'), may hold values from 0 to 50303
- included: int32 [4], P('dp'), may hold values 0 or 1
- tok_table: float32 [50304, 768], P(('col', 'row')), may hold values from -0.4330127 to 0.4330127, as said below
- pos_table: float32 [1024, 768], P('col', 'row'), may hold values from -3 to 3
- qkv_weight: float32 [768, 2304], P('row', 'col'), may hold values from -0.21875 to 0.21875
- attn_weight: float32 [768, 768], P('row', 'col'), may hold values from -1.25 to 1.25
- up_weight: float32 [768, 3072], P('row', 'col'), may hold values from -0.21875 to 0.21875
- down_weight: float32 [768, 3072], P('col', 'row'), may hold values from -0.109375 to 0.109375
- small_params: float32 [14, 768], replicated, may hold values from -3 to 3, as said below
- table_rows: float32 [50304], P(('col', 'row')), may hold values from 1.9204263e-07 to 7.6817054e-07
- table_cols: float32 [768], replicated, may hold values from 1.9204263e-07 to 7.6817054e-07
- pos_rows: float32 [1024], P('col'), may hold values from 1.9204263e-07 to 7.6817054e-07
- pos_cols: float32 [768], P('row'), may hold values from 1.9204263e-07 to 7.6817054e-07
- qkv_rows: float32 [768], P('row'), may hold values from 1.9204263e-07 to 7.6817054e-07
- qkv_cols: float32 [2304], P('col'), may hold values from 1.9204263e-07 to 7.6817054e-07
- attn_rows: float32 [768], P('row'), may hold values from 1.9204263e-07 to 7.6817054e-07
- attn_cols: float32 [768], P('col'), may hold values from 1.9204263e-07 to 7.6817054e-07
- up_rows: float32 [768], P('row'), may hold values from 1.9204263e-07 to 7.6817054e-07
- up_cols: float32 [3072], P('col'), may hold values from 1.9204263e-07 to 7.6817054e-07
- down_rows: float32 [768], P('col'), may hold values from 1.9204263e-07 to 7.6817054e-07
- down_cols: float32 [3072], P('row'), may hold values from 1.9204263e-07 to 7.6817054e-07
- small_second: float32 [14, 768], replicated, may hold values from 3.0322522e-06 to 1.2129009e-05
- table_noise: float32 [50304, 768], P(('col', 'row')), may hold values from -6 to 6
- pos_noise: float32 [1024, 768], P('col', 'row'), may hold values from -6 to 6
- qkv_noise: float32 [768, 2304], P('row', 'col'), may hold values from -6 to 6
- attn_noise: float32 [768, 768], P('row', 'col'), may hold values from -6 to 6
- up_noise: float32 [768, 3072], P('row', 'col'), may hold values from -6 to 6
- down_noise: float32 [768, 3072], P('col', 'row'), may hold values from -6 to 6
- small_noise: float32 [14, 768], replicated, may hold values from -6 to 6
Outputs:
- table_grad: float32 [50304, 768], P(('col', 'row'))
- table_rows_new: float32 [50304], P(('col', 'row'))
- table_cols_new: float32 [768], replicated
- table_new: float32 [50304, 768], P(('col', 'row'))
- pos_grad: float32 [1024, 768], P('col', 'row')
- pos_rows_new: float32 [1024], P('col')
- pos_cols_new: float32 [768], P('row')
- pos_new: float32 [1024, 768], P('col', 'row')
- qkv_grad: float32 [768, 2304], P('row', 'col')
- qkv_rows_new: float32 [768], P('row')
- qkv_cols_new: float32 [2304], P('col')
- qkv_new: float32 [768, 2304], P('row', 'col')
- attn_grad: float32 [768, 768], P('row', 'col')
- attn_rows_new: float32 [768], P('row')
- attn_cols_new: float32 [768], P('col')
- attn_new: float32 [768, 768], P('row', 'col')
- up_grad: float32 [768, 3072], P('row', 'col')
- up_rows_new: float32 [768], P('row')
- up_cols_new: float32 [3072], P('col')
- up_new: float32 [768, 3072], P('row', 'col')
- down_grad: float32 [768, 3072], P('col', 'row')
- down_rows_new: float32 [768], P('col')
- down_cols_new: float32 [3072], P('row')
- down_new: float32 [768, 3072], P('col', 'row')
- small_grad: float32 [14, 768], replicated
- small_second_new: float32 [14, 768], replicated
- small_new: float32 [14, 768], replicated
- loss_sum: float32 [], replicated
- token_count: float32 [], replicated
- example_norms: float32 [4], P('dp')
Inputs may be any that keep to these rules, and one draw needn't show every extreme that they name: `tok_table`: rows scaled by factors that differ over the vocabulary. `small_params`: gains near one, biases of both signs.
All inputs are finite; a program needn't handle non-finite values. No bound on the sum of `included` on one device may be relied on, other than what follows from the above.
Results may differ from a plain program's by a relative error of at most 0.012.
Values may be sent and summed in bfloat16 or wider, within the bound.
A program may use at most 640 MiB of HBM per device.

v0:
```python
import jax
import jax.numpy as jnp
from jax import lax
from jax.sharding import PartitionSpec as P

HEADS = 12
HEAD = 64
STEP = 10


clip_bound = 1.0
noise_mult = 0.002
sample_rate = 0.5
step_rate = 0.5


def shortened(array):
    return jax.tree.map(lambda a: a.astype(jnp.bfloat16) if a.dtype == jnp.float32 else a, array)


def row_scatter(operand):
    return lax.psum_scatter(operand, "row", scatter_dimension=3, tiled=True)


def row_gather(operand):
    return lax.all_gather(operand, "row", axis=3, tiled=True)


def width_sum(operand):
    return lax.psum(operand, "row")


def grid_sum(operand):
    return jax.tree.map(
        lambda part: part.astype(jnp.float32), lax.psum(shortened(operand), ("row", "col"))
    )


def token_gather(operand):
    return jax.tree.map(
        lambda part, own: part.astype(own.dtype),
        lax.all_gather(shortened(operand), "col", axis=1, tiled=True),
        operand,
    )


def grid_order(operand, n_row, n_col):
    ex_count, seq_len, model_dim = operand.shape
    ordered = operand.reshape(
        ex_count, n_col, seq_len // n_col, n_row, model_dim // n_row
    ).transpose(0, 3, 1, 2, 4)
    return ordered.reshape(ex_count, -1)


def grid_gather(operand, n_row, n_col):
    ex_count, tok_here, dim_here = operand.shape
    gathered = lax.all_gather(operand.reshape(ex_count, -1), ("row", "col"), axis=1, tiled=True)
    gathered = gathered.reshape(ex_count, n_row, n_col, tok_here, dim_here).transpose(0, 2, 3, 1, 4)
    return gathered.reshape(ex_count, n_col * tok_here, n_row * dim_here)


def norm_forward(inputs, gain, shift, model_dim):
    first_sum, second_sum = width_sum((jnp.sum(inputs, -1), jnp.sum(inputs * inputs, -1)))
    center = first_sum / model_dim
    spread_var = second_sum / model_dim - center * center
    inv_std = lax.rsqrt(spread_var + 1e-05)[..., None]
    normed = (inputs - center[..., None]) * inv_std
    return (normed * gain + shift, normed, inv_std)


def norm_backward(upstream, normed, inv_std, gain, model_dim):
    scaled = upstream * gain
    first_sum, second_sum = width_sum((jnp.sum(scaled, -1), jnp.sum(scaled * normed, -1)))
    result = inv_std * (
        scaled - first_sum[..., None] / model_dim - normed * second_sum[..., None] / model_dim
    )
    return (result, jnp.sum(upstream * normed, 1), jnp.sum(upstream, 1))


def gelu_tanh(inputs):
    return jax.nn.gelu(inputs, approximate=True)


def matmul_in(inputs, weight):
    return jnp.einsum("btk,kn->btn", inputs, weight, preferred_element_type=jnp.float32)


def matmul_back(grads, weight):
    return jnp.einsum("btn,kn->btk", grads, weight, preferred_element_type=jnp.float32)


def outer_sum(inputs, grads):
    return jnp.einsum("btk,btn->bkn", inputs, grads, preferred_element_type=jnp.float32)


def factor_parts(
    grad,
    rows_old,
    cols_old,
    at_rows,
    at_cols,
    keep_rows,
    keep_cols,
    parts_rows,
    parts_cols,
    decay_rate,
):
    count_rows, count_cols = grad.shape
    total_rows = count_rows * parts_rows
    total_cols = count_cols * parts_cols
    squares = grad * grad + 1e-30
    row_part = (
        decay_rate * keep_rows * rows_old + (1.0 - decay_rate) * jnp.sum(squares, 1) / total_cols
    )
    col_part = (
        decay_rate * keep_cols * cols_old + (1.0 - decay_rate) * jnp.sum(squares, 0) / total_rows
    )
    row_full = lax.dynamic_update_slice(
        jnp.zeros((total_rows,), jnp.float32), row_part, (at_rows * count_rows,)
    )
    col_full = lax.dynamic_update_slice(
        jnp.zeros((total_cols,), jnp.float32), col_part, (at_cols * count_cols,)
    )
    return (row_full, col_full)


def body(
    token_ids,
    target_ids,
    included,
    tok_table,
    pos_table,
    qkv_weight,
    attn_weight,
    up_weight,
    down_weight,
    small_params,
    table_rows,
    table_cols,
    pos_rows,
    pos_cols,
    qkv_rows,
    qkv_cols,
    attn_rows,
    attn_cols,
    up_rows,
    up_cols,
    down_rows,
    down_cols,
    small_second,
    table_noise,
    pos_noise,
    qkv_noise,
    attn_noise,
    up_noise,
    down_noise,
    small_noise,
):
    n_row = lax.axis_size("row")
    n_col = lax.axis_size("col")
    n_data = lax.axis_size("dp")
    row_at = lax.axis_index("row")
    col_at = lax.axis_index("col")
    ex_count, seq_len = token_ids.shape
    model_dim = small_params.shape[1]
    tok_here = seq_len // n_col
    dim_here = model_dim // n_row
    voc_sub = tok_table.shape[0]
    ff_dim = 4 * model_dim
    ff_here = ff_dim // n_row
    heads_here = HEADS // n_row
    decay_rate = 1.0 - STEP ** (-0.8)
    score_scale = HEAD ** (-0.5)

    def own_part(index):
        return lax.dynamic_slice_in_dim(small_params[index], row_at * dim_here, dim_here)

    up_bias = lax.dynamic_slice_in_dim(
        small_params[7:11].reshape(ff_dim), row_at * ff_here, ff_here
    )
    qkv_full_w, attn_full_w, up_full_w, down_full_w = (
        lax.all_gather(qkv_weight.astype(jnp.bfloat16), "col", axis=1, tiled=True),
        lax.all_gather(attn_weight.astype(jnp.bfloat16), "col", axis=1, tiled=True),
        lax.all_gather(up_weight.astype(jnp.bfloat16), "col", axis=1, tiled=True),
        lax.all_gather(down_weight.astype(jnp.bfloat16), "col", axis=0, tiled=True),
    )
    table_low = tok_table.astype(jnp.bfloat16)
    vocab_place = col_at * n_row + row_at
    vocab_start = vocab_place * voc_sub
    local_ids = token_ids - vocab_start
    in_mask = (local_ids >= 0) & (local_ids < voc_sub)
    inside = in_mask.astype(jnp.float32)
    safe_ids = jnp.clip(local_ids, 0, voc_sub - 1)
    looked = jnp.where(
        in_mask[..., None], jnp.take(table_low, safe_ids, axis=0), jnp.zeros((), jnp.bfloat16)
    )
    embedded = lax.psum_scatter(
        grid_order(looked, n_row, n_col), ("row", "col"), scatter_dimension=1, tiled=True
    ).astype(jnp.float32)
    stream_in = embedded.reshape(ex_count, tok_here, dim_here) + pos_table
    positions = col_at * tok_here + jnp.arange(tok_here)
    allowed = jnp.arange(seq_len)[None, :] <= positions[:, None]

    def split_heads(operand, count):
        return operand.reshape(ex_count, count, heads_here, HEAD)

    def attend_scores(queries, key_all):
        raw = jnp.einsum(
            "bqhe,bkhe->bhqk",
            split_heads(queries, tok_here),
            split_heads(key_all, seq_len),
            preferred_element_type=jnp.float32,
        )
        return jnp.where(allowed, raw * score_scale, -1e30)

    ln_one, norm_one, inv_one = norm_forward(stream_in, own_part(0), own_part(1), model_dim)
    ln_one = ln_one.astype(jnp.bfloat16)
    packed = row_scatter(matmul_in(ln_one, qkv_full_w).reshape(ex_count, tok_here, 3, model_dim))
    packed = packed + jnp.stack([own_part(2), jnp.zeros((dim_here,), jnp.float32), own_part(3)])
    packed = packed.astype(jnp.bfloat16)
    queries = packed[:, :, 0]
    key_all, value_all = token_gather((packed[:, :, 1], packed[:, :, 2]))
    scores = attend_scores(queries, key_all)
    row_max = jnp.max(scores, -1, keepdims=True)
    exp_scores = jnp.exp(scores - row_max)
    totals = jnp.sum(exp_scores, -1, keepdims=True)
    log_norm = row_max + jnp.log(totals)
    soft_probs = (exp_scores / totals).astype(jnp.bfloat16)
    attn_mixed = (
        jnp.einsum(
            "bhqk,bkhe->bqhe",
            soft_probs,
            split_heads(value_all, seq_len),
            preferred_element_type=jnp.float32,
        )
        .reshape(ex_count, tok_here, dim_here)
        .astype(jnp.bfloat16)
    )
    branch = row_scatter(
        matmul_in(attn_mixed, attn_full_w).reshape(ex_count, tok_here, 1, model_dim)
    )[:, :, 0] + own_part(4)
    stream_mid = stream_in + branch
    ln_two, norm_two, inv_two = norm_forward(stream_mid, own_part(5), own_part(6), model_dim)
    ln_two = ln_two.astype(jnp.bfloat16)
    up_pre = (
        row_scatter(matmul_in(ln_two, up_full_w).reshape(ex_count, tok_here, 1, ff_dim))[:, :, 0]
        + up_bias
    )
    up_act = gelu_tanh(up_pre).astype(jnp.bfloat16)
    down_out = row_scatter(
        matmul_back(up_act, down_full_w).reshape(ex_count, tok_here, 1, model_dim)
    )[:, :, 0] + own_part(11)
    kept = (
        ln_one,
        norm_one,
        inv_one,
        queries,
        key_all,
        value_all,
        log_norm,
        attn_mixed,
        ln_two,
        norm_two,
        inv_two,
        up_pre,
        up_act,
    )
    stream_out, kept = (stream_mid + down_out, kept)
    ln_fin, norm_fin, inv_fin = norm_forward(stream_out, own_part(12), own_part(13), model_dim)
    final_all = grid_gather(ln_fin.astype(jnp.bfloat16), n_row, n_col)
    logits = jnp.einsum("btd,vd->btv", final_all, table_low, preferred_element_type=jnp.float32)
    logit_max = lax.pmax(jnp.max(logits, -1), ("row", "col"))
    exp_logits = jnp.exp(logits - logit_max[..., None])
    hits = jnp.arange(voc_sub) == (target_ids - vocab_start)[..., None]
    exp_total, picked = grid_sum(
        (jnp.sum(exp_logits, -1), jnp.sum(jnp.where(hits, logits, 0.0), -1))
    )
    example_loss = jnp.sum(logit_max + jnp.log(exp_total) - picked, 1)
    logit_grad = (exp_logits / exp_total[..., None] - hits.astype(jnp.float32)).astype(jnp.bfloat16)
    head_terms = jnp.einsum(
        "btv,vd->btd", logit_grad, table_low, preferred_element_type=jnp.float32
    )
    final_grad = lax.psum_scatter(
        grid_order(head_terms, n_row, n_col), ("row", "col"), scatter_dimension=1, tiled=True
    ).reshape(ex_count, tok_here, dim_here)
    grad_out, gain_fin, shift_fin = norm_backward(
        final_grad, norm_fin, inv_fin, own_part(12), model_dim
    )
    (
        ln_one,
        norm_one,
        inv_one,
        queries,
        key_all,
        value_all,
        log_norm,
        attn_mixed,
        ln_two,
        norm_two,
        inv_two,
        up_pre,
        up_act,
    ) = kept
    down_grad = grad_out.astype(jnp.bfloat16)
    down_full = row_gather(down_grad[:, :, None])[:, :, 0]
    act_grad = matmul_in(down_full, down_full_w)
    pre_grad = jax.vjp(gelu_tanh, up_pre)[1](act_grad)[0].astype(jnp.bfloat16)
    up_full = row_gather(pre_grad[:, :, None])[:, :, 0]
    mid_part, gain_two, shift_two = norm_backward(
        matmul_back(up_full, up_full_w), norm_two, inv_two, own_part(5), model_dim
    )
    mid_grad = grad_out + mid_part
    branch_grad = mid_grad.astype(jnp.bfloat16)
    branch_full = row_gather(branch_grad[:, :, None])[:, :, 0]
    mixed_grad = split_heads(matmul_back(branch_full, attn_full_w).astype(jnp.bfloat16), tok_here)
    soft_probs = jnp.exp(attend_scores(queries, key_all) - log_norm)
    prob_grad = jnp.einsum(
        "bqhe,bkhe->bhqk",
        mixed_grad,
        split_heads(value_all, seq_len),
        preferred_element_type=jnp.float32,
    )
    value_part = jnp.einsum(
        "bhqk,bqhe->bkhe",
        soft_probs.astype(jnp.bfloat16),
        mixed_grad,
        preferred_element_type=jnp.float32,
    )
    score_grad = (
        soft_probs * (prob_grad - jnp.sum(prob_grad * soft_probs, -1, keepdims=True))
    ).astype(jnp.bfloat16)
    query_grad = (
        jnp.einsum(
            "bhqk,bkhe->bqhe",
            score_grad,
            split_heads(key_all, seq_len),
            preferred_element_type=jnp.float32,
        )
        * score_scale
    )
    key_part = (
        jnp.einsum(
            "bhqk,bqhe->bkhe",
            score_grad,
            split_heads(queries, tok_here),
            preferred_element_type=jnp.float32,
        )
        * score_scale
    )
    key_grad = lax.psum_scatter(
        key_part.reshape(ex_count, seq_len, dim_here).astype(jnp.bfloat16),
        "col",
        scatter_dimension=1,
        tiled=True,
    ).astype(jnp.float32)
    value_grad = lax.psum_scatter(
        value_part.reshape(ex_count, seq_len, dim_here).astype(jnp.bfloat16),
        "col",
        scatter_dimension=1,
        tiled=True,
    ).astype(jnp.float32)
    packed_grad = jnp.stack(
        [query_grad.reshape(ex_count, tok_here, dim_here), key_grad, value_grad], 2
    ).astype(jnp.bfloat16)
    packed_full = row_gather(packed_grad).reshape(ex_count, tok_here, 3 * model_dim)
    in_part, gain_one, shift_one = norm_backward(
        matmul_back(packed_full, qkv_full_w), norm_one, inv_one, own_part(0), model_dim
    )
    narrow = (
        gain_one,
        shift_one,
        jnp.sum(packed_grad[:, :, 0].astype(jnp.float32), 1),
        jnp.sum(packed_grad[:, :, 2].astype(jnp.float32), 1),
        jnp.sum(branch_grad.astype(jnp.float32), 1),
        gain_two,
        shift_two,
        jnp.sum(down_grad.astype(jnp.float32), 1),
    )
    pairs = (
        (ln_one, packed_full),
        (attn_mixed, branch_full),
        (ln_two, up_full),
        (up_act, down_full),
    )
    grad_in, narrow, up_sum, pairs = (
        mid_grad + in_part,
        narrow,
        jnp.sum(pre_grad.astype(jnp.float32), 1),
        pairs,
    )
    full_ex = [outer_sum(pairs[index][0], pairs[index][1]) for index in range(3)]
    full_ex.append(outer_sum(pairs[3][1], pairs[3][0]))
    layer_ex = list(
        (
            lax.psum_scatter(
                full_ex[0].astype(jnp.bfloat16), "col", scatter_dimension=2, tiled=True
            ).astype(jnp.float32),
            lax.psum_scatter(
                full_ex[1].astype(jnp.bfloat16), "col", scatter_dimension=2, tiled=True
            ).astype(jnp.float32),
            lax.psum_scatter(
                full_ex[2].astype(jnp.bfloat16), "col", scatter_dimension=2, tiled=True
            ).astype(jnp.float32),
            lax.psum_scatter(
                full_ex[3].astype(jnp.bfloat16), "col", scatter_dimension=1, tiled=True
            ).astype(jnp.float32),
        )
    )
    emb_grad_all = (
        grid_gather(grad_in.astype(jnp.bfloat16), n_row, n_col).astype(jnp.float32)
        * inside[..., None]
    )

    def add_rows(grads, indices):
        return jnp.zeros((voc_sub, model_dim), jnp.float32).at[indices].add(grads)

    table_ex = jnp.einsum(
        "btv,btd->bvd", logit_grad, final_all, preferred_element_type=jnp.float32
    ) + jax.vmap(add_rows)(emb_grad_all, safe_ids)
    ex_grads = [table_ex, grad_in] + layer_ex
    narrow_all = jnp.stack(list(narrow) + [gain_fin, shift_fin], 1)
    placed = lax.dynamic_update_slice(
        jnp.zeros((ex_count, 10, model_dim), jnp.float32), narrow_all, (0, 0, row_at * dim_here)
    )
    up_placed = lax.dynamic_update_slice(
        jnp.zeros((ex_count, ff_dim), jnp.float32), up_sum, (0, row_at * ff_here)
    ).reshape(ex_count, 4, model_dim)
    vec_part = jnp.concatenate([placed[:, :7], up_placed, placed[:, 7:]], 1)
    squares = sum((jnp.sum(item * item, (1, 2)) for item in ex_grads))
    weights_sq = jnp.stack(
        [
            jnp.sum(item * item)
            for item in (tok_table, pos_table, qkv_weight, attn_weight, up_weight, down_weight)
        ]
    )
    vec_total, square_total, weight_total = grid_sum((vec_part, squares, weights_sq))
    norm_sq = square_total + jnp.sum(vec_total * vec_total, (1, 2))
    example_norms = jnp.sqrt(norm_sq)
    taken = included.astype(jnp.float32)
    share = taken * jnp.minimum(1.0, clip_bound * lax.rsqrt(norm_sq + 1e-12))

    def weigh(grads):
        return jnp.tensordot(share, grads, 1, precision=lax.Precision.HIGHEST)

    sums = (
        lax.psum(weigh(ex_grads[0]).astype(jnp.bfloat16), "dp").astype(jnp.float32),
        lax.psum(weigh(ex_grads[1]).astype(jnp.bfloat16), "dp").astype(jnp.float32),
        lax.psum(weigh(ex_grads[2]).astype(jnp.bfloat16), "dp").astype(jnp.float32),
        lax.psum(weigh(ex_grads[3]).astype(jnp.bfloat16), "dp").astype(jnp.float32),
        lax.psum(weigh(ex_grads[4]).astype(jnp.bfloat16), "dp").astype(jnp.float32),
        lax.psum(weigh(ex_grads[5]).astype(jnp.bfloat16), "dp").astype(jnp.float32),
        lax.psum(weigh(vec_total).astype(jnp.bfloat16), "dp").astype(jnp.float32),
        lax.psum(jnp.sum(taken * example_loss).astype(jnp.bfloat16), "dp").astype(jnp.float32),
        lax.psum(jnp.sum(taken).astype(jnp.bfloat16), "dp").astype(jnp.float32),
    )
    divisor = sample_rate * ex_count * n_data
    plain_sums = list(sums[0:6])
    weights_in = [tok_table, pos_table, qkv_weight, attn_weight, up_weight, down_weight]
    noises = [table_noise, pos_noise, qkv_noise, attn_noise, up_noise, down_noise]
    grads_out = [
        (plain_sums[index] + noise_mult * clip_bound * noises[index]) / divisor
        for index in range(6)
    ]
    keep_row = (row_at == 0).astype(jnp.float32)
    keep_col = (col_at == 0).astype(jnp.float32)
    olds = [
        (table_rows, table_cols),
        (pos_rows, pos_cols),
        (qkv_rows, qkv_cols),
        (attn_rows, attn_cols),
        (up_rows, up_cols),
        (down_rows, down_cols),
    ]
    col_layout = (col_at, row_at, keep_row, keep_col, n_col, n_row)
    row_layout = (row_at, col_at, keep_col, keep_row, n_row, n_col)
    layouts = [
        (vocab_place, 0, 1.0, keep_row * keep_col, n_col * n_row, 1),
        col_layout,
        row_layout,
        row_layout,
        row_layout,
        col_layout,
    ]
    factor_in = []
    for index in range(6):
        at_rows, at_cols, keep_rows, keep_cols, parts_rows, parts_cols = layouts[index]
        factor_in.extend(
            factor_parts(
                grads_out[index],
                olds[index][0],
                olds[index][1],
                at_rows,
                at_cols,
                keep_rows,
                keep_cols,
                parts_rows,
                parts_cols,
                decay_rate,
            )
        )
    lengths = [item.shape[0] for item in factor_in]
    factor_full = grid_sum(jnp.concatenate(factor_in))
    offsets = [sum(lengths[:index]) for index in range(12)]
    results = []
    update_sq = []
    for index in range(6):
        at_rows, at_cols, keep_rows, keep_cols, parts_rows, parts_cols = layouts[index]
        count_rows, count_cols = grads_out[index].shape
        row_full = factor_full[offsets[2 * index] : offsets[2 * index] + lengths[2 * index]]
        col_full = factor_full[
            offsets[2 * index + 1] : offsets[2 * index + 1] + lengths[2 * index + 1]
        ]
        rows_new = lax.dynamic_slice_in_dim(row_full, at_rows * count_rows, count_rows)
        cols_new = lax.dynamic_slice_in_dim(col_full, at_cols * count_cols, count_cols)
        update = grads_out[index] * lax.rsqrt(
            rows_new[:, None] * cols_new[None, :] / jnp.mean(row_full)
        )
        update_sq.append(jnp.sum(update * update))
        results.append(
            (rows_new, cols_new, update, count_rows * parts_rows * count_cols * parts_cols)
        )
    update_total = grid_sum(jnp.stack(update_sq))
    outputs = []
    for index in range(6):
        rows_new, cols_new, update, entries = results[index]
        update = update / jnp.maximum(1.0, jnp.sqrt(update_total[index] / entries))
        size = step_rate * jnp.maximum(0.001, jnp.sqrt(weight_total[index] / entries))
        outputs.extend([grads_out[index], rows_new, cols_new, weights_in[index] - size * update])
    small_grad = (sums[6] + noise_mult * clip_bound * small_noise) / divisor
    second_new = decay_rate * small_second + (1.0 - decay_rate) * (small_grad * small_grad + 1e-30)
    small_update = small_grad * lax.rsqrt(second_new)
    small_update = small_update / jnp.maximum(1.0, jnp.sqrt(jnp.mean(small_update * small_update)))
    small_new = (
        small_params
        - step_rate
        * jnp.maximum(0.001, jnp.sqrt(jnp.mean(small_params * small_params)))
        * small_update
    )
    token_count = sums[8] * seq_len
    return (
        outputs[0],
        outputs[1],
        outputs[2],
        outputs[3],
        outputs[4],
        outputs[5],
        outputs[6],
        outputs[7],
        outputs[8],
        outputs[9],
        outputs[10],
        outputs[11],
        outputs[12],
        outputs[13],
        outputs[14],
        outputs[15],
        outputs[16],
        outputs[17],
        outputs[18],
        outputs[19],
        outputs[20],
        outputs[21],
        outputs[22],
        outputs[23],
        small_grad,
        second_new,
        small_new,
        sums[7],
        token_count,
        example_norms,
    )


def solution(mesh):
    return jax.shard_map(
        body,
        mesh=mesh,
        in_specs=(
            P("dp", None),
            P("dp", None),
            P("dp"),
            P(("col", "row"), None),
            P("col", "row"),
            P("row", "col"),
            P("row", "col"),
            P("row", "col"),
            P("col", "row"),
            P(),
            P(("col", "row")),
            P(),
            P("col"),
            P("row"),
            P("row"),
            P("col"),
            P("row"),
            P("col"),
            P("row"),
            P("col"),
            P("col"),
            P("row"),
            P(),
            P(("col", "row"), None),
            P("col", "row"),
            P("row", "col"),
            P("row", "col"),
            P("row", "col"),
            P("col", "row"),
            P(),
        ),
        out_specs=(
            P(("col", "row"), None),
            P(("col", "row")),
            P(),
            P(("col", "row"), None),
            P("col", "row"),
            P("col"),
            P("row"),
            P("col", "row"),
            P("row", "col"),
            P("row"),
            P("col"),
            P("row", "col"),
            P("row", "col"),
            P("row"),
            P("col"),
            P("row", "col"),
            P("row", "col"),
            P("row"),
            P("col"),
            P("row", "col"),
            P("col", "row"),
            P("col"),
            P("row"),
            P("col", "row"),
            P(),
            P(),
            P(),
            P(),
            P(),
            P("dp"),
        ),
        check_vma=False,
    )
```

profile of v0, /device:TPU:0, one launch (start us, length us, event | category | flops | bytes accessed | tf_op | source)
XLA Modules:
  0.0 1967.6 jit_solution(8322310072112248259)
XLA Ops:
  10.0 20.6 %multiply_reduce_fusion.2 = (bf16[]{:T(256)}, bf16[6288,768]{1,0:T(8,128)(2,1)}) fusion(f32[6288,768]{1,0:T(8,128)} %param.33), kind=kLoop, calls=%fused_computation.12 | loop fusion | flops 14487551 | bytes 28975106 | tf_op jit(solution)/shard_map/reduce_sum | solution.py:432
  61.3 22.0 %all_gather.36 = bf16[192,2304]{1,0:T(8,128)(2,1)S(1)} all-gather(bf16[192,1152]{1,0:T(8,128)(2,1)S(1)} %get-tuple-element.184), channel_id=1, replica_groups=mesh['dp'=4,'row'=4,'col'=2] {'col'}, dimensions={1}, use_global_device_ids=true | all-gather | bytes 1327104 | tf_op jit(solution)/shard_map/all_gather | solution.py:182
  83.3 108.2 %all-reduce.25.cloned.1.call-done = bf16[1,786432]{1,0:T(2,128)(2,1)} async-done(((bf16[1,786432]{1,0:T(2,128)(2,1)}), bf16[1,786432]{1,0:T(2,128)(2,1)}) %all-reduce.25.cloned.1.call-update) | async-done | bytes 1572880
  228.8 161.4 %all-reduce.27.cloned.1.call-done = f32[1,512,3,768]{1,0,2,3:T(1,128)} async-done(((f32[1,512,3,768]{1,0,2,3:T(1,128)}), f32[1,512,3,768]{1,0,2,3:T(1,128)}) %all-reduce.27.cloned.1.call-update) | async-done | bytes 4718608
  420.4 63.7 %all-reduce.29.cloned.1.call-done = f32[1,512,1,768]{1,2,0,3:T(1,128)} async-done(((f32[1,512,1,768]{1,2,0,3:T(1,128)}), f32[1,512,1,768]{1,2,0,3:T(1,128)}) %all-reduce.29.cloned.1.call-update) | async-done | bytes 1572880
  500.7 108.9 %reduce-scatter.14.cloned.1.call-done = f32[1,512,1,768]{3,1,2,0:T(8,128)} async-done(((f32[1,512,1,3072]{3,1,2,0:T(8,128)}), f32[1,512,1,768]{3,1,2,0:T(8,128)}) %reduce-scatter.14.cloned.1.call-update) | async-done | bytes 1572880 | tf_op jit(solution)/shard_map/reduce_scatter | solution.py:22
  615.5 69.5 %all-reduce.31.cloned.1.call-done = f32[1,512,1,768]{1,2,0,3:T(1,128)} async-done(((f32[1,512,1,768]{1,2,0,3:T(1,128)}), f32[1,512,1,768]{1,2,0,3:T(1,128)}) %all-reduce.31.cloned.1.call-update) | async-done | bytes 1572880
  711.3 45.2 %all-gather.16.cloned.1.call-done = bf16[1,786432]{1,0:T(2,128)(2,1)} async-done(((bf16[1,98304]{1,0:T(2,128)(2,1)}), bf16[1,786432]{1,0:T(2,128)(2,1)}) %all-gather.16.cloned.1.call-update) | async-done | bytes 1572880 | tf_op jit(solution)/shard_map/all_gather | solution.py:57
  756.5 34.8 %reduce.73 = bf16[786432]{0:T(1024)(128)(2,1)} reduce(bf16[1,786432]{1,0:T(2,128)(2,1)} %all-gather.16.cloned.1.call-done, bf16[]{:T(256)} %constant.312), dimensions={0}, to_apply=%all_gather.42.reduce_sub_computation | reduce | bytes 3145730 | tf_op jit(solution)/shard_map/all_gather | solution.py:57
  799.8 17.9 fusion.113
  817.7 19.0 pmax.7
  882.6 29.2 %reshape.1033 = bf16[2,512,6288]{1,0,2:T(2,128)(2,1)} reshape(bf16[1024,6288]{0,1:T(8,128)(2,1)} %subtract_convert_fusion) | data formatting | bytes 25755648 | tf_op jit(solution)/shard_map/reshape.513
  942.4 127.5 %all-reduce.33.cloned.1.call-done = f32[1,786432]{1,0:T(1,128)} async-done(((f32[1,786432]{1,0:T(1,128)}), f32[1,786432]{1,0:T(1,128)}) %all-reduce.33.cloned.1.call-update) | async-done | bytes 3145744
  1107.1 62.9 %all-gather.22.cloned.1.call-done = bf16[512,3072]{1,0:T(8,128)(2,1)} async-done(((bf16[512,768]{1,0:T(8,128)(2,1)}), bf16[512,3072]{1,0:T(8,128)(2,1)}) %all-gather.22.cloned.1.call-update) | async-done | bytes 3145744 | tf_op jit(solution)/shard_map/all_gather | solution.py:26
  1250.1 40.9 %all-gather.18.cloned.1.call-done = bf16[1,512,3,768]{1,3,2,0:T(8,128)(2,1)} async-done(((bf16[1,512,3,192]{1,3,2,0:T(8,128)(2,1)}), bf16[1,512,3,768]{1,3,2,0:T(8,128)(2,1)}) %all-gather.18.cloned.1.call-update) | async-done | bytes 2359312 | tf_op jit(solution)/shard_map/all_gather | solution.py:26
  1348.1 30.2 %all-gather.20.cloned.1.call-done = bf16[1,786432]{1,0:T(2,128)(2,1)} async-done(((bf16[1,98304]{1,0:T(2,128)(2,1)}), bf16[1,786432]{1,0:T(2,128)(2,1)}) %all-gather.20.cloned.1.call-update) | async-done | bytes 1572880 | tf_op jit(solution)/shard_map/all_gather | solution.py:57
  1378.2 27.3 %convert_reduce_fusion = f32[786432]{0:T(1024)S(1)} fusion(bf16[1,786432]{1,0:T(2,128)(2,1)} %all-gather.20.cloned.1.call-done), kind=kLoop, calls=%fused_computation.35 | loop fusion | flops 786432 | bytes 4718592 | tf_op jit(solution)/shard_map/convert_element_type | solution.py:410
  1419.3 21.4 %scatter_custom_fusion = f32[6288,768]{1,0:T(8,128)} fusion(f32[6288,768]{1,0:T(8,128)} %fusion.114, s32[1024]{0:T(1024)S(1)} %broadcast_select_fusion.2, f32[1,1024,768]{2,1,0:T(8,128)S(1)} %reshape.1100, f32[1024]{0:T(1024)S(1)} %bitcast.324), kind=kCustom, calls=%fused_computation.33 | custom fusion | flops 1572864 | bytes 22466560
  1456.8 35.2 %all-reduce.12 = (bf16[1]{0:T(256)(128)(2,1)}, bf16[1,14,768]{2,1,0:T(8,128)(2,1)S(1)}) all-reduce(bf16[1]{0:T(256)(128)(2,1)} %bitcast.76, bf16[1,14,768]{2,1,0:T(8,128)(2,1)S(1)} %pad_maximum_fusion.1), channel_id=1, replica_groups=mesh['dp'=4,'row'=4,'col'=2] {'row','col'}, use_global_device_ids=true, to_apply=%region_50.51 | all-reduce | flops 10753 | bytes 43012 | tf_op jit(solution)/shard_map/psum | solution.py:35
  1517.1 197.4 %all-reduce.35.cloned.1.call-done = (bf16[6288,768]{1,0:T(8,128)(2,1)}, bf16[512,192]{0,1:T(8,128)(2,1)}, bf16[192,1152]{1,0:T(8,128)(2,1)}, bf16[192,384]{1,0:T...) async-done(((bf16[6288,768]{1,0:T(8,128)(2,1)}, bf16[512,192]{0,1:T(8,128)(2,1)}, bf16[192,1152]{1,0:T(8,128)(2,1)}, bf16[192,384]{1,0:T(8,128)(2,1)}, ...) | async-done | bytes 11624464 | tf_op jit(solution)/shard_map/psum | solution.py:446
  1714.5 19.9 %fusion.1 = (f32[768]{0:T(1024)}, f32[6288]{0:T(1024)S(1)}, f32[6288,768]{1,0:T(8,128)}) fusion(f32[6288,768]{1,0:T(8,128)} %param.53, bf16[6288,768]{1,0:T(8,128)(2,1)} %get-tuple-element.144), kind=kLoop, calls=%fused_computation.15 | loop fusion | flops 38626416 | bytes 48320064 | tf_op jit(solution)/shard_map/reduce_sum | solution.py:116
  1765.7 68.4 %all-reduce.23.cloned.1.call-done = bf16[65152]{0:T(1024)(128)(2,1)} async-done(((bf16[65152]{0:T(1024)(128)(2,1)}), bf16[65152]{0:T(1024)(128)(2,1)}) %all-reduce.23.cloned.1.call-update) | async-done | bytes 130320 | tf_op jit(solution)/shard_map/psum | solution.py:35
  1877.0 20.7 %all-reduce.11 = (bf16[6]{0:T(256)(128)(2,1)}, bf16[6]{0:T(256)(128)(2,1)}, bf16[1,1024]{1,0:T(2,128)(2,1)}) all-reduce(bf16[6]{0:T(256)(128)(2,1)} %stack.127, bf16[6]{0:T(256)(128)(2,1)} %stack.134, bf16[1,1024]{1,0:T(2,128)(2,1)} %convert_element_type.488), channel_id=1, replica_groups=mesh['dp'=4,'row'=4,'col'=2] {'row','col'}, use_global_device_ids=true, to_apply=%region_89.90 | all-reduce | flops 1036 | bytes 4144 | tf_op jit(solution)/shard_map/psum | solution.py:35
  1934.9 20.9 %multiply_subtract_fusion = f32[6288,768]{1,0:T(8,128)} fusion(f32[6288,768]{1,0:T(8,128)} %param.33, f32[]{:T(128)} %bitcast.108, f32[]{:T(128)} %bitcast.101, f32[6288,768]{1,0:T(8,128)} %get-tuple-element.158, f32[]{:T(128)S(6)} %div.371, f32[768]{0:T(1024)S(1)} %copy-done.80, f32[6288]{0:T(1024)S(1)} %copy-done.59), kind=kLoop, calls=%fused_computation.9 | loop fusion | flops 28975104 | bytes 57978444 | tf_op jit(solution)/shard_map/sub | solution.py:528
  (573 shorter events, 550.6 us)
Async XLA Ops:
  8.0 183.4 %all-reduce.25.cloned.1.call-start = ((), (), s32[]{:S(2)}) async-start(), calls=%async_computation.21 | async-start | bytes 6291456
  58.5 331.6 %all-reduce.27.cloned.1.call-start = ((), (), s32[]{:S(2)}) async-start(), calls=%async_computation.22 | async-start | bytes 9437184
  219.8 264.3 %all-reduce.29.cloned.1.call-start = ((), (), s32[]{:S(2)}) async-start(), calls=%async_computation.23 | async-start | bytes 3145728
  415.5 79.9 %all-gather.12.cloned.1.call-start = ((), (), s32[]{:S(2)}) async-start(), calls=%async_computation.7 | async-start | bytes 1769472 | tf_op jit(solution)/shard_map/all_gather | solution.py:184
  418.4 82.3 %all-gather.14.cloned.1.call-start = ((), (), s32[]{:S(2)}) async-start(), calls=%async_computation.9 | async-start | bytes 1769472 | tf_op jit(solution)/shard_map/all_gather | solution.py:185
  420.1 189.4 %reduce-scatter.14.cloned.1.call-start = ((), (), s32[]{:S(2)}) async-start(), calls=%async_computation.8 | async-start | bytes 7864320 | tf_op jit(solution)/shard_map/reduce_scatter | solution.py:22
  485.5 697.4 %copy-start.6 = (f32[512,192]{0,1:T(8,128)}, f32[512,192]{0,1:T(8,128)S(1)}, u32[]{:S(2)}) copy-start(f32[512,192]{0,1:T(8,128)S(1)} %get-tuple-element.173) | copy-start | bytes 1179652
  500.5 184.5 %all-reduce.31.cloned.1.call-start = ((), (), s32[]{:S(2)}) async-start(), calls=%async_computation.24 | async-start | bytes 3145728
  615.2 141.2 %all-gather.16.cloned.1.call-start = ((), (), s32[]{:S(2)}) async-start(), calls=%async_computation.10 | async-start | bytes 3538944 | tf_op jit(solution)/shard_map/all_gather | solution.py:57
  696.3 388.1 %copy-start.72 = (f32[1,512]{1,0:T(1,128)}, f32[1,512]{1,0:T(1,128)S(1)}, u32[]{:S(2)}) copy-start(f32[1,512]{1,0:T(1,128)S(1)} %get-tuple-element.212) | copy-start | bytes 6148
  697.7 372.2 %all-reduce.33.cloned.1.call-start = ((), (), s32[]{:S(2)}) async-start(), calls=%async_computation.25 | async-start | bytes 6291456
  942.3 227.6 %all-gather.22.cloned.1.call-start = ((), (), s32[]{:S(2)}) async-start(), calls=%async_computation.18 | async-start | bytes 3932160 | tf_op jit(solution)/shard_map/all_gather | solution.py:26
  1107.0 115.5 %reduce-scatter.16.cloned.1.call-start = ((), (), s32[]{:S(2)}) async-start(), calls=%async_computation.11 | async-start | bytes 589824 | tf_op jit(solution)/shard_map/reduce_scatter | solution.py:350
  1210.6 27.8 %reduce-scatter.18.cloned.1.call-start = ((), (), s32[]{:S(2)}) async-start(), calls=%async_computation.12 | async-start | bytes 589824 | tf_op jit(solution)/shard_map/reduce_scatter | solution.py:356
  1215.5 75.6 %all-gather.18.cloned.1.call-start = ((), (), s32[]{:S(2)}) async-start(), calls=%async_computation.13 | async-start | bytes 2949120 | tf_op jit(solution)/shard_map/all_gather | solution.py:26
  1240.5 95.3 %reduce-scatter.22.cloned.1.call-start = ((), (), s32[]{:S(2)}) async-start(), calls=%async_computation.16 | async-start | bytes 1769472 | tf_op jit(solution)/shard_map/reduce_scatter | solution.py:404
  1244.0 93.9 %reduce-scatter.26.cloned.1.call-start = ((), (), s32[]{:S(2)}) async-start(), calls=%async_computation.20 | async-start | bytes 589824
  1246.0 94.5 %reduce-scatter.20.cloned.1.call-start = ((), (), s32[]{:S(2)}) async-start(), calls=%async_computation.15 | async-start | bytes 1769472 | tf_op jit(solution)/shard_map/reduce_scatter | solution.py:401
  1250.1 92.9 %reduce-scatter.24.cloned.1.call-start = ((), (), s32[]{:S(2)}) async-start(), calls=%async_computation.19 | async-start | bytes 1769472
  1301.9 76.3 %all-gather.20.cloned.1.call-start = ((), (), s32[]{:S(2)}) async-start(), calls=%async_computation.14 | async-start | bytes 3538944 | tf_op jit(solution)/shard_map/all_gather | solution.py:57
  1317.8 396.7 %all-reduce.35.cloned.1.call-start = ((), (), s32[]{:S(2)}) async-start(), calls=%async_computation.26 | async-start | bytes 23248896 | tf_op jit(solution)/shard_map/psum | solution.py:446
  1510.0 324.1 %all-reduce.23.cloned.1.call-start = ((), (), s32[]{:S(2)}) async-start(), calls=%async_computation.17 | async-start | bytes 262144 | tf_op jit(solution)/shard_map/psum | solution.py:35
  1738.0 194.7 %copy-start.3 = (f32[192,1152]{1,0:T(8,128)}, f32[192,1152]{1,0:T(8,128)S(1)}, u32[]{:S(2)}) copy-start(f32[192,1152]{1,0:T(8,128)S(1)} %get-tuple-element.156) | copy-start | bytes 2654212
  1739.2 192.6 %copy-start.23 = (f32[192,384]{1,0:T(8,128)}, f32[192,384]{1,0:T(8,128)S(1)}, u32[]{:S(2)}) copy-start(f32[192,384]{1,0:T(8,128)S(1)} %get-tuple-element.155) | copy-start | bytes 884740
  (133 other events, 3080.1 us)
Sparse Core Ops, SparseCore 0:
  58.6 132.8 all-reduce.24
  219.9 170.2 all-reduce.26
  415.6 68.4 all-reduce.28
  500.6 108.8 reduce-scatter.13
  615.3 69.6 all-reduce.30
  697.8 58.5 all-gather.15
  942.4 127.4 all-reduce.32
  1107.1 62.7 all-gather.21
  1240.6 50.4 all-gather.17
  1317.9 60.2 all-gather.19
  1764.5 69.5 all-reduce.22
Sparse Core Ops, SparseCore 1:
  418.5 21.9 all-gather.11
  442.4 22.6 all-gather.13
  1210.7 11.7 reduce-scatter.15
  1225.4 13.0 reduce-scatter.17
  1244.1 21.6 reduce-scatter.21
  1268.7 13.0 reduce-scatter.25
  1284.5 21.6 reduce-scatter.19
  1309.0 21.9 reduce-scatter.23
  1510.1 204.3 all-reduce.34
where the time goes:
time: 1980 us; the launch traced here: 1970 us
  waiting for transfers between devices  1100 us (56%)
  other arithmetic  274 us (14%)
  blocking collectives  238 us (12%)
  local copies, waits for them, and re-layouts  201 us (10%)
  matrix products  104 us (5%)
  between operations  43.9 us (2%)
    unnamed x27, waiting for transfers between devices  531 us
    psum x1, waiting for transfers between devices, body(): lax.psum(weigh(ex_grads[0]).astype(jnp.bfloat16), 'dp').astype(jnp.float32)  197 us
    reduce_scatter x1, waiting for transfers between devices, row_scatter(): return lax.psum_scatter(operand, 'row', scatter_dimension=3, tiled=True)  109 us
    all_gather x2, waiting for transfers between devices, row_gather(): return lax.all_gather(operand, 'row', axis=3, tiled=True)  104 us
    all_gather x2, waiting for transfers between devices, grid_gather(): lax.all_gather(operand.reshape(ex_count, -1), ('row', 'col'), axis=1, til...  75.3 us
    psum x3, blocking collectives, grid_sum(): lax.psum(shortened(operand), ('row', 'col'))  73.4 us
    psum x1, waiting for transfers between devices, grid_sum(): lax.psum(shortened(operand), ('row', 'col'))  68.4 us
    psum x6, blocking collectives, width_sum(): return lax.psum(operand, 'row')  57.4 us
  transfers between devices with their start and end apart: 20, of which 14 were waited for; matrix products, arithmetic and copies ran while one was open for 5% of the time, Pallas kernels for 0%

commit v1 on v0

v1 whole, which is shorter than its diff:
```python
import functools

import jax
import jax.numpy as jnp
from jax import lax
from jax.experimental import pallas as pl
from jax.experimental.pallas import tpu as pltpu
from jax.sharding import PartitionSpec as P

HEADS = 12
HEAD = 64
STEP = 10
CLIP = 1.0
NOISE = 0.002
SAMPLE = 0.5
RATE = 0.5
DECAY = 1.0 - STEP ** (-0.8)

F32 = jnp.float32
BF16 = jnp.bfloat16
PLANE = ("row", "col")
MESH = pl.DeviceIdType.MESH


def dot_f32(left, right, dims):
    return lax.dot_general(left, right, (dims, ((), ())), preferred_element_type=F32)


def mm(left, right):
    return dot_f32(left, right, ((1,), (0,)))


def mm_nt(left, right):
    return dot_f32(left, right, ((1,), (1,)))


def mm_tn(left, right):
    return dot_f32(left, right, ((0,), (0,)))


def gather_matrix(block, row_dim):
    part = lax.all_gather(block, "row", axis=row_dim, tiled=True)
    return lax.all_gather(part, "col", axis=1 - row_dim, tiled=True)


def plane_sum(array):
    return lax.psum(array, PLANE)


def example_sum(array):
    return lax.psum(array, "dp")


class Link:
    def __init__(self, send_sems, recv_sems):
        self.dp, self.row, self.col = (lax.axis_index(axis) for axis in ("dp", "row", "col"))
        self.x, self.core = self.dp // 2, self.dp % 2
        self.beside = 2 * (1 - self.x) + self.core
        self.sibling = 2 * self.x + 1 - self.core
        self.send_sems, self.recv_sems = send_sems, recv_sems
        self.n_send = 0
        self.open = []

    def device(self, **moved):
        return {"dp": self.dp, "row": self.row, "col": self.col, **moved}

    def send(self, src, dst, recv, device, when=None):
        sem = self.send_sems.at[self.n_send]
        self.n_send += 1
        copy = pltpu.make_async_remote_copy(
            src_ref=src,
            dst_ref=dst,
            send_sem=sem,
            recv_sem=self.recv_sems.at[recv],
            device_id=device,
            device_id_type=MESH,
        )
        self.open.append((copy, when))
        copy.start() if when is None else pl.when(when)(copy.start)

    def landed(self, dst, recv):
        pltpu.make_async_remote_copy(
            src_ref=dst,
            dst_ref=dst,
            send_sem=self.send_sems.at[0],
            recv_sem=self.recv_sems.at[recv],
            device_id=self.device(col=1 - self.col),
            device_id_type=MESH,
        ).wait_recv()

    def finish(self):
        for copy, when in self.open:
            copy.wait_send() if when is None else pl.when(when)(copy.wait_send)
        self.open = []

    def greet(self, devices):
        barrier = pltpu.get_barrier_semaphore()
        count = 0
        for device, when in devices:

            def signal(device=device):
                pl.semaphore_signal(barrier, inc=1, device_id=device, device_id_type=MESH)

            if when is None:
                signal()
                count = count + 1
            else:
                pl.when(when)(signal)
                count = count + when.astype(jnp.int32)
        pl.semaphore_wait(barrier, count)

    def plane_neighbours(self, n_row):
        return [
            (self.device(row=self.row + 1), self.row < n_row - 1),
            (self.device(row=self.row - 1), self.row > 0),
            (self.device(col=1 - self.col), None),
        ]


def run_together(*steps):
    steps = list(steps)
    while steps:
        for step in list(steps):
            try:
                next(step)
            except StopIteration:
                steps.remove(step)


def scatter_sum(link, base, n_row, part, from_col, ins, outs, own):
    row, col = link.row, link.col
    (up_in, down_in), (up_out, down_out) = ins, outs
    y_base, up_base, down_base = base, base + n_row, base + 2 * n_row
    order = [at for k in range(n_row // 2) for at in (n_row - 1 - k, k)]
    for at in order:
        link.send(part.at[1 - col, at], from_col.at[at], y_base + at, link.device(col=1 - col))
    yield
    for at in order:
        link.landed(from_col.at[at], y_base + at)

    def mine(at):
        return part[col, at].astype(F32) + from_col[at].astype(F32)

    for k in range(n_row - 1):
        for at, going, more, source, target, base_at, device in (
            (n_row - 1 - k, row < n_row - 1 - k, row > 0, up_in, up_out, up_base, link.device(row=row + 1)),
            (k, row > k, row < n_row - 1, down_in, down_out, down_base, link.device(row=row - 1)),
        ):

            @pl.when(going & more)
            def _():
                link.landed(source.at[at], base_at + at)
                target[at] = (mine(at) + source[at].astype(F32)).astype(BF16)

            @pl.when(going & jnp.logical_not(more))
            def _():
                target[at] = mine(at).astype(BF16)

            link.send(target.at[at], source.at[at], base_at + at, device, going)
        yield
    own[...] = mine(row)

    for more, source, base_at in ((row > 0, up_in, up_base), (row < n_row - 1, down_in, down_base)):

        @pl.when(more)
        def _():
            link.landed(source.at[row], base_at + row)
            own[...] += source[row].astype(F32)


def spread(link, base, n_row, own, place, onward=None):
    row, col = link.row, link.col
    up, down, side = (device for device, _ in link.plane_neighbours(n_row))
    here = place(row, col)
    link.send(own, here, base + row, up, row < n_row - 1)
    link.send(own, here, base + row, down, row > 0)
    link.send(own, here, base + n_row + row, side)
    yield
    for k in range(1, n_row):
        for at, there, device, further in (
            (row - k, row >= k, up, row < n_row - 1),
            (row + k, row + k < n_row, down, row > 0),
        ):
            block = place(at, col)
            pl.when(there)(functools.partial(link.landed, block, base + at))
            if k < n_row - 1:
                link.send(block, block, base + at, device, there & further)
            link.send(block, block, base + n_row + at, side, there)
            if onward is not None:
                onward(at, col, there)
        yield
    for k in range(n_row):
        for at, there in [(row - k, row >= k), (row + k, row + k < n_row)][: 2 if k else 1]:
            block = place(at, 1 - col)
            pl.when(there)(functools.partial(link.landed, block, base + n_row + at))
            if onward is not None:
                onward(at, 1 - col, there)
        if k % 2:
            yield


def spread_matrix(link, base, n_row, shard, whole, by_row, local_sems):
    row, col, at_x, at_core = link.row, link.col, link.x, link.core
    columns = shard.shape[-1]

    def block(at_row, at_col, x, core):
        lead, side = (at_row, at_col) if by_row else (at_col, at_row)
        return whole.at[lead, x, core, :, pl.ds(pl.multiple_of(side * columns, 128), columns)]

    local = []
    for index, x in enumerate((at_x, 1 - at_x)):
        copy = pltpu.make_async_copy(
            shard.at[2 * x + at_core], block(row, col, x, at_core), local_sems.at[index]
        )
        copy.start()
        local.append(copy)
    x_base, core_base = base + 2 * n_row, base + 4 * n_row
    beside, sibling = link.device(dp=link.beside), link.device(dp=link.sibling)

    def to_x(at_row, at_col, when):
        ref = block(at_row, at_col, at_x, at_core)
        link.send(ref, ref, x_base + at_col * n_row + at_row, beside, when)

    yield from spread(link, base, n_row, shard.at[link.dp], lambda r, c: block(r, c, at_x, at_core), to_x)
    for copy in local:
        copy.wait()
    ref = whole.at[:, at_x, at_core]
    link.send(ref, ref, core_base, sibling)
    yield
    for k in range(2 * n_row):
        at_row, at_col = lax.rem(row + k // 2, n_row), 1 - col if k % 2 else col
        if k:
            link.landed(block(at_row, at_col, 1 - at_x, at_core), x_base + at_col * n_row + at_row)
        if k % 2:
            yield
    ref = whole.at[:, 1 - at_x, at_core]
    link.send(ref, ref, core_base + 1, sibling)
    yield
    link.landed(whole.at[:, at_x, 1 - at_core], core_base)
    link.landed(whole.at[:, 1 - at_x, 1 - at_core], core_base + 1)


N_MATRIX = 4 * 4 + 2


def front_kernel(n_row, looked, pos, *refs):
    shards, (start, own_rows), wholes = refs[:4], refs[4:6], refs[6:10]
    from_col, up_in, down_in, up_out, down_out, own, own_low, send_sems, recv_sems, local_sems = refs[10:]
    link = Link(send_sems, recv_sems)
    link.greet(
        link.plane_neighbours(n_row)
        + [(link.device(dp=link.beside), None), (link.device(dp=link.sibling), None)]
    )

    def tokens():
        yield from scatter_sum(link, 0, n_row, looked, from_col, (up_in, down_in), (up_out, down_out), own)
        own_rows[...] = own[...].astype(BF16)
        own_low[...] = (own[...] + pos[...]).astype(BF16)
        start[link.col, link.row] = own_low[...]
        yield from spread(link, 3 * n_row, n_row, own_low, lambda r, c: start.at[c, r])

    matrices = [
        spread_matrix(
            link, 5 * n_row + index * N_MATRIX, n_row, shards[index], wholes[index], index < 3, local_sems.at[index]
        )
        for index in range(4)
    ]
    run_together(tokens(), *matrices)
    link.finish()


def front(looked, pos, shards, n_row):
    block, width = looked.shape[2:]
    wholes = [(n_row, 2, 2) + shard.shape[1:2] + (2 * shard.shape[2],) for shard in shards[:3]]
    wholes.append((2, 2, 2) + shards[3].shape[1:2] + (n_row * shards[3].shape[2],))
    rows = pltpu.VMEM((n_row, block, width), BF16)
    vmem, hbm = pl.BlockSpec(memory_space=pltpu.VMEM), pl.BlockSpec(memory_space=pl.ANY)
    return pl.pallas_call(
        functools.partial(front_kernel, n_row),
        out_shape=[jax.ShapeDtypeStruct(looked.shape, BF16), jax.ShapeDtypeStruct((block, width), BF16)]
        + [jax.ShapeDtypeStruct(shape, BF16) for shape in wholes],
        in_specs=[vmem, vmem] + [hbm] * 4,
        out_specs=[vmem, vmem] + [hbm] * 4,
        scratch_shapes=[rows] * 5
        + [pltpu.VMEM((block, width), F32), pltpu.VMEM((block, width), BF16)]
        + [
            pltpu.SemaphoreType.DMA((220,)),
            pltpu.SemaphoreType.DMA((5 * n_row + 4 * N_MATRIX,)),
            pltpu.SemaphoreType.DMA((4, 2)),
        ],
        compiler_params=pltpu.CompilerParams(
            collective_id=1, has_side_effects=True, vmem_limit_bytes=40 * 1024 * 1024
        ),
    )(looked, pos, *shards)


def total_kernel(n_row, part, total, *refs):
    from_col, up_in, down_in, up_out, down_out, own, own_low, send_sems, recv_sems = refs
    link = Link(send_sems, recv_sems)
    link.greet(link.plane_neighbours(n_row))

    def steps():
        yield from scatter_sum(link, 0, n_row, part, from_col, (up_in, down_in), (up_out, down_out), own)
        own_low[...] = own[...].astype(BF16)
        total[link.col, link.row] = own_low[...]
        yield from spread(link, 3 * n_row, n_row, own_low, lambda r, c: total.at[c, r])

    run_together(steps())
    link.finish()


def plane_total(part, collective_id):
    n_row, block, width = part.shape[1:]
    rows = pltpu.VMEM((n_row, block, width), BF16)
    vmem = pl.BlockSpec(memory_space=pltpu.VMEM)
    return pl.pallas_call(
        functools.partial(total_kernel, n_row),
        out_shape=jax.ShapeDtypeStruct(part.shape, BF16),
        in_specs=[vmem],
        out_specs=vmem,
        scratch_shapes=[rows] * 5
        + [pltpu.VMEM((block, width), F32), pltpu.VMEM((block, width), BF16)]
        + [pltpu.SemaphoreType.DMA((40,)), pltpu.SemaphoreType.DMA((5 * n_row,))],
        compiler_params=pltpu.CompilerParams(
            collective_id=collective_id, has_side_effects=True, vmem_limit_bytes=40 * 1024 * 1024
        ),
    )(part)


QUERIES = 256


def causal(scores):
    keys = lax.broadcasted_iota(jnp.int32, scores.shape, 0)
    queries = lax.broadcasted_iota(jnp.int32, scores.shape, 1)
    return jnp.where(keys <= queries, scores, -1e30)


def attend_kernel(q_ref, k_ref, v_ref, o_ref, log_ref):
    length = q_ref.shape[0]
    for head in range(2):
        lanes = slice(head * HEAD, (head + 1) * HEAD)
        keys, values = k_ref[:, lanes], v_ref[:, lanes].T
        for at in range(0, length, QUERIES):
            here = slice(at, at + QUERIES)
            queries = q_ref[here, lanes] * HEAD ** (-0.5)
            edge = causal(mm_nt(keys[here], queries))
            top = jnp.max(edge, 0, keepdims=True)
            if at:
                before = mm_nt(keys[:at], queries)
                top = jnp.maximum(top, jnp.max(before, 0, keepdims=True))
            edge = jnp.exp(edge - top)
            count = jnp.sum(edge, 0, keepdims=True)
            mixed = mm(values[:, here], edge.astype(BF16))
            if at:
                before = jnp.exp(before - top)
                count = count + jnp.sum(before, 0, keepdims=True)
                mixed = mixed + mm(values[:, :at], before.astype(BF16))
            o_ref[here, lanes] = (mixed / count).T.astype(BF16)
            log_ref[0, head : head + 1, here] = top + jnp.log(count)


def attend(packed):
    length, width = packed.shape[0], packed.shape[1] // 3
    pairs = HEADS // 2
    lanes = 2 * HEAD
    column = lambda first: pl.BlockSpec((length, lanes), lambda i: (0, first + i))
    return pl.pallas_call(
        attend_kernel,
        grid=(pairs,),
        out_shape=[
            jax.ShapeDtypeStruct((length, width), BF16),
            jax.ShapeDtypeStruct((pairs, 2, length), F32),
        ],
        in_specs=[column(0), column(pairs), column(2 * pairs)],
        out_specs=[column(0), pl.BlockSpec((1, 2, length), lambda i: (i, 0, 0))],
        compiler_params=pltpu.CompilerParams(vmem_limit_bytes=40 * 1024 * 1024),
    )(packed, packed, packed)


def attend_back_kernel(q_ref, k_ref, v_ref, g_ref, log_ref, out_ref, key_sum, value_sum):
    length = q_ref.shape[0]
    for head in range(2):
        lanes = slice(head * HEAD, (head + 1) * HEAD)
        keys, values = k_ref[:, lanes], v_ref[:, lanes]
        keys_turned = keys.T
        key_sum[...] = jnp.zeros_like(key_sum)
        value_sum[...] = jnp.zeros_like(value_sum)
        for at in range(0, length, QUERIES):
            here, seen = slice(at, at + QUERIES), slice(0, at + QUERIES)
            queries, grads = q_ref[here, lanes] * HEAD ** (-0.5), g_ref[here, lanes]
            log_norm = log_ref[0, head : head + 1, here]
            probs = jnp.exp(causal(mm_nt(keys[here], queries)) - log_norm)
            if at:
                probs = jnp.concatenate([jnp.exp(mm_nt(keys[:at], queries) - log_norm), probs], 0)
            prob_grad = mm_nt(values[seen], grads)
            level = jnp.sum(probs * prob_grad, 0, keepdims=True)
            score_grad = (probs * (prob_grad - level)).astype(BF16)
            value_sum[seen] += mm(probs.astype(BF16), grads)
            key_sum[seen] += mm(score_grad, queries)
            query_grad = mm(keys_turned[:, seen], score_grad) * HEAD ** (-0.5)
            out_ref[0, here, lanes] = query_grad.T.astype(BF16)
        out_ref[1, :, lanes] = key_sum[...].astype(BF16)
        out_ref[2, :, lanes] = value_sum[...].astype(BF16)


def attend_back(packed, mixed_grad, log_norm):
    length, width = mixed_grad.shape
    pairs = HEADS // 2
    lanes = 2 * HEAD
    column = lambda first: pl.BlockSpec((length, lanes), lambda i: (0, first + i))
    return pl.pallas_call(
        attend_back_kernel,
        grid=(pairs,),
        out_shape=jax.ShapeDtypeStruct((3, length, width), BF16),
        in_specs=[column(0), column(pairs), column(2 * pairs), column(0)]
        + [pl.BlockSpec((1, 2, length), lambda i: (i, 0, 0))],
        out_specs=pl.BlockSpec((3, length, lanes), lambda i: (0, 0, i)),
        scratch_shapes=[pltpu.VMEM((length, HEAD), F32)] * 2,
        compiler_params=pltpu.CompilerParams(vmem_limit_bytes=48 * 1024 * 1024),
    )(packed, packed, packed, mixed_grad, log_norm)


def norm_forward(inputs, gain, shift):
    center = jnp.mean(inputs, -1, keepdims=True)
    var = jnp.mean(inputs * inputs, -1, keepdims=True) - center * center
    inv = lax.rsqrt(var + 1e-05)
    normed = (inputs - center) * inv
    return (normed * gain + shift).astype(BF16), normed, inv


def norm_backward(upstream, normed, inv, gain):
    scaled = upstream * gain
    first = jnp.mean(scaled, -1, keepdims=True)
    second = jnp.mean(scaled * normed, -1, keepdims=True)
    result = inv * (scaled - first - normed * second)
    return result, jnp.sum(upstream * normed, 0), jnp.sum(upstream, 0)


def gelu_tanh(inputs):
    return jax.nn.gelu(inputs, approximate=True)


def body(
    token_ids,
    target_ids,
    included,
    tok_table,
    pos_table,
    qkv_weight,
    attn_weight,
    up_weight,
    down_weight,
    small_params,
    table_rows,
    table_cols,
    pos_rows,
    pos_cols,
    qkv_rows,
    qkv_cols,
    attn_rows,
    attn_cols,
    up_rows,
    up_cols,
    down_rows,
    down_cols,
    small_second,
    table_noise,
    pos_noise,
    qkv_noise,
    attn_noise,
    up_noise,
    down_noise,
    small_noise,
):
    n_row = lax.axis_size("row")
    n_col = lax.axis_size("col")
    n_data = lax.axis_size("dp")
    row_at = lax.axis_index("row")
    col_at = lax.axis_index("col")
    ids, targets = token_ids[0], target_ids[0]
    length = ids.shape[0]
    width = small_params.shape[1]
    vocab_here = tok_table.shape[0]
    vocab_start = (col_at * n_row + row_at) * vocab_here
    small = small_params

    weights_in = [tok_table, pos_table, qkv_weight, attn_weight, up_weight, down_weight]
    noises = [table_noise, pos_noise, qkv_noise, attn_noise, up_noise, down_noise]
    weight_sq = jnp.stack([jnp.sum(item * item) for item in weights_in])
    table_low = tok_table.astype(BF16)

    local_ids = ids - vocab_start
    inside = (local_ids >= 0) & (local_ids < vocab_here)
    safe_ids = jnp.clip(local_ids, 0, vocab_here - 1)
    looked = jnp.where(inside[:, None], jnp.take(table_low, safe_ids, axis=0), jnp.zeros((), BF16))
    tuned = (n_data, n_row, n_col) == (4, 4, 2)
    block = length // (n_row * n_col)
    lows = [item.astype(BF16) for item in weights_in[2:]]
    if tuned:
        pos_blocks = pos_table.reshape(n_row, block, -1)
        pieces = []
        for k in range(n_row):
            piece = lax.dynamic_index_in_dim(pos_blocks, row_at ^ k, 0, False)
            if k:
                piece = lax.ppermute(piece, "row", [(at, at ^ k) for at in range(n_row)])
            pieces.append(piece)
        pieces = jnp.stack(pieces)
        pos_own = jnp.concatenate([pieces[row_at ^ at] for at in range(n_row)], 1)
        shards = [item.reshape(n_data, -1, item.shape[1]) for item in lows]
        start, own_rows, qkv_full, attn_full, up_full, down_full = front(
            looked.reshape(n_col, n_row, block, width), pos_own, shards, n_row
        )
        stream_in = start.reshape(length, width).astype(F32)
        qkv_full, attn_full, up_full, down_full = (
            item.reshape(width, -1) for item in (qkv_full, attn_full, up_full, down_full)
        )
    else:
        stream_in = plane_sum(looked).astype(F32) + gather_matrix(pos_table, 1)
        qkv_full, attn_full, up_full = (gather_matrix(item, 0) for item in lows[:3])
        down_full = gather_matrix(lows[3], 1)

    ln_one, norm_one, inv_one = norm_forward(stream_in, small[0], small[1])
    bias = jnp.concatenate([small[2], jnp.zeros_like(small[2]), small[3]])
    packed = (mm(ln_one, qkv_full) + bias).astype(BF16)
    mixed, log_norm = attend(packed)
    stream_mid = stream_in + mm(mixed, attn_full) + small[4]
    ln_two, norm_two, inv_two = norm_forward(stream_mid, small[5], small[6])
    up_pre = mm(ln_two, up_full) + small[7:11].reshape(-1)
    up_act = gelu_tanh(up_pre).astype(BF16)
    stream_out = stream_mid + mm_nt(up_act, down_full) + small[11]
    ln_fin, norm_fin, inv_fin = norm_forward(stream_out, small[12], small[13])

    logits = mm_nt(table_low, ln_fin)
    top = jnp.max(logits, 0)
    hits = jnp.arange(vocab_here)[:, None] == (targets - vocab_start)[None, :]
    picked_here = jnp.sum(jnp.where(hits, logits, 0.0), 0)
    all_top = lax.pmax(top, PLANE)
    exp_logits = jnp.exp(logits - all_top[None, :])
    exp_total, picked = plane_sum((jnp.sum(exp_logits, 0), picked_here))
    loss = jnp.sum(all_top + jnp.log(exp_total) - picked)
    logit_grad = (exp_logits / exp_total[None, :] - hits.astype(F32)).astype(BF16)
    final_part = mm_tn(logit_grad, table_low).astype(BF16)
    if tuned:
        final_part = plane_total(final_part.reshape(n_col, n_row, block, width), 2)
        final_grad = final_part.reshape(length, width).astype(F32)
    else:
        final_grad = plane_sum(final_part).astype(F32)
    table_ex = mm(logit_grad, ln_fin)

    grad_out, gain_fin, shift_fin = norm_backward(final_grad, norm_fin, inv_fin, small[12])
    down_grad = grad_out.astype(BF16)
    act_grad = mm(down_grad, down_full)
    pre_grad = jax.vjp(gelu_tanh, up_pre)[1](act_grad)[0].astype(BF16)
    mid_part, gain_two, shift_two = norm_backward(mm_nt(pre_grad, up_full), norm_two, inv_two, small[5])
    mid_grad = grad_out + mid_part
    branch_grad = mid_grad.astype(BF16)
    mixed_grad = mm_nt(branch_grad, attn_full).astype(BF16)
    packed_grad = attend_back(packed, mixed_grad, log_norm)
    packed_grad = packed_grad.transpose(1, 0, 2).reshape(length, -1)
    in_part, gain_one, shift_one = norm_backward(mm_nt(packed_grad, qkv_full), norm_one, inv_one, small[0])
    grad_in = mid_grad + in_part

    def columns_of(array, at, parts):
        size = array.shape[1] // parts
        return lax.dynamic_slice_in_dim(array, at * size, size, 1)

    layer_ex = [
        mm_tn(columns_of(left, at_left, n_left), columns_of(right, at_right, n_right))
        for left, at_left, n_left, right, at_right, n_right in (
            (ln_one, row_at, n_row, packed_grad, col_at, n_col),
            (mixed, row_at, n_row, branch_grad, col_at, n_col),
            (ln_two, row_at, n_row, pre_grad, col_at, n_col),
            (down_grad, col_at, n_col, up_act, row_at, n_row),
        )
    ]
    tok_here, dim_here = pos_table.shape
    pos_ex = lax.dynamic_slice(grad_in, (col_at * tok_here, row_at * dim_here), (tok_here, dim_here))
    column = lambda item: jnp.sum(item.astype(F32), 0)
    packed_sums = column(packed_grad).reshape(3, width)
    small_ex = jnp.stack(
        [gain_one, shift_one, packed_sums[0], packed_sums[2], column(branch_grad), gain_two, shift_two]
        + list(column(pre_grad).reshape(-1, width))
        + [column(down_grad), gain_fin, shift_fin]
    )
    emb_grad = jnp.where(inside[:, None], grad_in.astype(BF16).astype(F32), 0.0)
    table_ex = table_ex + jnp.zeros_like(table_ex).at[safe_ids].add(emb_grad)

    own_sq = sum(jnp.sum(item * item) for item in [table_ex] + layer_ex)
    total = plane_sum(jnp.concatenate([weight_sq, own_sq[None]]))
    weight_total = total[:6]
    norm_sq = total[6] + jnp.sum(grad_in * grad_in) + jnp.sum(small_ex * small_ex)
    example_norm = jnp.sqrt(norm_sq)
    taken = included[0].astype(F32)
    share = taken * jnp.minimum(1.0, CLIP * lax.rsqrt(norm_sq + 1e-12))

    sums = [
        example_sum((share * item).astype(BF16)).astype(F32)
        for item in [table_ex, pos_ex] + layer_ex + [small_ex]
    ]
    loss_sum, taken_sum = example_sum(jnp.stack([taken * loss, taken]))
    divisor = SAMPLE * n_data
    grads = [(sums[index] + NOISE * CLIP * noises[index]) / divisor for index in range(6)]

    olds = [
        (table_rows, table_cols),
        (pos_rows, pos_cols),
        (qkv_rows, qkv_cols),
        (attn_rows, attn_cols),
        (up_rows, up_cols),
        (down_rows, down_cols),
    ]
    axes = [(PLANE, None), ("col", "row"), ("row", "col"), ("row", "col"), ("row", "col"), ("col", "row")]
    outputs = []
    for index in range(6):
        grad, (old_rows, old_cols), (rows_over, cols_over) = grads[index], olds[index], axes[index]
        squares = grad * grad + 1e-30
        row_sum, col_sum = jnp.sum(squares, 1), jnp.sum(squares, 0)
        n_rows, n_cols = grad.shape[0] * lax.axis_size(rows_over), grad.shape[1]
        if cols_over is not None:
            n_cols = n_cols * lax.axis_size(cols_over)
            row_sum = lax.psum(row_sum, cols_over)
        col_sum = lax.psum(col_sum, rows_over)
        rows_new = DECAY * old_rows + (1.0 - DECAY) * (row_sum / n_cols)
        cols_new = DECAY * old_cols + (1.0 - DECAY) * (col_sum / n_rows)
        row_mean = lax.psum(jnp.sum(rows_new), rows_over) / n_rows
        update = grad * lax.rsqrt(rows_new[:, None] * cols_new[None, :] / row_mean)
        update_total = lax.psum(jnp.sum(update * update), PLANE)
        entries = n_rows * n_cols
        size = RATE * jnp.maximum(1e-3, jnp.sqrt(weight_total[index] / entries))
        size = size / jnp.maximum(1.0, jnp.sqrt(update_total / entries))
        outputs.extend([grad, rows_new, cols_new, weights_in[index] - size * update])
    small_grad = (sums[6] + NOISE * CLIP * small_noise) / divisor
    second_new = DECAY * small_second + (1.0 - DECAY) * (small_grad * small_grad + 1e-30)
    small_update = small_grad * lax.rsqrt(second_new)
    small_update = small_update / jnp.maximum(1.0, jnp.sqrt(jnp.mean(small_update * small_update)))
    small_size = RATE * jnp.maximum(1e-3, jnp.sqrt(jnp.mean(small_params * small_params)))
    small_new = small_params - small_size * small_update
    return tuple(outputs) + (
        small_grad,
        second_new,
        small_new,
        loss_sum,
        taken_sum * length,
        example_norm[None],
    )


def solution(mesh):
    table, by_col, by_row = P(("col", "row"), None), P("col", "row"), P("row", "col")
    return jax.shard_map(
        body,
        mesh=mesh,
        in_specs=(P("dp", None), P("dp", None), P("dp"))
        + (table, by_col, by_row, by_row, by_row, by_col, P())
        + (P(("col", "row")), P(), P("col"), P("row"))
        + (P("row"), P("col")) * 3
        + (P("col"), P("row"), P())
        + (table, by_col, by_row, by_row, by_row, by_col, P()),
        out_specs=(table, P(("col", "row")), P(), table)
        + (by_col, P("col"), P("row"), by_col)
        + (by_row, P("row"), P("col"), by_row) * 3
        + (by_col, P("col"), P("row"), by_col)
        + (P(), P(), P(), P(), P(), P("dp")),
        check_vma=False,
    )
```

time: 1980 us -> 1000 us (0.51)
  waiting for transfers between devices: 1100 us -> 184 us
  Pallas kernels: 0 us -> 220 us
  local copies, waits for them, and re-layouts: 201 us -> 39.4 us
  blocking collectives: 238 us -> 145 us
  other arithmetic: 274 us -> 229 us
  matrix products: 104 us -> 132 us
    unnamed x27 -> x1, waiting for transfers between devices: 531 us -> 0.02 us
    pallas_call x0 -> x4, Pallas kernels: none -> 220 us  [the longest x1 110 us: front(): pl.pallas_call(functools.partial(front_kernel, n_row), out_shape=[jax.Sha...]
    all_gather x6 -> x0, waiting for transfers between devices: 179 us -> none  [the longest x2 104 us: row_gather(): return lax.all_gather(operand, 'row', axis=3, tiled=True)]
    reduce_scatter x5 -> x0, waiting for transfers between devices: 129 us -> none  [the longest x1 109 us: row_scatter(): return lax.psum_scatter(operand, 'row', scatter_dimension=3, tiled=True)]
    psum x2 -> x1, waiting for transfers between devices: 266 us -> 184 us  [example_sum(): return lax.psum(array, 'dp')]
    all_gather x6 -> x0, blocking collectives: 76.1 us -> none  [the longest x2 34.5 us: row_gather(): return lax.all_gather(operand, 'row', axis=3, tiled=True)]
    unnamed x302 -> x165, local copies, waits for them, and re-layouts: 54.2 us -> 1.45 us
    another operation x14 -> x15, local copies, waits for them, and re-layouts: 38.3 us -> 1.48 us  [the longest x1 1.34 us: body(): loss_sum, taken_sum = example_sum(jnp.stack([taken * loss, taken]))]
  transfers between devices with their start and end apart: 20 -> 4, of which waited for: 14 -> 1; matrix products, arithmetic and copies ran while one was open for 5% -> 4% of each run, Pallas kernels for 0% -> 0%
where the time goes in v1:
time: 1000 us; the launch traced here: 995 us
  other arithmetic  229 us (23%)
  Pallas kernels  220 us (22%)
  waiting for transfers between devices  184 us (18%)
  blocking collectives  145 us (14%)
  matrix products  132 us (13%)
  local copies, waits for them, and re-layouts  39.4 us (4%)
  between operations  39 us (4%)
    psum x1, waiting for transfers between devices, example_sum(): return lax.psum(array, 'dp')  184 us
    dot_general x15, matrix products, dot_f32(): lax.dot_general(left, right, (dims, ((), ())), preferred_element_type=F32)  132 us
    pallas_call x1, Pallas kernels, front(): pl.pallas_call(functools.partial(front_kernel, n_row), out_shape=[jax.Sha...  110 us
    pallas_call x1, Pallas kernels, plane_total(): pl.pallas_call(functools.partial(total_kernel, n_row), out_shape=jax.Shap...  53.4 us
    psum x2, blocking collectives, plane_sum(): return lax.psum(array, PLANE)  40.4 us
    pallas_call x1, Pallas kernels, attend_back(): pl.pallas_call(attend_back_kernel, grid=(pairs,), out_shape=jax.ShapeDtyp...  34.8 us
    reduce_sum x6, other arithmetic, body(): row_sum, col_sum = (jnp.sum(squares, 1), jnp.sum(squares, 0))  31.1 us
    sub x6, other arithmetic, body(): weights_in[index] - size * update  30.1 us
  transfers between devices with their start and end apart: 4, of which 1 were waited for; matrix products, arithmetic and copies ran while one was open for 4% of the time, Pallas kernels for 0%

profile of v1, /device:TPU:0, one launch (start us, length us, event | category | flops | bytes accessed | tf_op | source)
XLA Modules:
  0.0 994.6 jit_solution(2999756895575807399)
XLA Ops:
  22.0 20.2 %multiply_reduce_fusion.2 = (f32[]{:T(128)}, bf16[6288,768]{1,0:T(8,128)(2,1)}) fusion(f32[6288,768]{1,0:T(8,128)} %param.33), kind=kLoop, calls=%fused_computation.16 | loop fusion | flops 14487551 | bytes 28975108 | tf_op jit(solution)/shard_map/reduce_sum | solution.py:490
  58.8 110.0 %shard_map.517 = (bf16[2,4,128,768]{3,2,1,0:T(8,128)(2,1)S(1)}, bf16[128,768]{1,0:T(8,128)(2,1)}, bf16[4,2,2,48,2304]{4,3,2,1,0:T(8,128)(2,1)S(1)}, bf16[4,2,2,4...) custom-call(bf16[2,4,128,768]{3,2,1,0:T(8,128)(2,1)S(1)} %select_select_fusio, ...), custom_call_target="tpu_custom_call" | custom-call | tf_op jit(solution)/shard_map/pallas_call | solution.py:278
  175.3 22.0 %shard_map.518 = (bf16[1024,768]{1,0:T(8,128)(2,1)S(1)}, f32[6,2,1024]{2,1,0:T(2,128)S(1)}) custom-call(bf16[1024,2304]{1,0:T(8,128)(2,1)S(1)} %add_convert_fusion.q_ref.k_ref.v_ref, bf16[1024,2304]{1,0:T(8,128)(2,1)S(1)} %add_convert_fusion.q_ref.k_ref.v_ref, bf16[1024,2304]{1,0:T(8,128)(2,1)S(1)} %add_convert_fusion.q_ref.k_ref.v_ref), custom_call_target="tpu_custom_call" | custom-call | tf_op jit(solution)/shard_map/pallas_call | solution.py:368
  204.3 12.3 %multiply_convert_fusion.1 = (bf16[1024,3072]{1,0:T(8,128)(2,1)}, f32[1024,3072]{1,0:T(8,128)}) fusion(f32[3072]{0:T(1024)S(1)} %add.401, bf16[1024,768]{0,1:T(8,128)(2,1)S(1)} %add_convert_fusion.2, bf16[768,3072]{1,0:T(8,128)(2,1)S(1)} %bitcast.125), kind=kOutput, calls=%fused_computation.29 | convolution fusion | flops 4863295488 | bytes 25178112 | tf_op jit(solution)/shard_map/dot_general | solution.py:26
  224.8 14.1 %fusion.58 = (f32[1024]{0:T(1024)S(1)}, f32[1024,6288]{0,1:T(8,128)}) fusion(bf16[6288,768]{1,0:T(8,128)(2,1)S(1)} %bitcast.105, f32[1024,768]{0,1:T(8,128)S(1)} %get-tuple-element.190, f32[768]{0:T(1024)S(1)} %get-tuple-element.77, f32[768]{0:T(1024)S(1)} %get-tuple-element.76, f32[1024]{0:T(1024)S(1)} %get-tuple-element.175, f32[1024]{0:T(1024)S(1)} %get-tuple-element.174), kind=kOutput, calls=%fused_computation.212 | convolution fusion | flops 9900538880 | bytes 38578176 | tf_op jit(solution)/shard_map/dot_general | solution.py:26
  238.9 17.1 %pmax.7 = f32[1024]{0:T(1024)S(1)} all-reduce(f32[1024]{0:T(1024)S(1)} %get-tuple-element.191), channel_id=1, replica_groups=mesh['dp'=4,'row'=4,'col'=2] {'row','col'}, use_global_device_ids=true, to_apply=%region_13.14 | all-reduce | flops 1024 | bytes 8192 | tf_op jit(solution)/shard_map/pmax | solution.py:538
  256.0 12.5 %fusion.1 = (f32[1024]{0:T(1024)}, f32[1024]{0:T(1024)S(1)}) fusion(f32[1024,6288]{0,1:T(8,128)} %get-tuple-element.192, s32[1024]{0:T(1024)S(1)} %bitcast.115, f32[1024]{0:T(1024)S(1)} %pmax.7), kind=kLoop, calls=%fused_computation.5 | loop fusion | flops 32192512 | bytes 25772032 | tf_op jit(solution)/shard_map/reduce_sum | solution.py:537
  268.6 19.1 %psum.238 = f32[1024]{0:T(1024)S(1)} all-reduce(f32[1024]{0:T(1024)S(1)} %get-tuple-element.45), channel_id=1, replica_groups=mesh['dp'=4,'row'=4,'col'=2] {'row','col'}, use_global_device_ids=true, to_apply=%region_15.16 | all-reduce | flops 1024 | bytes 8192 | tf_op jit(solution)/shard_map/psum | solution.py:47
  287.7 16.1 %subtract_convert_fusion = bf16[6288,1024]{1,0:T(8,128)(2,1)} fusion(f32[1024,6288]{0,1:T(8,128)} %get-tuple-element.192, s32[1024]{0:T(1024)S(1)} %bitcast.116, f32[1024]{0:T(1024)S(1)} %psum.238, f32[1024]{0:T(1024)S(1)} %pmax.7), kind=kLoop, calls=%fused_computation.6 | loop fusion | flops 38633472 | bytes 38645760 | tf_op jit(solution)/shard_map/convert_element_type | solution.py:542
  303.9 16.2 %convolution_convert_fusion.1 = bf16[1024,768]{1,0:T(8,128)(2,1)S(1)} fusion(bf16[6288,1024]{1,0:T(8,128)(2,1)} %subtract_convert_fusion, bf16[6288,768]{1,0:T(8,128)(2,1)} %get-tuple-element.148), kind=kOutput, calls=%fused_computation.65 | convolution fusion | flops 9890955264 | bytes 24109056 | tf_op jit(solution)/shard_map/dot_general | solution.py:26
  320.1 17.4 %fusion.43 = f32[6288,768]{1,0:T(8,128)} fusion(bf16[6288,1024]{1,0:T(8,128)(2,1)} %subtract_convert_fusion, f32[1024,768]{0,1:T(8,128)S(1)} %get-tuple-element.190, f32[768]{0:T(1024)S(1)} %get-tuple-element.77, f32[768]{0:T(1024)S(1)} %get-tuple-element.76, f32[1024]{0:T(1024)S(1)} %get-tuple-element.175, f32[1024]{0:T(1024)S(1)} %get-tuple-element.174), kind=kOutput, calls=%fused_computation.198 | convolution fusion | flops 9894100992 | bytes 35354624 | tf_op jit(solution)/shard_map/dot_general | solution.py:26
  337.5 53.4 %shard_map.519 = bf16[2,4,128,768]{3,2,1,0:T(8,128)(2,1)S(1)} custom-call(bf16[2,4,128,768]{3,2,1,0:T(8,128)(2,1)S(1)} %bitcast.98), custom_call_target="tpu_custom_call" | custom-call | tf_op jit(solution)/shard_map/pallas_call | solution.py:316
  399.7 19.9 %convert_reduce_fusion = (f32[3072]{0:T(1024)}, bf16[1024,3072]{1,0:T(8,128)(2,1)}) fusion(f32[1024,3072]{1,0:T(8,128)} %get-tuple-element.189, f32[3072]{0:T(1024)S(1)} %add.401, bf16[1024,768]{0,1:T(8,128)(2,1)S(1)} %get-tuple-element.138, bf16[768,3072]{1,0:T(8,128)(2,1)} %bitcast.126), kind=kOutput, calls=%fused_computation.28 | convolution fusion | flops 4904186880 | bytes 25190400 | tf_op jit(solution)/shard_map/dot_general | solution.py:26
  435.5 34.8 %shard_map.520 = bf16[3,1024,768]{2,1,0:T(8,128)(2,1)} custom-call(bf16[1024,2304]{1,0:T(8,128)(2,1)} %copy-done, bf16[1024,2304]{1,0:T(8,128)(2,1)} %copy-done, bf16[1024,2304]{1,0:T(8,128)(2,1)} %copy-done, bf16[1024,768]{1,0:T(8,128)(2,1)S(1)} %convolution_convert_fusion.g_ref, f32[6,2,1024]{2,1,0:T(2,128)S(1)} %get-tuple-element.43.log_ref), custom_call_target="tpu_custom_call" | custom-call | tf_op jit(solution)/shard_map/pallas_call | solution.py:412
  505.6 21.8 %scatter_fusion = f32[6288,768]{1,0:T(8,128)} fusion(f32[6288,768]{1,0:T(8,128)} %fusion.43, s32[1024]{0:T(1024)S(1)} %bitcast.118, f32[1024,768]{1,0:T(8,128)} %copy.76), kind=kCustom, calls=%fused_computation.1 | custom fusion | flops 786432 | bytes 9441280 | tf_op jit(solution)/shard_map/scatter-add | solution.py:587
  527.3 12.1 %multiply_reduce_fusion.1 = f32[]{:T(128)} fusion(f32[6288,768]{1,0:T(8,128)} %scatter_fusion), kind=kLoop, calls=%fused_computation.15 | loop fusion | flops 9658367 | bytes 19316740 | tf_op jit(solution)/shard_map/reduce_sum | solution.py:589
  556.1 21.3 %psum.239 = f32[7]{0:T(128)S(1)} all-reduce(f32[7]{0:T(128)S(1)} %concatenate.11), channel_id=1, replica_groups=mesh['dp'=4,'row'=4,'col'=2] {'row','col'}, use_global_device_ids=true, to_apply=%region_28.29 | all-reduce | flops 7 | bytes 56 | tf_op jit(solution)/shard_map/psum | solution.py:47
  580.1 12.1 %multiply_convert_fusion = bf16[6288,768]{1,0:T(8,128)(2,1)} fusion(f32[6288,768]{1,0:T(8,128)} %scatter_fusion, f32[]{:T(128)S(6)} %mul.824), kind=kLoop, calls=%fused_computation.14 | loop fusion | flops 9658368 | bytes 28975108 | tf_op jit(solution)/shard_map/convert_element_type | solution.py:598
  616.1 183.9 %all-reduce.8.cloned.1.call-done = (bf16[6288,768]{1,0:T(8,128)(2,1)}, bf16[512,192]{0,1:T(8,128)(2,1)}, bf16[192,1152]{1,0:T(8,128)(2,1)}, bf16[192,384]{1,0:T(...) async-done(((bf16[6288,768]{1,0:T(8,128)(2,1)}, bf16[512,192]{0,1:T(8,128)(2,1)}, bf16[192,1152]{1,0:T(8,128)(2,1)}, bf16[192,384]{1,0:T(8,128)(2,1)}, ...) | async-done | bytes 11624464 | tf_op jit(solution)/shard_map/psum | solution.py:51
  820.7 20.2 %all-reduce.2 = (f32[512]{0:T(512)}, f32[]{:T(128)}, f32[1152]{0:T(1024)}, f32[]{:T(128)}, f32[384]{0:T(512)}, /*index=5*/f32[]{:T(128)}, f32[1536]{0:T(1024)}, f32[384]{0:T(512)}) all-reduce(f32[512]{0:T(512)} %get-tuple-element.73, f32[]{:T(128)} %get-tuple-element.128, ...), channel_id=1, replica_groups=mesh['dp'=4,'row'=4,'col'=2] {'row'}, use_global_device_ids=true, to_apply=%region_51.52 | all-reduce | flops 3971 | bytes 31768 | tf_op jit(solution)/shard_map/psum | solution.py:622
  858.8 19.9 %fusion.3 = (f32[768]{0:T(1024)}, f32[6288]{0:T(1024)S(1)}, f32[6288,768]{1,0:T(8,128)}) fusion(f32[6288,768]{1,0:T(8,128)} %param.53, bf16[6288,768]{1,0:T(8,128)(2,1)} %get-tuple-element.110), kind=kLoop, calls=%fused_computation.19 | loop fusion | flops 38626416 | bytes 48320064 | tf_op jit(solution)/shard_map/reduce_sum | solution.py:618
  879.9 19.8 %all-reduce.1 = (f32[768]{0:T(1024)}, f32[]{:T(128)}) all-reduce(f32[768]{0:T(1024)} %get-tuple-element.46, f32[]{:T(128)} %get-tuple-element.134), channel_id=1, replica_groups=mesh['dp'=4,'row'=4,'col'=2] {'row','col'}, use_global_device_ids=true, to_apply=%region_44.45 | all-reduce | flops 769 | bytes 6152 | tf_op jit(solution)/shard_map/psum | solution.py:623
  920.7 18.6 %all-reduce = (f32[]{:T(128)}, f32[]{:T(128)}, f32[]{:T(128)}, f32[]{:T(128)}, f32[]{:T(128)}, /*index=5*/f32[]{:T(128)}, f32[1024]{0:T(1024)}) all-reduce(f32[]{:T(128)} %multiply_reduce_fusion, f32[]{:T(128)} %multiply_reduce_fusion.25, f32[]{:T(128)} %multiply_reduce_fusion.22, ...), channel_id=1, replica_groups=mesh['dp'=4,'row'=4,'col'=2] {'row','col'}, use_global_device_ids=true, to_apply=%region_48.49 | all-reduce | flops 1030 | bytes 8240 | tf_op jit(solution)/shard_map/psum | solution.py:628
  963.8 20.6 %multiply_subtract_fusion = f32[6288,768]{1,0:T(8,128)} fusion(f32[6288,768]{1,0:T(8,128)} %param.33, f32[]{:T(128)S(6)} %div.260, f32[6288,768]{1,0:T(8,128)} %get-tuple-element.136, f32[]{:T(128)S(6)} %div.256, f32[768]{0:T(1024)S(1)} %copy-done.53, f32[6288]{0:T(1024)S(1)} %copy-done.38), kind=kLoop, calls=%fused_computation.9 | loop fusion | flops 24145920 | bytes 57978440 | tf_op jit(solution)/shard_map/sub | solution.py:632
  (298 shorter events, 220.1 us)
Async XLA Ops:
  7.2 792.8 %all-reduce.8.cloned.1.call-start = ((), (), s32[]{:S(2)}) async-start(), calls=%async_computation | async-start | bytes 23248896 | tf_op jit(solution)/shard_map/psum | solution.py:51
  9.5 47.9 %collective-permute-start = (f32[128,192]{1,0:T(8,128)}, f32[128,192]{1,0:T(8,128)}, u32[]{:S(2)}, u32[]{:S(2)}) collective-permute-start(f32[128,192]{1,0:T(8,128)} %bitcast.11), channel_id=1, source_target_pairs={{0,2},{2,0},{4,6},{6,4},{1,3},{3,1},{5,7},{7,5},{8,10},{10,8},{12,... | collective-permute-start | bytes 294920 | tf_op jit(solution)/shard_map/ppermute | solution.py:506
  13.3 44.2 %collective-permute-start.1 = (f32[128,192]{1,0:T(8,128)}, f32[128,192]{1,0:T(8,128)}, u32[]{:S(2)}, u32[]{:S(2)}) collective-permute-start(f32[128,192]{1,0:T(8,128)} %bitcast.13), channel_id=1, source_target_pairs={{0,4},{2,6},{4,0},{6,2},{1,5},{3,7},{5,1},{7,3},{8,12},{10,14},{12... | collective-permute-start | bytes 294920 | tf_op jit(solution)/shard_map/ppermute | solution.py:506
  16.6 40.8 %collective-permute-start.2 = (f32[128,192]{1,0:T(8,128)}, f32[128,192]{1,0:T(8,128)}, u32[]{:S(2)}, u32[]{:S(2)}) collective-permute-start(f32[128,192]{1,0:T(8,128)} %bitcast.15), channel_id=1, source_target_pairs={{0,6},{2,4},{4,2},{6,0},{1,7},{3,5},{5,3},{7,1},{8,14},{10,12},{12... | collective-permute-start | bytes 294920 | tf_op jit(solution)/shard_map/ppermute | solution.py:506
  17.4 24.8 %copy-start.54 = (s32[1024,1]{0,1:T(1,128)}, s32[1024,1]{0,1:T(1,128)S(1)}, u32[]{:S(2)}) copy-start(s32[1024,1]{0,1:T(1,128)S(1)} %get-tuple-element.145) | copy-start | bytes 12292
  18.1 38.9 %copy-start.66 = (pred[1024]{0:T(1024)(128)(4,1)}, pred[1024]{0:T(1024)(128)(4,1)S(1)}, u32[]{:S(2)}) copy-start(pred[1024]{0:T(1024)(128)(4,1)S(1)} %and_reduce_fusion) | copy-start | bytes 3076
  19.3 151.0 %copy-start.47 = (f32[768]{0:T(1024)}, f32[768]{0:T(1024)S(1)}, u32[]{:S(2)}) copy-start(f32[768]{0:T(1024)S(1)} %get-tuple-element.85) | copy-start | bytes 9220
  22.0 20.3 %copy-start.16 = (f32[192,1536]{1,0:T(8,128)S(1)}, f32[192,1536]{1,0:T(8,128)}, u32[]{:S(2)}) copy-start(f32[192,1536]{1,0:T(8,128)} %param.37) | copy-start | bytes 3538948
  22.0 21.2 %copy-start.17 = (f32[384,768]{1,0:T(8,128)S(1)}, f32[384,768]{1,0:T(8,128)}, u32[]{:S(2)}) copy-start(f32[384,768]{1,0:T(8,128)} %param.38) | copy-start | bytes 3538948
  175.3 22.1 %copy-start = (bf16[1024,2304]{1,0:T(8,128)(2,1)}, bf16[1024,2304]{1,0:T(8,128)(2,1)S(1)}, u32[]{:S(2)}) copy-start(bf16[1024,2304]{1,0:T(8,128)(2,1)S(1)} %add_convert_fusion.q_ref.k_ref.v_ref) | copy-start | bytes 14155780
  204.3 20.4 %slice-start = ((s8[9658368]{0:T(1024)(128)(4,1)}), s8[4194304]{0:T(1024)(128)(4,1)S(1)}, s32[]{:S(2)}) async-start(s8[9658368]{0:T(1024)(128)(4,1)} %bitcast.104), calls=%async_computation.1 | async-start | bytes 8388608
  204.3 20.4 %slice-start.1 = ((s8[9658368]{0:T(1024)(128)(4,1)}), s8[4194304]{0:T(1024)(128)(4,1)S(1)}, s32[]{:S(2)}) async-start(s8[9658368]{0:T(1024)(128)(4,1)} %bitcast.104), calls=%async_computation.2 | async-start | bytes 8388608
  224.7 95.4 %copy-start.7 = (f32[1024,768]{0,1:T(8,128)}, f32[1024,768]{0,1:T(8,128)S(1)}, u32[]{:S(2)}) copy-start(f32[1024,768]{0,1:T(8,128)S(1)} %get-tuple-element.190) | copy-start | bytes 9437188
  256.0 31.7 %copy-start.44 = (f32[1024]{0:T(1024)}, f32[1024]{0:T(1024)S(1)}, u32[]{:S(2)}) copy-start(f32[1024]{0:T(1024)S(1)} %pmax.7) | copy-start | bytes 12292
  399.7 19.9 %copy-start.29 = (bf16[1024,768]{0,1:T(8,128)(2,1)}, bf16[1024,768]{0,1:T(8,128)(2,1)S(1)}, u32[]{:S(2)}) copy-start(bf16[1024,768]{0,1:T(8,128)(2,1)S(1)} %get-tuple-element.138) | copy-start | bytes 4718596
  596.2 203.8 %copy-start.33 = (f32[192,1536]{1,0:T(8,128)S(1)}, f32[192,1536]{1,0:T(8,128)}, u32[]{:S(2)}) copy-start(f32[192,1536]{1,0:T(8,128)} %param.57) | copy-start | bytes 3538948
  610.6 189.4 %copy-start.39 = (f32[14,768]{1,0:T(8,128)}, f32[14,768]{1,0:T(8,128)S(1)}, u32[]{:S(2)}) copy-start(f32[14,768]{1,0:T(8,128)S(1)} %get-tuple-element.117) | copy-start | bytes 129028
  610.6 189.4 %copy-start.40 = (f32[14,768]{1,0:T(8,128)}, f32[14,768]{1,0:T(8,128)S(1)}, u32[]{:S(2)}) copy-start(f32[14,768]{1,0:T(8,128)S(1)} %get-tuple-element.118) | copy-start | bytes 129028
  802.1 151.7 %copy-start.12 = (f32[192,1536]{1,0:T(8,128)}, f32[192,1536]{1,0:T(8,128)S(1)}, u32[]{:S(2)}) copy-start(f32[192,1536]{1,0:T(8,128)S(1)} %get-tuple-element.130) | copy-start | bytes 3538948
  804.1 155.5 %copy-start.14 = (f32[192,1152]{1,0:T(8,128)}, f32[192,1152]{1,0:T(8,128)S(1)}, u32[]{:S(2)}) copy-start(f32[192,1152]{1,0:T(8,128)S(1)} %get-tuple-element.132) | copy-start | bytes 2654212
  806.0 151.2 %copy-start.27 = (f32[192,384]{1,0:T(8,128)}, f32[192,384]{1,0:T(8,128)S(1)}, u32[]{:S(2)}) copy-start(f32[192,384]{1,0:T(8,128)S(1)} %get-tuple-element.131) | copy-start | bytes 884740
  815.9 134.5 %copy-start.13 = (f32[384,768]{1,0:T(8,128)}, f32[384,768]{1,0:T(8,128)S(1)}, u32[]{:S(2)}) copy-start(f32[384,768]{1,0:T(8,128)S(1)} %get-tuple-element.123) | copy-start | bytes 3538948
  854.9 98.9 %copy-start.42 = (f32[1536]{0:T(1024)}, f32[1536]{0:T(1024)S(1)}, u32[]{:S(2)}) copy-start(f32[1536]{0:T(1024)S(1)} %multiply_add_fusion.10) | copy-start | bytes 18436
  856.9 102.7 %copy-start.43 = (f32[1152]{0:T(1024)}, f32[1152]{0:T(1024)S(1)}, u32[]{:S(2)}) copy-start(f32[1152]{0:T(1024)S(1)} %multiply_add_fusion.11) | copy-start | bytes 13828
  (62 other events, 466.4 us)
Sparse Core Ops, SparseCore 0:
  596.3 203.5 all-reduce.7

commit v2 on v1

--- a/solution.py
+++ b/solution.py
@@ -109,6 +109,16 @@
                 count = count + when.astype(jnp.int32)
         pl.semaphore_wait(barrier, count)
 
+    def plane_peers(self, n_row):
+        me, peers = self.col * n_row + self.row, []
+        for k in range(1, 2 * n_row):
+            index = (me + k) % (2 * n_row)
+            peers.append((index, self.device(row=index % n_row, col=index // n_row)))
+        return me, peers
+
+    def example_peers(self):
+        return [((self.dp + k) % 4, self.device(dp=(self.dp + k) % 4)) for k in range(1, 4)]
+
     def plane_neighbours(self, n_row):
         return [
             (self.device(row=self.row + 1), self.row < n_row - 1),
@@ -135,13 +145,16 @@
     for at in order:
         link.send(part.at[1 - col, at], from_col.at[at], y_base + at, link.device(col=1 - col))
     yield
-    for at in order:
-        link.landed(from_col.at[at], y_base + at)
+    waiting = list(order)
 
     def mine(at):
         return part[col, at].astype(F32) + from_col[at].astype(F32)
 
     for k in range(n_row - 1):
+        for at in (n_row - 1 - k, k):
+            if at in waiting:
+                waiting.remove(at)
+                link.landed(from_col.at[at], y_base + at)
         for at, going, more, source, target, base_at, device in (
             (n_row - 1 - k, row < n_row - 1 - k, row > 0, up_in, up_out, up_base, link.device(row=row + 1)),
             (k, row > k, row < n_row - 1, down_in, down_out, down_base, link.device(row=row - 1)),
@@ -374,6 +387,7 @@
         ],
         in_specs=[column(0), column(pairs), column(2 * pairs)],
         out_specs=[column(0), pl.BlockSpec((1, 2, length), lambda i: (i, 0, 0))],
+        cost_estimate=cost(20 * length * length * width, 8 * length * width),
         compiler_params=pltpu.CompilerParams(vmem_limit_bytes=40 * 1024 * 1024),
     )(packed, packed, packed)
 
@@ -417,28 +431,799 @@
         + [pl.BlockSpec((1, 2, length), lambda i: (i, 0, 0))],
         out_specs=pl.BlockSpec((3, length, lanes), lambda i: (0, 0, i)),
         scratch_shapes=[pltpu.VMEM((length, HEAD), F32)] * 2,
+        cost_estimate=cost(30 * length * length * width, 16 * length * width),
         compiler_params=pltpu.CompilerParams(vmem_limit_bytes=48 * 1024 * 1024),
     )(packed, packed, packed, mixed_grad, log_norm)
 
 
-def norm_forward(inputs, gain, shift):
+def meet(link, base, value, slots, me, peers):
+    slots[me] = value[...]
+    for _, device in peers:
+        link.send(value, slots.at[me], base + me, device)
+    for index, _ in peers:
+        link.landed(slots.at[index], base + index)
+
+
+def added(slots):
+    total = slots[0]
+    for k in range(1, slots.shape[0]):
+        total = total + slots[k]
+    return total
+
+
+def sum_small_kernel(n_row, value, total, middle, slots, dp_slots, send_sems, recv_sems):
+    link = Link(send_sems, recv_sems)
+    me, peers = link.plane_peers(n_row)
+    examples = link.example_peers()
+    link.greet([(device, None) for _, device in peers + examples])
+    meet(link, 0, value, slots, me, peers)
+    middle[...] = added(slots)
+    meet(link, 2 * n_row, middle, dp_slots, link.dp, examples)
+    total[...] = added(dp_slots)
+    link.finish()
+
+
+def sum_small(value, n_row, collective_id):
+    vmem = pl.BlockSpec(memory_space=pltpu.VMEM)
+    return pl.pallas_call(
+        functools.partial(sum_small_kernel, n_row),
+        out_shape=jax.ShapeDtypeStruct(value.shape, F32),
+        in_specs=[vmem],
+        out_specs=vmem,
+        scratch_shapes=[pltpu.VMEM(value.shape, F32), pltpu.VMEM((2 * n_row,) + value.shape, F32)]
+        + [pltpu.VMEM((4,) + value.shape, F32)]
+        + [pltpu.SemaphoreType.DMA((2 * n_row + 2,)), pltpu.SemaphoreType.DMA((2 * n_row + 4,))],
+        compiler_params=pltpu.CompilerParams(collective_id=collective_id, has_side_effects=True),
+    )(value)
+
+
+def log_total_kernel(n_row, tops, sums, picked, log_ref, pick_ref, value, slots, send_sems, recv_sems):
+    link = Link(send_sems, recv_sems)
+    me, peers = link.plane_peers(n_row)
+    link.greet([(device, None) for _, device in peers])
+    top = jnp.max(tops[...], 0)
+    value[0] = top
+    value[1] = jnp.sum(sums[...] * jnp.exp(tops[...] - top[None]), 0)
+    value[2] = picked[...]
+    meet(link, 0, value, slots, me, peers)
+    everyone = range(2 * n_row)
+    top, total, pick = slots[0, 0], jnp.zeros_like(top), jnp.zeros_like(top)
+    for k in everyone:
+        top = jnp.maximum(top, slots[k, 0])
+    for k in everyone:
+        total = total + slots[k, 1] * jnp.exp(slots[k, 0] - top)
+        pick = pick + slots[k, 2]
+    log_ref[...] = top + jnp.log(total)
+    pick_ref[...] = pick
+    link.finish()
+
+
+def log_total(tops, sums, picked, n_row, collective_id):
+    length = picked.shape[-1]
+    tile = (length // 128, 128)
+    tops, sums, picked = (item.reshape(item.shape[:-2] + tile) for item in (tops, sums, picked))
+    vmem = pl.BlockSpec(memory_space=pltpu.VMEM)
+    log_norm, picked = pl.pallas_call(
+        functools.partial(log_total_kernel, n_row),
+        out_shape=[jax.ShapeDtypeStruct(tile, F32)] * 2,
+        in_specs=[vmem] * 3,
+        out_specs=[vmem] * 2,
+        scratch_shapes=[pltpu.VMEM((3,) + tile, F32), pltpu.VMEM((2 * n_row, 3) + tile, F32)]
+        + [pltpu.SemaphoreType.DMA((2 * n_row,))] * 2,
+        compiler_params=pltpu.CompilerParams(collective_id=collective_id, has_side_effects=True),
+    )(tops, sums, picked)
+    return log_norm.reshape(1, length), picked.reshape(1, length)
+
+
+BLOCK = 1056
+MEGA = 1024 * 1024
+
+
+def cost(flops, bytes_accessed):
+    return pl.CostEstimate(flops=flops, bytes_accessed=bytes_accessed, transcendentals=0)
+
+
+def blocks_of(limit):
+    return pl.cdiv(limit, BLOCK)
+
+
+def entries(shape, first=0):
+    return lax.broadcasted_iota(jnp.int32, shape, 0) + (pl.program_id(0) + first) * BLOCK
+
+
+def head_kernel(limit, table_ref, z_ref, target_ref, low_ref, exp_ref, top_ref, sum_ref, pick_ref, square_ref):
+    table = table_ref[...]
+    table = jnp.where(entries(table.shape) < limit, table, 0.0)
+    low = table.astype(BF16)
+    low_ref[...] = low
+    logits = mm_nt(low, z_ref[...])
+    entry = entries(logits.shape)
+    logits = jnp.where(entry < limit, logits, -1e30)
+    top = jnp.max(logits, 0, keepdims=True)
+    picked = jnp.sum(jnp.where(entry == target_ref[...], logits, 0.0), 0, keepdims=True)
+    exps = jnp.exp(logits - top)
+    exp_ref[...] = exps.astype(BF16)
+    top_ref[0] = top
+    sum_ref[0] = jnp.sum(exps, 0, keepdims=True)
+    square = jnp.sum(table * table, 0, keepdims=True)
+
+    @pl.when(pl.program_id(0) == 0)
+    def _():
+        pick_ref[...] = jnp.zeros_like(pick_ref)
+        square_ref[...] = jnp.zeros_like(square_ref)
+
+    pick_ref[...] += picked
+    square_ref[...] += square
+
+
+def whole_block(shape):
+    return pl.BlockSpec(shape, lambda i, *_: (0,) * len(shape), pipeline_mode=pl.Buffered(1))
+
+
+def row_block(width):
+    return pl.BlockSpec((BLOCK, width), lambda i, *_: (i, 0))
+
+
+def line_block(width):
+    return pl.BlockSpec((1, 1, width), lambda i, *_: (i, 0, 0))
+
+
+def head(table, z, target):
+    limit, width = table.shape
+    length, count = z.shape[0], blocks_of(limit)
+    shape = jax.ShapeDtypeStruct
+    return pl.pallas_call(
+        functools.partial(head_kernel, limit),
+        grid=(count,),
+        out_shape=[
+            shape((count * BLOCK, width), BF16),
+            shape((count * BLOCK, length), BF16),
+            shape((count, 1, length), F32),
+            shape((count, 1, length), F32),
+            shape((1, length), F32),
+            shape((1, width), F32),
+        ],
+        in_specs=[row_block(width), whole_block((length, width)), whole_block((1, length))],
+        out_specs=[row_block(width), row_block(length), line_block(length), line_block(length)]
+        + [whole_block((1, length)), whole_block((1, width))],
+        cost_estimate=cost(2 * limit * width * length, 6 * limit * width + 2 * limit * length),
+        compiler_params=pltpu.CompilerParams(vmem_limit_bytes=48 * MEGA),
+    )(table, z, target)
+
+
+def head_back_kernel(exp_ref, top_ref, log_ref, target_ref, low_ref, z_ref, grad_ref, table_ref, total):
+    at = pl.program_id(0)
+    scale = jnp.exp(top_ref[0] - log_ref[...])
+    exps = exp_ref[...].astype(F32)
+    hit = (entries(exps.shape) == target_ref[...]).astype(F32)
+    slope = (exps * scale - hit).astype(BF16)
+    table_ref[...] = mm(slope, z_ref[...]).astype(BF16)
+    part = mm_tn(low_ref[...], slope)
+
+    @pl.when(at == 0)
+    def _():
+        total[...] = part
+
+    @pl.when(at > 0)
+    def _():
+        total[...] += part
+
+    @pl.when(at == pl.num_programs(0) - 1)
+    def _():
+        grad_ref[...] = total[...].T.astype(BF16)
+
+
+def head_back(exps, tops, log_norm, target, low, z):
+    length, width = z.shape
+    return pl.pallas_call(
+        head_back_kernel,
+        grid=(low.shape[0] // BLOCK,),
+        out_shape=[jax.ShapeDtypeStruct((length, width), BF16), jax.ShapeDtypeStruct(low.shape, BF16)],
+        in_specs=[row_block(length), line_block(length), whole_block((1, length)), whole_block((1, length))]
+        + [row_block(width), whole_block((length, width))],
+        out_specs=[whole_block((length, width)), row_block(width)],
+        scratch_shapes=[pltpu.VMEM((width, length), F32)],
+        cost_estimate=cost(4 * low.size * length, 4 * low.size + 2 * exps.size),
+        compiler_params=pltpu.CompilerParams(vmem_limit_bytes=48 * MEGA),
+    )(exps, tops, log_norm, target, low, z)
+
+
+def token_lists(ids, start, limit):
+    length = ids.shape[0]
+    token = jnp.arange(length, dtype=jnp.int32)
+    one, two = ids[:, None], ids[None, :]
+    ahead = (two < one) | ((two == one) & (token[None, :] < token[:, None]))
+    place = jnp.sum(ahead.astype(jnp.int32), 1)
+    at = place[:, None] == token[None, :]
+    order = jnp.sum(jnp.where(at, token[:, None], 0), 0)
+    ordered = jnp.sum(jnp.where(at, ids[:, None], 0), 0)
+    edges = start + jnp.minimum(jnp.arange(blocks_of(limit) + 1) * BLOCK, limit)
+    bounds = jnp.sum((ids[None, :] < edges[:, None]).astype(jnp.int32), 1)
+    return ordered - start, order, bounds
+
+
+def add_rows(total, ids_ref, order_ref, bounds_ref, grad_ref, first=0):
+    at = pl.program_id(0) + first
+
+    def step(k, carry):
+        row, token = ids_ref[k] - at * BLOCK, order_ref[k]
+        total[pl.ds(row, 1), :] += grad_ref[pl.ds(token, 1), :]
+        return carry
+
+    lax.fori_loop(bounds_ref[at], bounds_ref[at + 1], step, 0)
+
+
+def own_rows_kernel(ids_ref, order_ref, bounds_ref, table_ref, grad_ref, out_ref, square_ref, total):
+    total[...] = table_ref[...].astype(F32)
+    add_rows(total, ids_ref, order_ref, bounds_ref, grad_ref)
+    full = total[...]
+    out_ref[...] = full.astype(BF16)
+
+    @pl.when(pl.program_id(0) == 0)
+    def _():
+        square_ref[...] = jnp.zeros_like(square_ref)
+
+    square_ref[...] += jnp.sum(full * full, 0, keepdims=True)
+
+
+def add_own_rows(table, lists, grad):
+    width = table.shape[1]
+    return pl.pallas_call(
+        own_rows_kernel,
+        grid_spec=pltpu.PrefetchScalarGridSpec(
+            num_scalar_prefetch=3,
+            grid=(table.shape[0] // BLOCK,),
+            in_specs=[row_block(width), whole_block(grad.shape)],
+            out_specs=[row_block(width), whole_block((1, width))],
+            scratch_shapes=[pltpu.VMEM((BLOCK, width), F32)],
+        ),
+        out_shape=[jax.ShapeDtypeStruct(table.shape, BF16), jax.ShapeDtypeStruct((1, width), F32)],
+        cost_estimate=cost(0, 4 * table.size),
+        compiler_params=pltpu.CompilerParams(vmem_limit_bytes=56 * MEGA),
+    )(*lists, table, grad)
+
+
+def table_sum_kernel(first, ids_ref, order_ref, bounds_ref, share_ref, *refs):
+    low_ref, z_ref, log_ref, target_ref, own_ref, grad_ref, out_ref, total = refs
+    exps = jnp.exp(mm_nt(low_ref[...], z_ref[...]) - log_ref[...])
+    hit = (entries(exps.shape, first) == target_ref[...]).astype(F32)
+    total[...] = mm((exps - hit).astype(BF16), z_ref[...])
+    add_rows(total, ids_ref, order_ref, bounds_ref, grad_ref, first)
+    out_ref[...] = (share_ref[0] * own_ref[...].astype(F32) + share_ref[1] * total[...]).astype(BF16)
+
+
+def table_sum(own, low, z, log_norm, target, lists, grad, shares, first, count):
+    length, width = z.shape
+    rows = lambda i, *_: (i + first, 0)
+    return pl.pallas_call(
+        functools.partial(table_sum_kernel, first),
+        grid_spec=pltpu.PrefetchScalarGridSpec(
+            num_scalar_prefetch=4,
+            grid=(count,),
+            in_specs=[pl.BlockSpec((BLOCK, width), rows), whole_block((length, width))]
+            + [whole_block((1, length)), whole_block((1, length))]
+            + [pl.BlockSpec((BLOCK, width), rows), whole_block(grad.shape)],
+            out_specs=row_block(width),
+            scratch_shapes=[pltpu.VMEM((BLOCK, width), F32)],
+        ),
+        out_shape=jax.ShapeDtypeStruct((count * BLOCK, width), BF16),
+        cost_estimate=cost(4 * count * BLOCK * width * length, 6 * count * BLOCK * width),
+        compiler_params=pltpu.CompilerParams(vmem_limit_bytes=48 * MEGA),
+    )(*lists, shares, low, z, log_norm, target, own, grad)
+
+
+def turned(line, height):
+    return jnp.broadcast_to(line, (height, line.shape[1])).T
+
+
+def gradient_kernel(limit, count, divisor, first, *refs):
+    sums, (noise_ref, old_ref), outs = refs[:count], refs[count : count + 2], refs[-5:]
+    grad_ref, rows_ref, cols_ref, scaled_ref, level_ref = outs
+    total = sums[0][...].astype(F32)
+    for item in sums[1:]:
+        total = total + item[...].astype(F32)
+    grad = (total + NOISE * CLIP * noise_ref[...]) * (1.0 / divisor)
+    inside = entries((BLOCK, 1), first) < limit
+    grad_ref[...] = grad
+    squares = jnp.where(inside, grad * grad, 0.0)
+    mean = jnp.sum(squares, 1, keepdims=True) / grad.shape[1] + 1e-30
+    old = turned(old_ref[0], 128)[:, :1]
+    rows = DECAY * old + (1.0 - DECAY) * mean
+    rows_ref[0] = line_of(rows)
+
+    @pl.when(pl.program_id(0) == 0)
+    def _():
+        cols_ref[...] = jnp.zeros_like(cols_ref)
+        scaled_ref[...] = jnp.zeros_like(scaled_ref)
+        level_ref[...] = jnp.zeros_like(level_ref)
+
+    cols_ref[...] += jnp.sum(squares, 0, keepdims=True)
+    scaled_ref[...] += jnp.sum(squares * (1.0 / rows), 0, keepdims=True)
+    level_ref[...] += jnp.broadcast_to(jnp.sum(jnp.where(inside, rows, 0.0), 0, keepdims=True), level_ref.shape)
+
+
+def table_gradient(sums, noise, old, divisor, first, count, into=None):
+    limit, width = noise.shape
+    shape = jax.ShapeDtypeStruct
+    rows = pl.BlockSpec((BLOCK, width), lambda i: (i + first, 0))
+    extra = [] if into is None else [into]
+    return pl.pallas_call(
+        functools.partial(gradient_kernel, limit, len(sums), divisor, first),
+        grid=(count,),
+        out_shape=[shape((limit, width), F32), shape((count, 1, BLOCK), F32)]
+        + [shape((1, width), F32)] * 2
+        + [shape((1, 128), F32)],
+        in_specs=[row_block(width)] * len(sums)
+        + [rows, pl.BlockSpec((1, 1, BLOCK), lambda i: (i + first, 0, 0))]
+        + [pl.BlockSpec(memory_space=pl.ANY)] * len(extra),
+        out_specs=[rows, line_block(BLOCK), whole_block((1, width)), whole_block((1, width))]
+        + [whole_block((1, 128))],
+        input_output_aliases={len(sums) + 2: 0} if extra else {},
+        cost_estimate=cost(0, (8 + 2 * len(sums)) * count * BLOCK * width),
+        compiler_params=pltpu.CompilerParams(vmem_limit_bytes=48 * MEGA),
+    )(*sums, noise, old, *extra)
+
+
+SIDE = 256
+
+
+def pack_small(pos_ex, layer_packed, small_ex):
+    tall = pos_ex.shape[0] // 4
+    pos = jnp.pad(pos_ex, ((0, 0), (0, SIDE - pos_ex.shape[1])))
+    pos = [pos[k * tall : (k + 1) * tall] for k in range(4)]
+    blank = jnp.zeros_like(pos[0])
+    pieces = [layer_packed, jnp.concatenate(pos[:3], 1), jnp.concatenate([pos[3], blank, blank], 1)]
+    pieces.append(jnp.pad(small_ex, ((0, 32 - small_ex.shape[0]), (0, 0))))
+    return jnp.concatenate(pieces, 0)
+
+
+def line_of(column):
+    return jnp.broadcast_to(column, (column.shape[0], 128)).T[:1]
+
+
+BY_ROW = (False, True, True, True, False)
+
+
+def small_gradients_kernel(divisor, *refs):
+    packed, small, small_second, small_noise = refs[:4]
+    weights, noises, grads = (refs[4 + 5 * k : 9 + 5 * k] for k in range(3))
+    small_outs, (to_col, to_row, square_ref) = refs[19:22], refs[22:]
+    width = small.shape[1]
+    scale = 1.0 / divisor
+    side = weights[1].shape[0]
+    cuts = (0, weights[1].shape[1], weights[1].shape[1] + weights[2].shape[1])
+    for index in (1, 2, 3):
+        at, end, lane_to = cuts[index - 1], cuts[index - 1] + weights[index].shape[1], 0
+        while at < end:
+            piece, lane = at // width, at % width
+            size = min(width - lane, end - at)
+            part = packed[piece * side : (piece + 1) * side, lane : lane + size].astype(F32)
+            lanes = slice(lane_to, lane_to + size)
+            grads[index][:, lanes] = (part + NOISE * CLIP * noises[index][:, lanes]) * scale
+            at, lane_to = at + size, lane_to + size
+    first = side * ((cuts[2] + weights[3].shape[1]) // width)
+    down = weights[4].shape[0]
+    grads[4][...] = (packed[first : first + down, :].astype(F32) + NOISE * CLIP * noises[4][...]) * scale
+    first += down
+    tall, wide = weights[0].shape[0] // 4, weights[0].shape[1]
+    for k in range(4):
+        lane, start = SIDE * (k % 3), first + tall * (k // 3)
+        part = packed[start : start + tall, lane : lane + wide].astype(F32)
+        lines = slice(k * tall, (k + 1) * tall)
+        grads[0][lines] = (part + NOISE * CLIP * noises[0][lines]) * scale
+    first += 2 * tall
+
+    to_col[...] = jnp.zeros_like(to_col)
+    to_row[...] = jnp.zeros_like(to_row)
+    lane = lax.broadcasted_iota(jnp.int32, (1, width), 1)
+    weight_sq = jnp.zeros((1, width), F32)
+    for index, along in enumerate(BY_ROW):
+        squares = grads[index][...] * grads[index][...]
+        row_sum = line_of(jnp.sum(squares, 1, keepdims=True))
+        col_sum = jnp.sum(squares, 0, keepdims=True)
+        rows_to, cols_to = (to_col, to_row) if along else (to_row, to_col)
+        rows_to[index : index + 1, : row_sum.shape[1]] = row_sum
+        cols_to[index : index + 1, : col_sum.shape[1]] = col_sum
+        total = jnp.sum(jnp.sum(weights[index][...] * weights[index][...], 0, keepdims=True), 1, keepdims=True)
+        weight_sq = weight_sq + jnp.where(lane == index, total, 0.0)
+    square_ref[...] = weight_sq
+
+    count = small.shape[0]
+    small_grad = (packed[first : first + 16, :].astype(F32)[:count] + NOISE * CLIP * small_noise[...]) * scale
+    second_new = DECAY * small_second[...] + (1.0 - DECAY) * (small_grad * small_grad + 1e-30)
+    update = small_grad * lax.rsqrt(second_new)
+    mean = lambda item: jnp.sum(jnp.sum(item * item, 0, keepdims=True), 1, keepdims=True) / (count * width)
+    size = RATE * jnp.maximum(1e-3, jnp.sqrt(mean(small[...])))
+    size = size / jnp.maximum(1.0, jnp.sqrt(mean(update)))
+    small_outs[0][...] = small_grad
+    small_outs[1][...] = second_new
+    small_outs[2][...] = small[...] - size * update
+
+
+def small_gradients(packed, small, small_second, small_noise, weights, noises, divisor):
+    width = small.shape[1]
+    wide = max(item.shape[1] for item in weights)
+    shape = lambda dims: jax.ShapeDtypeStruct(dims, F32)
+    operands = [packed, small, small_second, small_noise, *weights, *noises]
+    shapes = [item.shape for item in weights] + [small.shape] * 3 + [(8, width), (8, wide), (1, width)]
+    out = pl.pallas_call(
+        functools.partial(small_gradients_kernel, divisor),
+        grid=(1,),
+        out_shape=[shape(dims) for dims in shapes],
+        in_specs=[whole_block(item.shape) for item in operands],
+        out_specs=[whole_block(dims) for dims in shapes],
+        compiler_params=pltpu.CompilerParams(vmem_limit_bytes=48 * MEGA),
+        cost_estimate=cost(0, 16 * MEGA),
+    )(*operands)
+    return out[:5], out[5:8], out[8:]
+
+
+def statistics_kernel(n_row, vocab, *refs):
+    table_over, over_cols, over_rows, old_lines = refs[:4]
+    grads, (lines_ref, factor_ref), held = refs[4:9], refs[9:11], refs[11:16]
+    to_level, both_slots, col_slots, row_slots, level_slots, send_sems, recv_sems, local_sems = refs[16:]
+    n_col, width = 2, table_over.shape[1]
+    everyone = n_row * n_col
+    copies = [pltpu.make_async_copy(grads[k], held[k], local_sems.at[k]) for k in range(5)]
+    for copy in copies:
+        copy.start()
+    link = Link(send_sems, recv_sems)
+    me, peers = link.plane_peers(n_row)
+    link.greet([(device, None) for _, device in peers])
+    row_peers = [((link.row + k) % n_row, link.device(row=(link.row + k) % n_row)) for k in range(1, n_row)]
+    meet(link, 0, table_over, both_slots, me, peers)
+    meet(link, everyone, over_cols, col_slots, link.col, [(1 - link.col, link.device(col=1 - link.col))])
+    meet(link, everyone + n_col, over_rows, row_slots, link.row, row_peers)
+    both, over_col, over_row = added(both_slots), added(col_slots), added(row_slots)
+    for copy in copies:
+        copy.wait()
+
+    lane = lax.broadcasted_iota(jnp.int32, (1, 128), 1)
+
+    def pick(line, at):
+        return jnp.sum(jnp.where(lane == at, line[:, :128], 0.0), 1, keepdims=True)
+
+    def step_size(weight_sum, level, square_sum, entries_all):
+        size = RATE * jnp.maximum(1e-3, jnp.sqrt(weight_sum / entries_all))
+        size = size / jnp.maximum(1.0, jnp.sqrt(square_sum * level / entries_all))
+        return size * jnp.sqrt(level)
+
+    whole = lambda line: jnp.sum(line, 1, keepdims=True)
+    cols_new = DECAY * table_over[5:6] + (1.0 - DECAY) * (both[0:1] / vocab + 1e-30)
+    level = pick(both[2:3], 0) / vocab
+    size = step_size(whole(both[3:4]), level, whole(both[1:2] / cols_new), float(vocab * width))
+    factor_ref[...] = jnp.zeros_like(factor_ref)
+    factor_ref[0:1] = cols_new
+    factor_ref[1:2] = size * lax.rsqrt(cols_new)
+
+    lines_ref[...] = jnp.zeros_like(lines_ref)
+    levels = jnp.zeros((1, 128), F32)
+    for index, along in enumerate(BY_ROW):
+        rows, cols = held[index].shape
+        parts_rows, parts_cols = (n_row, n_col) if along else (n_col, n_row)
+        rows_from, cols_from = (over_col, over_row) if along else (over_row, over_col)
+        row_mean = rows_from[index : index + 1, :rows] / (cols * parts_cols) + 1e-30
+        col_mean = cols_from[index : index + 1, :cols] / (rows * parts_rows) + 1e-30
+        rows_line = DECAY * old_lines[index : index + 1, :rows] + (1.0 - DECAY) * row_mean
+        cols_line = DECAY * old_lines[8 + index : 9 + index, :cols] + (1.0 - DECAY) * col_mean
+        lines_ref[index : index + 1, :rows] = rows_line
+        lines_ref[8 + index : 9 + index, :cols] = cols_line
+        level = whole(rows_line) / (rows * parts_rows * parts_cols)
+        scaled = held[index][...] * held[index][...] * (1.0 / turned(rows_line, 128)[:, :1])
+        scaled = whole(jnp.sum(scaled, 0, keepdims=True) / cols_line)
+        levels = levels + jnp.where(lane == 2 * index, level, 0.0) + jnp.where(lane == 2 * index + 1, scaled, 0.0)
+    to_level[...] = jnp.zeros_like(to_level)
+    to_level[:1] = levels
+    meet(link, everyone + n_col + n_row, to_level, level_slots, me, peers)
+    levels = added(level_slots)[:1]
+    sizes = jnp.zeros((1, 128), F32)
+    for index in range(5):
+        entries_all = float(held[index].shape[0] * held[index].shape[1] * everyone)
+        size = step_size(pick(both[4:5], index), pick(levels, 2 * index), pick(levels, 2 * index + 1), entries_all)
+        sizes = sizes + jnp.where(lane == index, size, 0.0)
+    factor_ref[2:3, :128] = sizes
+    link.finish()
+
+
+def statistics(table_over, over_cols, over_rows, old_lines, grads, n_row, vocab, collective_id):
+    width, wide = table_over.shape[1], over_rows.shape[1]
+    everyone = 2 * n_row
+    vmem, hbm = pl.BlockSpec(memory_space=pltpu.VMEM), pl.BlockSpec(memory_space=pl.ANY)
+    return pl.pallas_call(
+        functools.partial(statistics_kernel, n_row, vocab),
+        out_shape=[jax.ShapeDtypeStruct((16, wide), F32), jax.ShapeDtypeStruct((8, width), F32)],
+        in_specs=[vmem] * 4 + [hbm] * 5,
+        out_specs=[vmem] * 2,
+        scratch_shapes=[pltpu.VMEM(item.shape, F32) for item in grads]
+        + [pltpu.VMEM((8, 128), F32), pltpu.VMEM((everyone, 8, width), F32), pltpu.VMEM((2, 8, width), F32)]
+        + [pltpu.VMEM((n_row, 8, wide), F32), pltpu.VMEM((everyone, 8, 128), F32)]
+        + [pltpu.SemaphoreType.DMA((3 * everyone,)), pltpu.SemaphoreType.DMA((2 * everyone + 2 + n_row,))]
+        + [pltpu.SemaphoreType.DMA((5,))],
+        compiler_params=pltpu.CompilerParams(
+            collective_id=collective_id, has_side_effects=True, vmem_limit_bytes=32 * MEGA
+        ),
+    )(table_over, over_cols, over_rows, old_lines, *grads)
+
+
+def update_kernel(table_ref, table_grad_ref, rows_ref, factor_ref, lines_ref, *refs):
+    weights, grads, (table_new_ref, table_cols_ref) = refs[:5], refs[5:10], refs[10:12]
+    rows_outs, cols_outs, news = refs[12:17], refs[17:22], refs[22:27]
+    rows = turned(lax.rsqrt(rows_ref[0]), 128)[:, :1]
+    table_new_ref[...] = table_ref[...] - table_grad_ref[...] * rows * factor_ref[1:2]
+
+    @pl.when(pl.program_id(0) == 0)
+    def _():
+        table_cols_ref[...] = factor_ref[0:1]
+        for index in range(5):
+            count_rows, count_cols = weights[index].shape
+            rows_line = lines_ref[index : index + 1, :count_rows]
+            cols_line = lines_ref[8 + index : 9 + index, :count_cols]
+            rows_outs[index][...] = rows_line
+            cols_outs[index][...] = cols_line
+            rows = turned(lax.rsqrt(rows_line), 128)[:, :1]
+            factors = factor_ref[2:3, index : index + 1] * lax.rsqrt(cols_line)
+            news[index][...] = weights[index][...] - grads[index][...] * rows * factors
+
+
+def update(table, table_grad, table_rows, factors, lines, weights, grads):
+    limit, width = table.shape
+    shape = lambda dims: jax.ShapeDtypeStruct(dims, F32)
+    small_shapes = [(1, width)] + [(1, item.shape[0]) for item in weights] + [(1, item.shape[1]) for item in weights]
+    small_shapes += [item.shape for item in weights]
+    out = pl.pallas_call(
+        update_kernel,
+        grid=(blocks_of(limit),),
+        out_shape=[shape(table.shape)] + [shape(dims) for dims in small_shapes],
+        in_specs=[row_block(width), row_block(width), line_block(BLOCK), whole_block(factors.shape)]
+        + [whole_block(lines.shape)]
+        + [whole_block(item.shape) for item in weights] * 2,
+        out_specs=[row_block(width)] + [whole_block(dims) for dims in small_shapes],
+        compiler_params=pltpu.CompilerParams(vmem_limit_bytes=56 * MEGA),
+        cost_estimate=cost(0, 3 * 4 * limit * width),
+    )(table, table_grad, table_rows, factors, lines, *weights, *grads)
+    flat = lambda items: [item[0] for item in items]
+    return out[0], out[1][0], flat(out[2:7]), flat(out[7:12]), out[12:]
+
+
+HIDDEN = 1024
+CHUNK = 512
+
+
+def normed_of(inputs):
     center = jnp.mean(inputs, -1, keepdims=True)
     var = jnp.mean(inputs * inputs, -1, keepdims=True) - center * center
     inv = lax.rsqrt(var + 1e-05)
-    normed = (inputs - center) * inv
-    return (normed * gain + shift).astype(BF16), normed, inv
-
-
-def norm_backward(upstream, normed, inv, gain):
+    return (inputs - center) * inv, inv
+
+
+def normed_back(upstream, normed, inv, gain):
     scaled = upstream * gain
     first = jnp.mean(scaled, -1, keepdims=True)
     second = jnp.mean(scaled * normed, -1, keepdims=True)
-    result = inv * (scaled - first - normed * second)
-    return result, jnp.sum(upstream * normed, 0), jnp.sum(upstream, 0)
-
-
-def gelu_tanh(inputs):
-    return jax.nn.gelu(inputs, approximate=True)
+    return inv * (scaled - first - normed * second)
+
+
+def columns_sum(item):
+    return jnp.sum(item.astype(F32), 0, keepdims=True)
+
+
+def chunks_of(length):
+    return [slice(at, at + CHUNK) for at in range(0, length, CHUNK)]
+
+
+GELU_SCALE = (2.0 / jnp.pi) ** 0.5
+
+
+def gelu_parts(inputs):
+    square = inputs * inputs
+    turn = jnp.tanh(inputs * (GELU_SCALE + (GELU_SCALE * 0.044715) * square))
+    half = 0.5 + 0.5 * turn
+    inner = GELU_SCALE + (3.0 * GELU_SCALE * 0.044715) * square
+    return inputs * half, half + 0.5 * inputs * (1.0 - turn * turn) * inner
+
+
+def middle_kernel(start_ref, mixed_ref, attn_ref, up_ref, bias_ref, down_ref, small_ref, *outs):
+    mid_ref, low_ref, out_ref, z_ref, total = outs
+    at = pl.program_id(0)
+    length = start_ref.shape[0]
+
+    @pl.when(at == 0)
+    def _():
+        for rows in chunks_of(length):
+            mid = start_ref[rows].astype(F32) + mm(mixed_ref[rows], attn_ref[...]) + small_ref[4:5]
+            mid_ref[rows] = mid
+            low_ref[rows] = (normed_of(mid)[0] * small_ref[5:6] + small_ref[6:7]).astype(BF16)
+            total[rows] = mid + small_ref[11:12]
+
+    for rows in chunks_of(length):
+        hidden = gelu_parts(mm(low_ref[rows], up_ref[...]) + bias_ref[...])[0].astype(BF16)
+        total[rows] += mm_nt(hidden, down_ref[...])
+
+    @pl.when(at == pl.num_programs(0) - 1)
+    def _():
+        for rows in chunks_of(length):
+            out = total[rows]
+            out_ref[rows] = out
+            z_ref[rows] = (normed_of(out)[0] * small_ref[12:13] + small_ref[13:14]).astype(BF16)
+
+
+def middle_forward(start, mixed, attn, up, up_bias, down, small):
+    length, width = start.shape
+    shape = jax.ShapeDtypeStruct
+    whole = lambda item: whole_block(item.shape)
+    tokens = whole_block((length, width))
+    return pl.pallas_call(
+        middle_kernel,
+        grid=(up.shape[1] // HIDDEN,),
+        out_shape=[shape((length, width), kind) for kind in (F32, BF16, F32, BF16)],
+        in_specs=[whole(start), whole(mixed), whole(attn), pl.BlockSpec((width, HIDDEN), lambda i: (0, i))]
+        + [pl.BlockSpec((1, HIDDEN), lambda i: (0, i)), pl.BlockSpec((width, HIDDEN), lambda i: (0, i))]
+        + [whole(small)],
+        out_specs=[tokens] * 4,
+        scratch_shapes=[pltpu.VMEM((length, width), F32)],
+        cost_estimate=cost(4 * length * width * up.shape[1], 16 * length * width),
+        compiler_params=pltpu.CompilerParams(vmem_limit_bytes=56 * MEGA),
+    )(start, mixed, attn, up, up_bias, down, small)
+
+
+def middle_back_kernel(*refs):
+    grad_ref, out_ref, mid_ref, low_ref, attn_ref, up_ref, bias_ref, down_ref, small_ref = refs[:9]
+    down_grad_ref, pre_ref, act_ref, pre_sum_ref, mid_grad_ref, branch_ref, mixed_ref, rows_ref, total = refs[9:]
+    at = pl.program_id(0)
+    length, width = grad_ref.shape
+
+    @pl.when(at == 0)
+    def _():
+        rows_ref[...] = jnp.zeros_like(rows_ref)
+        for rows in chunks_of(length):
+            grad = grad_ref[rows].astype(F32)
+            normed, inv = normed_of(out_ref[rows])
+            back = normed_back(grad, normed, inv, small_ref[12:13])
+            mid_grad_ref[rows] = back
+            low = back.astype(BF16)
+            down_grad_ref[rows] = low
+            rows_ref[0:1] += columns_sum(grad * normed)
+            rows_ref[1:2] += columns_sum(grad)
+            rows_ref[2:3] += columns_sum(low)
+        total[...] = jnp.zeros_like(total)
+
+    pre_sum = jnp.zeros((1, pre_ref.shape[1]), F32)
+    for rows in chunks_of(length):
+        act, slope = gelu_parts(mm(low_ref[rows], up_ref[...]) + bias_ref[...])
+        act_ref[rows] = act.astype(BF16)
+        pre = (mm(down_grad_ref[rows], down_ref[...]) * slope).astype(BF16)
+        pre_ref[rows] = pre
+        pre_sum = pre_sum + columns_sum(pre)
+        total[rows] += mm_nt(pre, up_ref[...])
+    pre_sum_ref[...] = pre_sum
+
+    @pl.when(at == pl.num_programs(0) - 1)
+    def _():
+        for rows in chunks_of(length):
+            grad = total[rows]
+            normed, inv = normed_of(mid_ref[rows])
+            mid_grad = mid_grad_ref[rows] + normed_back(grad, normed, inv, small_ref[5:6])
+            mid_grad_ref[rows] = mid_grad
+            low = mid_grad.astype(BF16)
+            branch_ref[rows] = low
+            rows_ref[3:4] += columns_sum(grad * normed)
+            rows_ref[4:5] += columns_sum(grad)
+            rows_ref[5:6] += columns_sum(low)
+            mixed_ref[rows] = mm_nt(low, attn_ref[...]).astype(BF16)
+
+
+def middle_back(grad, out, mid, low, attn, up, up_bias, down, small):
+    length, width = grad.shape
+    hidden = up.shape[1]
+    shape = jax.ShapeDtypeStruct
+    whole = lambda item: whole_block(item.shape)
+    tokens = whole_block((length, width))
+    wide = pl.BlockSpec((length, HIDDEN), lambda i: (0, i))
+    weight = pl.BlockSpec((width, HIDDEN), lambda i: (0, i))
+    line = pl.BlockSpec((1, HIDDEN), lambda i: (0, i))
+    return pl.pallas_call(
+        middle_back_kernel,
+        grid=(hidden // HIDDEN,),
+        out_shape=[shape((length, width), BF16), shape((length, hidden), BF16), shape((length, hidden), BF16)]
+        + [shape((1, hidden), F32), shape((length, width), F32), shape((length, width), BF16)]
+        + [shape((length, width), BF16), shape((8, width), F32)],
+        in_specs=[tokens] * 4 + [whole(attn), weight, line, weight, whole(small)],
+        out_specs=[tokens, wide, wide, line, tokens, tokens, tokens, whole_block((8, width))],
+        scratch_shapes=[pltpu.VMEM((length, width), F32)],
+        cost_estimate=cost(6 * length * width * hidden, 40 * length * width),
+        compiler_params=pltpu.CompilerParams(vmem_limit_bytes=58 * MEGA),
+    )(grad, out, mid, low, attn, up, up_bias, down, small)
+
+
+def start_back_kernel(packed_ref, weight_ref, mid_grad_ref, start_ref, small_ref, out_ref, low_ref, wide_ref, rows_ref):
+    width = start_ref.shape[1]
+    grad = sum(mm_nt(packed_ref[k], weight_ref[:, k * width : (k + 1) * width]) for k in range(3))
+    normed, inv = normed_of(start_ref[...].astype(F32))
+    back = mid_grad_ref[...] + normed_back(grad, normed, inv, small_ref[0:1])
+    out_ref[...] = back
+    low_ref[...] = back.astype(BF16)
+    wide_ref[...] = back.astype(BF16).astype(F32)
+
+    @pl.when(pl.program_id(0) == 0)
+    def _():
+        rows_ref[...] = jnp.zeros_like(rows_ref)
+
+    rows_ref[0:1] += columns_sum(grad * normed)
+    rows_ref[1:2] += columns_sum(grad)
+    rows_ref[2:3] += columns_sum(packed_ref[0])
+    rows_ref[3:4] += columns_sum(packed_ref[2])
+    rows_ref[4:5] += columns_sum(back * back)
+
+
+def start_back(packed_grad, weight, mid_grad, start, small):
+    length, width = start.shape
+    shape = jax.ShapeDtypeStruct
+    tokens = pl.BlockSpec((CHUNK, width), lambda i: (i, 0))
+    return pl.pallas_call(
+        start_back_kernel,
+        grid=(length // CHUNK,),
+        out_shape=[shape((length, width), kind) for kind in (F32, BF16, F32)] + [shape((8, width), F32)],
+        in_specs=[pl.BlockSpec((3, CHUNK, width), lambda i: (0, i, 0)), whole_block(weight.shape), tokens, tokens]
+        + [whole_block(small.shape)],
+        out_specs=[tokens, tokens, tokens, whole_block((8, width))],
+        cost_estimate=cost(6 * length * width * width, 20 * length * width),
+        compiler_params=pltpu.CompilerParams(vmem_limit_bytes=40 * MEGA),
+    )(packed_grad, weight, mid_grad, start, small)
+
+
+def weight_grads_kernel(place_ref, ones_ref, mixed_ref, low_ref, *refs):
+    packed, (branch_ref, pre_ref, down_ref, act_ref), (out_ref, square_ref, wide) = refs[:3], refs[3:7], refs[7:]
+    width = ones_ref.shape[1]
+    tall = width // 4
+    start = pl.multiple_of(place_ref[0], 128)
+    skip = pl.multiple_of(place_ref[1], 8)
+    pieces = (
+        (ones_ref, ((packed[0], 0, 0), (packed[1], 0, 1), (packed[2], 1, 0))),
+        (mixed_ref, ((branch_ref, 1, 1),)),
+        (low_ref, ((pre_ref, 2, 0), (pre_ref, 2, 1), (pre_ref, 3, 0), (pre_ref, 3, 1))),
+    )
+    half = width // 2
+    square = jnp.zeros((1, half), F32)
+    for left_ref, rights in pieces:
+        left = left_ref[:, pl.ds(start, SIDE)].T
+        for k, (right_ref, piece, side) in enumerate(rights):
+            right = right_ref[0] if len(right_ref.shape) == 3 else right_ref[:, pl.ds(k * half, half)]
+            wide[...] = mm(left, right)
+            grad = wide[pl.ds(skip, tall), :]
+            out_ref[piece * tall : (piece + 1) * tall, side * half : (side + 1) * half] = grad
+            square = square + jnp.sum(grad * grad, 0, keepdims=True)
+    left = down_ref[...].T
+    for side in range(2):
+        grad = mm(left, act_ref[:, side * half : (side + 1) * half])
+        out_ref[4 * tall :, side * half : (side + 1) * half] = grad
+        square = square + jnp.sum(grad * grad, 0, keepdims=True)
+    square_ref[...] = square
+
+
+def weight_grads(ln_one, mixed, low, packed_grad, branch, pre, down_grad, act, row_at, col_at):
+    length, width = ln_one.shape
+    half, tall = width // 2, width // 4
+    hidden = pre.shape[1] // 2
+    shape = jax.ShapeDtypeStruct
+    first = row_at * tall
+    place = jnp.stack([first // 128 * 128, first % 128, row_at, col_at]).astype(jnp.int32)
+    unit = lambda k: pl.BlockSpec((1, length, half), lambda i, at: ((3 * at[3] + k) // 2, 0, (3 * at[3] + k) % 2))
+    return pl.pallas_call(
+        weight_grads_kernel,
+        grid_spec=pltpu.PrefetchScalarGridSpec(
+            num_scalar_prefetch=1,
+            grid=(1,),
+            in_specs=[whole_block((length, width))] * 3
+            + [unit(k) for k in range(3)]
+            + [pl.BlockSpec((length, half), lambda i, at: (0, at[3])), pl.BlockSpec((length, hidden), lambda i, at: (0, at[3]))]
+            + [pl.BlockSpec((length, half), lambda i, at: (0, at[3])), pl.BlockSpec((length, width), lambda i, at: (0, at[2]))],
+            out_specs=[whole_block((4 * tall + half, width)), whole_block((1, half))],
+            scratch_shapes=[pltpu.VMEM((SIDE, half), F32)],
+        ),
+        out_shape=[shape((4 * tall + half, width), F32), shape((1, half), F32)],
+        cost_estimate=cost(2 * length * width * width * 2, 16 * length * width),
+        compiler_params=pltpu.CompilerParams(vmem_limit_bytes=56 * MEGA),
+    )(place, ln_one, mixed, low, packed_grad, packed_grad, packed_grad, branch, pre, down_grad, act)
 
 
 def body(
@@ -485,18 +1270,25 @@
     vocab_start = (col_at * n_row + row_at) * vocab_here
     small = small_params
 
+    target = targets - vocab_start
+    target = jnp.where((target >= 0) & (target < vocab_here), target, -1)[None]
+    lists = token_lists(ids, vocab_start, vocab_here)
+    tuned = (n_data, n_row, n_col) == (4, 4, 2)
+    block = length // (n_row * n_col)
+    if tuned:
+        beside = lambda item: lax.ppermute(item, "dp", [(at, at ^ 2) for at in range(4)])
+        met_ids, met_target = beside(jnp.stack([ids, targets]))
+        met_target = met_target - vocab_start
+        met_target = jnp.where((met_target >= 0) & (met_target < vocab_here), met_target, -1)[None]
+        met_lists = token_lists(met_ids, vocab_start, vocab_here)
+
     weights_in = [tok_table, pos_table, qkv_weight, attn_weight, up_weight, down_weight]
     noises = [table_noise, pos_noise, qkv_noise, attn_noise, up_noise, down_noise]
-    weight_sq = jnp.stack([jnp.sum(item * item) for item in weights_in])
-    table_low = tok_table.astype(BF16)
-
+    lows = [item.astype(BF16) for item in weights_in[2:]]
     local_ids = ids - vocab_start
     inside = (local_ids >= 0) & (local_ids < vocab_here)
     safe_ids = jnp.clip(local_ids, 0, vocab_here - 1)
-    looked = jnp.where(inside[:, None], jnp.take(table_low, safe_ids, axis=0), jnp.zeros((), BF16))
-    tuned = (n_data, n_row, n_col) == (4, 4, 2)
-    block = length // (n_row * n_col)
-    lows = [item.astype(BF16) for item in weights_in[2:]]
+    looked = jnp.where(inside[:, None], jnp.take(tok_table, safe_ids, axis=0), 0.0).astype(BF16)
     if tuned:
         pos_blocks = pos_table.reshape(n_row, block, -1)
         pieces = []
@@ -511,139 +1303,216 @@
         start, own_rows, qkv_full, attn_full, up_full, down_full = front(
             looked.reshape(n_col, n_row, block, width), pos_own, shards, n_row
         )
-        stream_in = start.reshape(length, width).astype(F32)
+        stream_in = start.reshape(length, width)
         qkv_full, attn_full, up_full, down_full = (
             item.reshape(width, -1) for item in (qkv_full, attn_full, up_full, down_full)
         )
     else:
-        stream_in = plane_sum(looked).astype(F32) + gather_matrix(pos_table, 1)
+        stream_in = (plane_sum(looked).astype(F32) + gather_matrix(pos_table, 1)).astype(BF16)
         qkv_full, attn_full, up_full = (gather_matrix(item, 0) for item in lows[:3])
         down_full = gather_matrix(lows[3], 1)
 
-    ln_one, norm_one, inv_one = norm_forward(stream_in, small[0], small[1])
+    ln_one = (normed_of(stream_in.astype(F32))[0] * small[0] + small[1]).astype(BF16)
     bias = jnp.concatenate([small[2], jnp.zeros_like(small[2]), small[3]])
     packed = (mm(ln_one, qkv_full) + bias).astype(BF16)
-    mixed, log_norm = attend(packed)
-    stream_mid = stream_in + mm(mixed, attn_full) + small[4]
-    ln_two, norm_two, inv_two = norm_forward(stream_mid, small[5], small[6])
-    up_pre = mm(ln_two, up_full) + small[7:11].reshape(-1)
-    up_act = gelu_tanh(up_pre).astype(BF16)
-    stream_out = stream_mid + mm_nt(up_act, down_full) + small[11]
-    ln_fin, norm_fin, inv_fin = norm_forward(stream_out, small[12], small[13])
-
-    logits = mm_nt(table_low, ln_fin)
-    top = jnp.max(logits, 0)
-    hits = jnp.arange(vocab_here)[:, None] == (targets - vocab_start)[None, :]
-    picked_here = jnp.sum(jnp.where(hits, logits, 0.0), 0)
-    all_top = lax.pmax(top, PLANE)
-    exp_logits = jnp.exp(logits - all_top[None, :])
-    exp_total, picked = plane_sum((jnp.sum(exp_logits, 0), picked_here))
-    loss = jnp.sum(all_top + jnp.log(exp_total) - picked)
-    logit_grad = (exp_logits / exp_total[None, :] - hits.astype(F32)).astype(BF16)
-    final_part = mm_tn(logit_grad, table_low).astype(BF16)
+    mixed, attn_log = attend(packed)
+    up_bias = small[7:11].reshape(1, -1)
+    stream_mid, ln_two, stream_out, ln_fin = middle_forward(
+        stream_in, mixed, attn_full, up_full, up_bias, down_full, small
+    )
+
+    table_low, exps, tops, exp_sums, picked, table_sq = head(tok_table, ln_fin, target)
+    if tuned:
+        met_z = beside(ln_fin)
+        log_norm, picked = log_total(tops, exp_sums, picked, n_row, 3)
+        met_log = beside(log_norm)
+    else:
+        top = lax.pmax(jnp.max(tops, 0), PLANE)
+        log_norm = top + jnp.log(plane_sum(jnp.sum(exp_sums * jnp.exp(tops - top[None]), 0)))
+        picked = plane_sum(picked)
+    loss = jnp.sum(log_norm - picked)
+    final_part, table_ex = head_back(exps, tops, log_norm, target, table_low, ln_fin)
     if tuned:
         final_part = plane_total(final_part.reshape(n_col, n_row, block, width), 2)
-        final_grad = final_part.reshape(length, width).astype(F32)
+        final_grad = final_part.reshape(length, width)
     else:
-        final_grad = plane_sum(final_part).astype(F32)
-    table_ex = mm(logit_grad, ln_fin)
-
-    grad_out, gain_fin, shift_fin = norm_backward(final_grad, norm_fin, inv_fin, small[12])
-    down_grad = grad_out.astype(BF16)
-    act_grad = mm(down_grad, down_full)
-    pre_grad = jax.vjp(gelu_tanh, up_pre)[1](act_grad)[0].astype(BF16)
-    mid_part, gain_two, shift_two = norm_backward(mm_nt(pre_grad, up_full), norm_two, inv_two, small[5])
-    mid_grad = grad_out + mid_part
-    branch_grad = mid_grad.astype(BF16)
-    mixed_grad = mm_nt(branch_grad, attn_full).astype(BF16)
-    packed_grad = attend_back(packed, mixed_grad, log_norm)
-    packed_grad = packed_grad.transpose(1, 0, 2).reshape(length, -1)
-    in_part, gain_one, shift_one = norm_backward(mm_nt(packed_grad, qkv_full), norm_one, inv_one, small[0])
-    grad_in = mid_grad + in_part
-
-    def columns_of(array, at, parts):
-        size = array.shape[1] // parts
-        return lax.dynamic_slice_in_dim(array, at * size, size, 1)
-
-    layer_ex = [
-        mm_tn(columns_of(left, at_left, n_left), columns_of(right, at_right, n_right))
-        for left, at_left, n_left, right, at_right, n_right in (
-            (ln_one, row_at, n_row, packed_grad, col_at, n_col),
-            (mixed, row_at, n_row, branch_grad, col_at, n_col),
-            (ln_two, row_at, n_row, pre_grad, col_at, n_col),
-            (down_grad, col_at, n_col, up_act, row_at, n_row),
+        final_grad = plane_sum(final_part)
+
+    down_grad, pre_grad, up_act, pre_sum, mid_grad, branch_grad, mixed_grad, mid_rows = middle_back(
+        final_grad, stream_out, stream_mid, ln_two, attn_full, up_full, up_bias, down_full, small
+    )
+    packed_grad = attend_back(packed, mixed_grad, attn_log)
+    grad_in, emb_low, emb_grad, start_rows = start_back(packed_grad, qkv_full, mid_grad, stream_in, small)
+    if tuned:
+        met_grad = beside(emb_low)
+        layer_packed, layer_sq = weight_grads(
+            ln_one, mixed, ln_two, packed_grad, branch_grad, pre_grad, down_grad, up_act, row_at, col_at
         )
-    ]
+        layer_sq = jnp.sum(layer_sq)
+    else:
+        all_grads = packed_grad.transpose(1, 0, 2).reshape(length, -1)
+
+        def columns_of(array, at, parts):
+            size = array.shape[1] // parts
+            return lax.dynamic_slice_in_dim(array, at * size, size, 1)
+
+        layer_ex = [
+            mm_tn(columns_of(left, at_left, n_left), columns_of(right, at_right, n_right))
+            for left, at_left, n_left, right, at_right, n_right in (
+                (ln_one, row_at, n_row, all_grads, col_at, n_col),
+                (mixed, row_at, n_row, branch_grad, col_at, n_col),
+                (ln_two, row_at, n_row, pre_grad, col_at, n_col),
+                (down_grad, col_at, n_col, up_act, row_at, n_row),
+            )
+        ]
+        layer_sq = sum(jnp.sum(item * item) for item in layer_ex)
     tok_here, dim_here = pos_table.shape
     pos_ex = lax.dynamic_slice(grad_in, (col_at * tok_here, row_at * dim_here), (tok_here, dim_here))
-    column = lambda item: jnp.sum(item.astype(F32), 0)
-    packed_sums = column(packed_grad).reshape(3, width)
-    small_ex = jnp.stack(
-        [gain_one, shift_one, packed_sums[0], packed_sums[2], column(branch_grad), gain_two, shift_two]
-        + list(column(pre_grad).reshape(-1, width))
-        + [column(down_grad), gain_fin, shift_fin]
+    small_ex = jnp.concatenate(
+        [start_rows[:4], mid_rows[5:6], mid_rows[3:5], pre_sum.reshape(-1, width), mid_rows[2:3], mid_rows[:2]], 0
     )
-    emb_grad = jnp.where(inside[:, None], grad_in.astype(BF16).astype(F32), 0.0)
-    table_ex = table_ex + jnp.zeros_like(table_ex).at[safe_ids].add(emb_grad)
-
-    own_sq = sum(jnp.sum(item * item) for item in [table_ex] + layer_ex)
-    total = plane_sum(jnp.concatenate([weight_sq, own_sq[None]]))
-    weight_total = total[:6]
-    norm_sq = total[6] + jnp.sum(grad_in * grad_in) + jnp.sum(small_ex * small_ex)
-    example_norm = jnp.sqrt(norm_sq)
+    table_ex, own_sq = add_own_rows(table_ex, lists, emb_grad)
+
+    own_sq = jnp.sum(own_sq) + layer_sq
+    same_sq = jnp.sum(start_rows[4]) + jnp.sum(small_ex * small_ex)
     taken = included[0].astype(F32)
+    ex_at = lax.axis_index("dp")
+    leads = (row_at + col_at == 0).astype(F32)
+    at_own = (jnp.arange(n_data) == ex_at).astype(F32)
+    total = jnp.concatenate([at_own * (own_sq + leads * same_sq), at_own * leads * taken, leads * taken * loss[None]])
+    if tuned:
+        total = jnp.pad(total, (0, 1024 - total.shape[0])).reshape(8, 128)
+        total, met_grad = lax.optimization_barrier((total, met_grad))
+        total = sum_small(total, n_row, 4).reshape(-1)
+    else:
+        total = lax.psum(lax.psum(total, PLANE), "dp")
+    norm_sq, taken, loss_sum = total[:n_data], total[n_data : 2 * n_data], total[2 * n_data]
     share = taken * jnp.minimum(1.0, CLIP * lax.rsqrt(norm_sq + 1e-12))
-
-    sums = [
-        example_sum((share * item).astype(BF16)).astype(F32)
-        for item in [table_ex, pos_ex] + layer_ex + [small_ex]
-    ]
-    loss_sum, taken_sum = example_sum(jnp.stack([taken * loss, taken]))
+    example_norm = jnp.sqrt(norm_sq[ex_at])
+    own_share = share[ex_at]
+
     divisor = SAMPLE * n_data
-    grads = [(sums[index] + NOISE * CLIP * noises[index]) / divisor for index in range(6)]
-
-    olds = [
-        (table_rows, table_cols),
-        (pos_rows, pos_cols),
-        (qkv_rows, qkv_cols),
-        (attn_rows, attn_cols),
-        (up_rows, up_cols),
-        (down_rows, down_cols),
-    ]
-    axes = [(PLANE, None), ("col", "row"), ("row", "col"), ("row", "col"), ("row", "col"), ("col", "row")]
-    outputs = []
-    for index in range(6):
-        grad, (old_rows, old_cols), (rows_over, cols_over) = grads[index], olds[index], axes[index]
+    vocab = vocab_here * n_row * n_col
+    count = blocks_of(vocab_here)
+    table_old = jnp.pad(table_rows, (0, count * BLOCK - vocab_here), constant_values=1.0).reshape(count, 1, BLOCK)
+    olds = [(pos_rows, pos_cols), (qkv_rows, qkv_cols), (attn_rows, attn_cols), (up_rows, up_cols)]
+    olds.append((down_rows, down_cols))
+    ends = (token_ids.shape[1] * jnp.sum(taken), example_norm[None])
+    if tuned:
+        core = ex_at % 2
+        to_core = lambda item: lax.ppermute(item, "dp", [(at, at ^ 1) for at in range(4)])
+        halves = (own_share * pack_small(pos_ex, layer_packed, small_ex)).astype(BF16).reshape(2, -1, width)
+        half = (halves[core].astype(F32) + to_core(halves[1 - core]).astype(F32)).astype(BF16)
+        shares = jnp.stack([own_share, share[ex_at ^ 2]])
+        half, shares = lax.optimization_barrier((half, shares))
+        half = (half.astype(F32) + beside(half).astype(F32)).astype(BF16)
+        other_half = to_core(half)
+        packed = jnp.concatenate(
+            [jnp.where(core == 0, half, other_half), jnp.where(core == 0, other_half, half)], 0
+        )
+
+        middle = count // 2
+        spans = [(0, middle), (middle, count - middle)]
+        met = (met_z, met_log, met_target, met_lists, met_grad.astype(F32), shares)
+        pair_sums = [table_sum(table_ex, table_low, *met, *span) for span in spans]
+        pair_sums = [[item, to_core(item)] for item in pair_sums]
+        into, over = None, []
+        for pair, span in zip(pair_sums, spans):
+            into, *more = table_gradient(pair, table_noise, table_old, divisor, *span, into)
+            over.append(more)
+        table_grad = into
+        rows_blocks = jnp.concatenate([item[0] for item in over], 0)
+        cols, scaled, level = (over[0][k] + over[1][k] for k in (1, 2, 3))
+        level = jnp.pad(level[:, :1], ((0, 0), (0, width - 1)))
+        small_grads, smalls, (over_cols, over_rows, squares) = small_gradients(
+            packed, small_params, small_second, small_noise, weights_in[1:], noises[1:], divisor
+        )
+        table_over = jnp.concatenate(
+            [cols, scaled, level, table_sq, squares, table_cols[None], jnp.zeros((2, width), F32)], 0
+        )
+        wide = over_rows.shape[1]
+        lines = [jnp.pad(item, (0, wide - item.shape[0])) for pair in zip(*olds) for item in pair + (pair[0],) * 3]
+        old_lines = jnp.stack(lines)
+        lines, factors = statistics(table_over, over_cols, over_rows, old_lines, small_grads, n_row, vocab, 5)
+        table_new, table_cols_new, rows_new, cols_new, news = update(
+            tok_table, table_grad, rows_blocks, factors, lines, weights_in[1:], small_grads
+        )
+        outputs = [table_grad, rows_blocks.reshape(-1)[:vocab_here], table_cols_new, table_new]
+        for group in zip(small_grads, rows_new, cols_new, news):
+            outputs.extend(group)
+        return tuple(outputs) + tuple(smalls) + (loss_sum,) + ends
+
+    weight_total = plane_sum(
+        jnp.stack([jnp.sum(table_sq)] + [jnp.sum(item * item) for item in weights_in[1:]])
+    )
+    table_sum_all = example_sum((own_share * table_ex.astype(F32)).astype(BF16))
+    others = [(own_share * item).astype(BF16) for item in [pos_ex] + layer_ex + [small_ex]]
+    sums = [example_sum(item).astype(F32) for item in others]
+    grads = [(sums[index] + NOISE * CLIP * noises[index + 1]) / divisor for index in range(5)]
+    table_grad, table_rows_new, *table_over = table_gradient(
+        [table_sum_all], table_noise, table_old, divisor, 0, count
+    )
+    table_rows_new = table_rows_new.reshape(-1)[:vocab_here]
+    by_row = [False, True, True, True, False]
+    over = {"col": [], "row": []}
+    for grad, first in zip(grads, by_row):
         squares = grad * grad + 1e-30
-        row_sum, col_sum = jnp.sum(squares, 1), jnp.sum(squares, 0)
-        n_rows, n_cols = grad.shape[0] * lax.axis_size(rows_over), grad.shape[1]
-        if cols_over is not None:
-            n_cols = n_cols * lax.axis_size(cols_over)
-            row_sum = lax.psum(row_sum, cols_over)
-        col_sum = lax.psum(col_sum, rows_over)
-        rows_new = DECAY * old_rows + (1.0 - DECAY) * (row_sum / n_cols)
-        cols_new = DECAY * old_cols + (1.0 - DECAY) * (col_sum / n_rows)
-        row_mean = lax.psum(jnp.sum(rows_new), rows_over) / n_rows
-        update = grad * lax.rsqrt(rows_new[:, None] * cols_new[None, :] / row_mean)
-        update_total = lax.psum(jnp.sum(update * update), PLANE)
-        entries = n_rows * n_cols
-        size = RATE * jnp.maximum(1e-3, jnp.sqrt(weight_total[index] / entries))
-        size = size / jnp.maximum(1.0, jnp.sqrt(update_total / entries))
-        outputs.extend([grad, rows_new, cols_new, weights_in[index] - size * update])
-    small_grad = (sums[6] + NOISE * CLIP * small_noise) / divisor
+        over["col" if first else "row"].append(jnp.sum(squares, 1))
+        over["row" if first else "col"].append(jnp.sum(squares, 0))
+    over = {axis: [lax.psum(item, axis) for item in items] for axis, items in over.items()}
+    table_over = [plane_sum(item[0]) for item in table_over]
+    news, levels = [], []
+    for index, (grad, first) in enumerate(zip(grads, by_row)):
+        rows_parts, cols_parts = (n_row, n_col) if first else (n_col, n_row)
+        row_sum = over["col" if first else "row"][index]
+        col_sum = over["row" if first else "col"][index]
+        rows_new = DECAY * olds[index][0] + (1.0 - DECAY) * (row_sum / (grad.shape[1] * cols_parts))
+        cols_new = DECAY * olds[index][1] + (1.0 - DECAY) * (col_sum / (grad.shape[0] * rows_parts))
+        news.append((rows_new, cols_new))
+        levels += [
+            jnp.sum(rows_new) / (grad.shape[0] * rows_parts * cols_parts),
+            jnp.sum(grad * grad / (rows_new[:, None] * cols_new[None, :])),
+        ]
+    levels = plane_sum(jnp.stack(levels))
+
+    def updated(index, weight, grad, rows_new, cols_new, level, square_sum, entries_all):
+        size = RATE * jnp.maximum(1e-3, jnp.sqrt(weight_total[index] / entries_all))
+        size = size / jnp.maximum(1.0, jnp.sqrt(square_sum * level / entries_all))
+        size = size * jnp.sqrt(level)
+        return weight - grad * lax.rsqrt(rows_new)[:, None] * (size * lax.rsqrt(cols_new))[None, :]
+
+    table_cols_new = DECAY * table_cols + (1.0 - DECAY) * (table_over[0] / vocab + 1e-30)
+    table_new = updated(
+        0,
+        tok_table,
+        table_grad,
+        table_rows_new,
+        table_cols_new,
+        table_over[2][0] / vocab,
+        jnp.sum(table_over[1] / table_cols_new),
+        vocab * width,
+    )
+    outputs = [table_grad, table_rows_new, table_cols_new, table_new]
+    for index, grad in enumerate(grads):
+        rows_new, cols_new = news[index]
+        weight_new = updated(
+            index + 1,
+            weights_in[index + 1],
+            grad,
+            rows_new,
+            cols_new,
+            levels[2 * index],
+            levels[2 * index + 1],
+            grad.shape[0] * grad.shape[1] * n_row * n_col,
+        )
+        outputs.extend([grad, rows_new, cols_new, weight_new])
+    small_grad = (sums[5] + NOISE * CLIP * small_noise) / divisor
     second_new = DECAY * small_second + (1.0 - DECAY) * (small_grad * small_grad + 1e-30)
     small_update = small_grad * lax.rsqrt(second_new)
     small_update = small_update / jnp.maximum(1.0, jnp.sqrt(jnp.mean(small_update * small_update)))
     small_size = RATE * jnp.maximum(1e-3, jnp.sqrt(jnp.mean(small_params * small_params)))
     small_new = small_params - small_size * small_update
-    return tuple(outputs) + (
-        small_grad,
-        second_new,
-        small_new,
-        loss_sum,
-        taken_sum * length,
-        example_norm[None],
-    )
+    return tuple(outputs) + (small_grad, second_new, small_new, loss_sum) + ends
 
 
 def solution(mesh):

time: 1000 us -> 641 us (0.64)
  Pallas kernels: 220 us -> 481 us
  other arithmetic: 229 us -> 50.2 us
  waiting for transfers between devices: 184 us -> 25.2 us
  blocking collectives: 145 us -> 0 us
  matrix products: 132 us -> 4.31 us
  between operations: 39 us -> 9.62 us
  local copies, waits for them, and re-layouts: 39.4 us -> 49.4 us
    pallas_call x0 -> x16, Pallas kernels: none -> 273 us  [the longest x2 35.4 us: table_sum(): pl.pallas_call(functools.partial(table_sum_kernel, first), grid_spec=pltp...]
    psum x1 -> x0, waiting for transfers between devices: 184 us -> none  [example_sum(): return lax.psum(array, 'dp')]
    psum x9 -> x0, blocking collectives: 128 us -> none  [the longest x2 40.4 us: plane_sum(): return lax.psum(array, PLANE)]
    dot_general x15 -> x1, matrix products: 132 us -> 4.31 us  [dot_f32(): lax.dot_general(left, right, (dims, ((), ())), preferred_element_type=F32)]
    reduce_sum x36 -> x11, other arithmetic: 129 us -> 11.3 us  [the longest x2 3.18 us: token_lists(): order = jnp.sum(jnp.where(at, token[:, None], 0), 0)]
    sub x8 -> x2, other arithmetic: 30.8 us -> 0.6 us  [token_lists(): return (ordered - start, order, bounds)]
    unnamed x165 -> x132, local copies, waits for them, and re-layouts: 1.45 us -> 28.9 us
    ppermute x0 -> x9, waiting for transfers between devices: none -> 25.2 us  [the longest x5 25.2 us: body(): lax.ppermute(item, 'dp', [(at, at ^ 2) for at in range(4)])]
  transfers between devices with their start and end apart: 4 -> 12, of which waited for: 1 -> 1; matrix products, arithmetic and copies ran while one was open for 4% -> 10% of each run, Pallas kernels for 0% -> 41%
where the time goes in v2:
time: 641 us; the launch traced here: 632 us
  Pallas kernels  481 us (75%)
  other arithmetic  50.2 us (8%)
  local copies, waits for them, and re-layouts  49.4 us (8%)
  waiting for transfers between devices  25.2 us (4%)
  starting transfers between devices  12.2 us (2%)
  between operations  9.62 us (2%)
    pallas_call x1, Pallas kernels, front(): pl.pallas_call(functools.partial(front_kernel, n_row), out_shape=[jax.Sha...  99.6 us
    pallas_call x1, Pallas kernels, plane_total(): pl.pallas_call(functools.partial(total_kernel, n_row), out_shape=jax.Shap...  50.9 us
    pallas_call x2, Pallas kernels, table_sum(): pl.pallas_call(functools.partial(table_sum_kernel, first), grid_spec=pltp...  35.4 us
    pallas_call x1, Pallas kernels, attend_back(): pl.pallas_call(attend_back_kernel, grid=(pairs,), out_shape=jax.ShapeDtyp...  34.9 us
    pallas_call x1, Pallas kernels, middle_back(): pl.pallas_call(middle_back_kernel, grid=(hidden // HIDDEN,), out_shape=[s...  33.1 us
    pallas_call x1, Pallas kernels, head_back(): pl.pallas_call(head_back_kernel, grid=(low.shape[0] // BLOCK,), out_shape...  30.1 us
    unnamed x132, local copies, waits for them, and re-layouts  28.9 us
    pallas_call x2, Pallas kernels, table_gradient(): pl.pallas_call(functools.partial(gradient_kernel, limit, len(sums), divis...  25.8 us
  transfers between devices with their start and end apart: 12, of which 1 were waited for; matrix products, arithmetic and copies ran while one was open for 10% of the time, Pallas kernels for 41%

profile of v2, /device:TPU:0, one launch (start us, length us, event | category | flops | bytes accessed | tf_op | source)
XLA Modules:
  0.0 631.6 jit_solution(9219029568677571283)
XLA Ops:
  2.3 5.1 collective-permute-start.3
  19.2 12.1 %gather_fusion = bf16[1024,768]{1,0:T(8,128)(2,1)} fusion(f32[6288,768]{1,0:T(8,128)} %table_ref.3, s32[1024]{0:T(1024)S(1)} %broadcast_clamp_fusion), kind=kCustom, calls=%fused_computation | custom fusion | bytes 3149824 | tf_op jit(solution)/shard_map/jit(_take)/gather | solution.py:1291
  40.9 99.6 %shard_map.517 = (bf16[2,4,128,768]{3,2,1,0:T(8,128)(2,1)S(1)}, bf16[128,768]{1,0:T(8,128)(2,1)}, bf16[4,2,2,48,2304]{4,3,2,1,0:T(8,128)(2,1)S(1)}, bf16[4,2,2,4...) custom-call(bf16[2,4,128,768]{3,2,1,0:T(8,128)(2,1)S(1)} %copy-done.6, ...), custom_call_target="tpu_custom_call" | custom-call | tf_op jit(solution)/shard_map/pallas_call | solution.py:291
  147.0 22.0 %shard_map.518 = (bf16[1024,768]{1,0:T(8,128)(2,1)S(1)}, f32[6,2,1024]{2,1,0:T(2,128)S(1)}) custom-call(bf16[1024,2304]{1,0:T(8,128)(2,1)S(1)} %add_convert_fusion.q_ref.k_ref.v_ref, bf16[1024,2304]{1,0:T(8,128)(2,1)S(1)} %add_convert_fusion.q_ref.k_ref.v_ref, bf16[1024,2304]{1,0:T(8,128)(2,1)S(1)} %add_convert_fusion.q_ref.k_ref.v_ref), custom_call_target="tpu_custom_call" | custom-call | flops 16106127360 | bytes 6291456 | tf_op jit(solution)/shard_map/pallas_call | solution.py:381
  170.3 20.9 %shard_map.519 = (f32[1024,768]{1,0:T(8,128)}, bf16[1024,768]{1,0:T(8,128)(2,1)}, f32[1024,768]{1,0:T(8,128)}, bf16[1024,768]{1,0:T(8,128)(2,1)}) custom-call(bf16[1024,768]{1,0:T(8,128)(2,1)} %bitcast.73, bf16[1024,768]{1,0:T(8,128)(2,1)} %copy-done.15, bf16[768,768]{1,0:T(8,128)(2,1)} %bitcast.90, bf16[768,3072]{1,0:T(8,128)(2,1)} %bitcast.117, ...), custom_call_target="tpu_custom_call" | custom-call | flops 9663676416 | bytes 12582912 | tf_op jit(solution)/shard_map/pallas_call | solution.py:1055
  193.8 23.3 %shard_map.520 = (bf16[6336,768]{1,0:T(8,128)(2,1)}, bf16[6336,1024]{1,0:T(8,128)(2,1)}, f32[6,1,1024]{2,1,0:T(1,128)S(1)}, f32[6,1,1024]{2,1,0:T(1,128)S(1)}, f...) custom-call(f32[6288,768]{1,0:T(8,128)} %table_ref.3, bf16[1024,768]{1,0:T(8,128)(2,1)S(1)} %copy-done.32, ...), custom_call_target="tpu_custom_call" | custom-call | flops 9890168832 | bytes 41852928 | tf_op jit(solution)/shard_map/pallas_call | solution.py:575
  218.9 9.1 %shard_map.521 = (f32[8,128]{1,0:T(8,128)}, f32[8,128]{1,0:T(8,128)}) custom-call(f32[6,8,128]{2,1,0:T(8,128)} %bitcast.83, f32[6,8,128]{2,1,0:T(8,128)} %bitcast.84, f32[8,128]{1,0:T(8,128)} %bitcast.87), custom_call_target="tpu_custom_call" | custom-call | tf_op jit(solution)/shard_map/pallas_call | solution.py:506
  229.4 30.1 %shard_map.522 = (bf16[1024,768]{1,0:T(8,128)(2,1)S(1)}, bf16[6336,768]{1,0:T(8,128)(2,1)}) custom-call(bf16[6336,1024]{1,0:T(8,128)(2,1)} %get-tuple-element.118.exp_ref, f32[6,1,1024]{2,1,0:T(1,128)S(1)} %copy-done.27, f32[1,1024]{1,0:T(1,128)S(1)} %bitcast.85, s32[1,1024]{1,0:T(1,128)S(1)} %and_select_fusion.1.target_ref, ...), custom_call_target="tpu_custom_call" | custom-call | flops 19931332608 | bytes 32440320 | tf_op jit(solution)/shard_map/pallas_call | solution.py:618
  259.5 50.9 %shard_map.523 = bf16[2,4,128,768]{3,2,1,0:T(8,128)(2,1)S(1)} custom-call(bf16[2,4,128,768]{3,2,1,0:T(8,128)(2,1)S(1)} %bitcast.81), custom_call_target="tpu_custom_call" | custom-call | tf_op jit(solution)/shard_map/pallas_call | solution.py:329
  311.6 33.1 %shard_map.524 = (bf16[1024,768]{1,0:T(8,128)(2,1)}, bf16[1024,3072]{1,0:T(8,128)(2,1)}, bf16[1024,3072]{1,0:T(8,128)(2,1)}, f32[1,3072]{1,0:T(1,128)}, f32[1024...) custom-call(bf16[1024,768]{1,0:T(8,128)(2,1)} %bitcast.80, ...), custom_call_target="tpu_custom_call" | custom-call | flops 14495514624 | bytes 31457280 | tf_op jit(solution)/shard_map/pallas_call | solution.py:1124
  346.2 34.9 %shard_map.525.packed_ref.refs_0_.refs_1_.refs_2_ = bf16[3,1024,768]{2,1,0:T(8,128)(2,1)} custom-call(bf16[1024,2304]{1,0:T(8,128)(2,1)} %copy-done.37, bf16[1024,2304]{1,0:T(8,128)(2,1)} %copy-done.37, bf16[1024,2304]{1,0:T(8,128)(2,1)} %copy-done.37, bf16[1024,768]{1,0:T(8,128)(2,1)S(1)} %copy-done.38, f32[6,2,1024]{2,1,0:T(2,128)S(1)} %get-tuple-element.130.log_ref), custom_call_target="tpu_custom_call" | custom-call | flops 24159191040 | bytes 12582912 | tf_op jit(solution)/shard_map/pallas_call | solution.py:426
  381.1 9.5 %shard_map.526 = (f32[1024,768]{1,0:T(8,128)S(1)}, bf16[1024,768]{1,0:T(8,128)(2,1)S(1)}, f32[1024,768]{1,0:T(8,128)S(1)}, f32[8,768]{1,0:T(8,128)S(1)}) custom-call(bf16[3,1024,768]{2,1,0:T(8,128)(2,1)} %shard_map.525.packed_ref.refs_0_.refs_1_.refs_2_, bf16[768,2304]{1,0:T(8,128)(2,1)} %bitcast.89, f32[1024,768]{1,0:T(8,128)S(1)} %copy-done.36, ...), custom_call_target="tpu_custom_call" | custom-call | flops 3623878656 | bytes 15728640 | tf_op jit(solution)/shard_map/pallas_call | solution.py:1162
  399.7 11.9 %shard_map.527 = (bf16[6336,768]{1,0:T(8,128)(2,1)}, f32[1,768]{1,0:T(1,128)}) custom-call(s32[1024]{0:T(1024)} %broadcast_subtract_fusion.ids_ref, s32[1024]{0:T(1024)} %get-tuple-element.288.order_ref, s32[7]{0:T(128)} %get-tuple-element.292.bounds_ref, bf16[6336,768]{1,0:T(8,128)(2,1)} %get-tuple-element.124.table_ref, f32[1024,768]{1,0:T(8,128)} %copy-done.13), custom_call_target="tpu_custom_call" | custom-call | bytes 19464192 | tf_op jit(solution)/shard_map/pallas_call | solution.py:671
  414.7 10.9 %shard_map.528 = (f32[1152,768]{1,0:T(8,128)}, f32[1,384]{1,0:T(1,128)}) custom-call(s32[4]{0:T(128)} %pad_add_fusion.1.place_ref, bf16[1024,768]{1,0:T(8,128)(2,1)} %add_convert_fusion.1.ones_ref, bf16[1024,768]{1,0:T(8,128)(2,1)} %copy-done.15, bf16[1024,768]{1,0:T(8,128)(2,1)} %get-tuple-element.128.refs_3_.low_ref, ...), custom_call_target="tpu_custom_call" | custom-call | flops 2415919104 | bytes 12582912 | tf_op jit(solution)/shard_map/pallas_call | solution.py:1211
  431.5 11.0 %shard_map.529 = f32[8,128]{1,0:T(8,128)} custom-call(f32[8,128]{1,0:T(8,128)} %fusion.13.value), custom_call_target="tpu_custom_call" | custom-call | tf_op jit(solution)/shard_map/pallas_call | solution.py:468
  444.6 7.4 %fusion.1 = bf16[1440,768]{1,0:T(8,128)(2,1)S(1)} fusion(f32[14,768]{1,0:T(8,128)S(1)} %concatenate.33, f32[128,256]{1,0:T(8,128)S(1)} %get-tuple-element.301, f32[128,256]{1,0:T(8,128)S(1)} %get-tuple-element.300, f32[128,256]{1,0:T(8,128)S(1)} %get-tuple-element.299, f32[128,256]{1,0:T(8,128)S(1)} %get-tuple-element.298, ...), kind=kLoop, calls=%fused_computation.9 | loop fusion | flops 14376960 | bytes 6318084 | tf_op jit(solution)/shard_map/convert_element_type | solution.py:1404
  460.7 17.5 %shard_map.531.refs_0_ = bf16[3168,768]{1,0:T(8,128)(2,1)} custom-call(s32[1024]{0:T(1024)S(1)} %broadcast_subtract_fusion.1.ids_ref, s32[1024]{0:T(1024)S(1)} %get-tuple-element.290.order_ref, s32[7]{0:T(128)S(1)} %get-tuple-element.293.bounds_ref, f32[2]{0:T(128)S(1)} %pad_maximum_fusion.4.share_ref, bf16[6336,768]{1,0:T(8,128)(2,1)} %get-tuple-element.123.low_ref.refs_0_, ...), custom_call_target="tpu_custom_call" | custom-call | flops 9965666304 | bytes 14598144 | tf_op jit(solution)/shard_map/pallas_call | solution.py:698
  478.4 17.9 %shard_map.530.refs_0_ = bf16[3168,768]{1,0:T(8,128)(2,1)} custom-call(s32[1024]{0:T(1024)S(1)} %broadcast_subtract_fusion.1.ids_ref, s32[1024]{0:T(1024)S(1)} %get-tuple-element.290.order_ref, s32[7]{0:T(128)S(1)} %get-tuple-element.293.bounds_ref, f32[2]{0:T(128)S(1)} %pad_maximum_fusion.4.share_ref, bf16[6336,768]{1,0:T(8,128)(2,1)} %get-tuple-element.123.low_ref.refs_0_, ...), custom_call_target="tpu_custom_call" | custom-call | flops 9965666304 | bytes 14598144 | tf_op jit(solution)/shard_map/pallas_call | solution.py:698
  498.1 25.2 %collective-permute-done.10 = bf16[720,768]{1,0:T(8,128)(2,1)S(1)} collective-permute-done((bf16[720,768]{1,0:T(8,128)(2,1)S(1)}, bf16[720,768]{1,0:T(8,128)(2,1)S(1)}, u32[]{:S(2)}, u32[]{:S(2)}) %collective-permute-start.10) | collective-permute-done | bytes 1105952 | tf_op jit(solution)/shard_map/ppermute | solution.py:1279
  533.3 5.1 shard_map.534
  541.9 13.0 %shard_map.532 = (f32[6288,768]{1,0:T(8,128)}, f32[3,1,1056]{2,1,0:T(1,128)S(1)}, f32[1,768]{1,0:T(1,128)S(1)}, f32[1,768]{1,0:T(1,128)S(1)}, f32[1,128]{1,0:T(1,128)S(1)}) custom-call(bf16[3168,768]{1,0:T(8,128)(2,1)S(1)} %copy-done.7, bf16[3168,768]{1,0:T(8,128)(2,1)} %collective-permute-done.9.refs_1_, f32[6288,768]{1,0:T(8,128)} %refs_2_.5, ...), custom_call_target="tpu_custom_call" | custom-call | bytes 29196288 | tf_op jit(solution)/shard_map/pallas_call | solution.py:750
  554.9 12.8 %shard_map.533 = (f32[6288,768]{1,0:T(8,128)}, f32[3,1,1056]{2,1,0:T(1,128)S(1)}, f32[1,768]{1,0:T(1,128)S(1)}, f32[1,768]{1,0:T(1,128)S(1)}, f32[1,128]{1,0:T(1,128)S(1)}) custom-call(bf16[3168,768]{1,0:T(8,128)(2,1)S(1)} %bitcast.76, bf16[3168,768]{1,0:T(8,128)(2,1)} %collective-permute-done.8.refs_1_, ...), custom_call_target="tpu_custom_call", output_to_operand_aliasing={{0}: (4, {})} | custom-call | bytes 29196288 | tf_op jit(solution)/shard_map/pallas_call | solution.py:750
  570.5 23.6 %shard_map.535 = (f32[16,1536]{1,0:T(8,128)S(1)}, f32[8,768]{1,0:T(8,128)S(1)}) custom-call(f32[8,768]{1,0:T(8,128)S(1)} %concatenate.40.refs_0_, f32[8,768]{1,0:T(8,128)S(1)} %get-tuple-element.163.refs_1_, f32[8,1536]{1,0:T(8,128)S(1)} %get-tuple-element.164.refs_2_, f32[16,1536]{1,0:T(8,128)S(1)} %stack.94.refs_3_, ...), custom_call_target="tpu_custom_call" | custom-call | tf_op jit(solution)/shard_map/pallas_call | solution.py:932
  595.4 23.4 %shard_map.536 = (f32[6288,768]{1,0:T(8,128)}, f32[1,768]{1,0:T(1,128)}, f32[1,512]{1,0:T(1,128)}, f32[1,192]{1,0:T(1,128)}, f32[1,192]{1,0:T(1,128)}, /*index=5...) custom-call(f32[6288,768]{1,0:T(8,128)} %table_ref.3, ...), custom_call_target="tpu_custom_call" | custom-call | bytes 57950208 | tf_op jit(solution)/shard_map/pallas_call | solution.py:973
  (258 shorter events, 91.7 us)
Async XLA Ops:
  2.3 35.9 %collective-permute-start.3 = (f32[128,192]{1,0:T(8,128)S(1)}, f32[128,192]{1,0:T(8,128)}, u32[]{:S(2)}, u32[]{:S(2)}) collective-permute-start(f32[128,192]{1,0:T(8,128)S(1)} %bitcast.96), channel_id=1, source_target_pairs={{0,6},{2,4},{4,2},{6,0},{1,7},{3,5},{5,3},{7,1},{8,14},{10,12},{12... | collective-permute-start | bytes 294920 | tf_op jit(solution)/shard_map/ppermute | solution.py:1298
  7.5 30.7 %collective-permute-start.1 = (f32[128,192]{1,0:T(8,128)S(1)}, f32[128,192]{1,0:T(8,128)}, u32[]{:S(2)}, u32[]{:S(2)}) collective-permute-start(f32[128,192]{1,0:T(8,128)S(1)} %bitcast.97), channel_id=1, source_target_pairs={{0,2},{2,0},{4,6},{6,4},{1,3},{3,1},{5,7},{7,5},{8,10},{10,8},{12,... | collective-permute-start | bytes 294920 | tf_op jit(solution)/shard_map/ppermute | solution.py:1298
  7.7 30.5 %collective-permute-start.2 = (f32[128,192]{1,0:T(8,128)S(1)}, f32[128,192]{1,0:T(8,128)}, u32[]{:S(2)}, u32[]{:S(2)}) collective-permute-start(f32[128,192]{1,0:T(8,128)S(1)} %bitcast.98), channel_id=1, source_target_pairs={{0,4},{2,6},{4,0},{6,2},{1,5},{3,7},{5,1},{7,3},{8,12},{10,14},{12... | collective-permute-start | bytes 294920 | tf_op jit(solution)/shard_map/ppermute | solution.py:1298
  9.0 28.4 %collective-permute-start = (s32[2,1024]{1,0:T(2,128)S(1)}, s32[2,1024]{1,0:T(2,128)S(1)}, u32[]{:S(2)}, u32[]{:S(2)}) collective-permute-start(s32[2,1024]{1,0:T(2,128)S(1)} %pad_add_fusion), channel_id=1, source_target_pairs={{0,16},{8,24},{16,0},{24,8},{1,17},{9,25},{17,1},{25,9},{2,18},{10... | collective-permute-start | bytes 24584 | tf_op jit(solution)/shard_map/ppermute | solution.py:1279
  191.1 269.6 %collective-permute-start.6 = (bf16[1024,768]{1,0:T(8,128)(2,1)}, bf16[1024,768]{1,0:T(8,128)(2,1)}, u32[]{:S(2)}, u32[]{:S(2)}) collective-permute-start(bf16[1024,768]{1,0:T(8,128)(2,1)} %get-tuple-element.117.z_ref), channel_id=1, source_target_pairs={{0,16},{8,24},{16,0},{24,8},{1,17},{9,25},{17,1},{25,9},{2,18},{10... | collective-permute-start | bytes 4718600 | tf_op jit(solution)/shard_map/ppermute | solution.py:1279
  193.8 34.2 %copy-start.33 = (bf16[1024,768]{1,0:T(8,128)(2,1)S(1)}, bf16[1024,768]{1,0:T(8,128)(2,1)}, u32[]{:S(2)}) copy-start(bf16[1024,768]{1,0:T(8,128)(2,1)} %get-tuple-element.117.z_ref) | copy-start | bytes 4718596
  346.2 34.9 %copy-start.1 = (bf16[2,4,128,768]{3,2,1,0:T(8,128)(2,1)S(1)}, bf16[2,4,128,768]{3,2,1,0:T(8,128)(2,1)}, u32[]{:S(2)}) copy-start(bf16[2,4,128,768]{3,2,1,0:T(8,128)(2,1)} %copy-done) | copy-start | bytes 4718596
  346.2 34.9 %copy-start.20 = (f32[14,768]{1,0:T(8,128)S(1)}, f32[14,768]{1,0:T(8,128)}, u32[]{:S(2)}) copy-start(f32[14,768]{1,0:T(8,128)} %refs_1_.2) | copy-start | bytes 129028
  346.2 34.9 %copy-start.36 = (f32[1024,768]{1,0:T(8,128)S(1)}, f32[1024,768]{1,0:T(8,128)}, u32[]{:S(2)}) copy-start(f32[1024,768]{1,0:T(8,128)} %get-tuple-element.131.mid_grad_ref) | copy-start | bytes 9437188
  396.4 35.1 %collective-permute-start.4 = (bf16[1024,768]{1,0:T(8,128)(2,1)}, bf16[1024,768]{1,0:T(8,128)(2,1)}, u32[]{:S(2)}, u32[]{:S(2)}) collective-permute-start(bf16[1024,768]{1,0:T(8,128)(2,1)} %copy-done.34), channel_id=1, source_target_pairs={{0,16},{8,24},{16,0},{24,8},{1,17},{9,25},{17,1},{25,9},{2,18},{10... | collective-permute-start | bytes 4718600 | tf_op jit(solution)/shard_map/ppermute | solution.py:1279
  453.4 5.7 collective-permute-start.5
  455.4 5.3 collective-permute-start.7
  478.2 61.1 %collective-permute-start.9 = (bf16[3168,768]{1,0:T(8,128)(2,1)}, bf16[3168,768]{1,0:T(8,128)(2,1)}, u32[]{:S(2)}, u32[]{:S(2)}) collective-permute-start(bf16[3168,768]{1,0:T(8,128)(2,1)} %shard_map.531.refs_0_), channel_id=1, source_target_pairs={{0,8},{8,0},{16,24},{24,16},{1,9},{9,1},{17,25},{25,17},{2,10},{10... | collective-permute-start | bytes 14598152 | tf_op jit(solution)/shard_map/ppermute | solution.py:1403
  496.4 29.0 %copy-start.58 = (f32[192]{0:T(256)S(1)}, f32[192]{0:T(256)}, u32[]{:S(2)}) copy-start(f32[192]{0:T(256)} %param.48) | copy-start | bytes 2308
  496.4 29.0 %copy-start.54 = (f32[384]{0:T(512)S(1)}, f32[384]{0:T(512)}, u32[]{:S(2)}) copy-start(f32[384]{0:T(512)} %param.50) | copy-start | bytes 4612
  496.4 29.0 %copy-start.59 = (f32[192]{0:T(256)S(1)}, f32[192]{0:T(256)}, u32[]{:S(2)}) copy-start(f32[192]{0:T(256)} %param.43) | copy-start | bytes 2308
  496.4 29.0 %copy-start.49 = (f32[1152]{0:T(1024)S(1)}, f32[1152]{0:T(1024)}, u32[]{:S(2)}) copy-start(f32[1152]{0:T(1024)} %param.45) | copy-start | bytes 13828
  496.4 29.1 %copy-start.55 = (f32[384]{0:T(512)S(1)}, f32[384]{0:T(512)}, u32[]{:S(2)}) copy-start(f32[384]{0:T(512)} %param.47) | copy-start | bytes 4612
  496.4 29.1 %copy-start.50 = (f32[768]{0:T(1024)S(1)}, f32[768]{0:T(1024)}, u32[]{:S(2)}) copy-start(f32[768]{0:T(1024)} %param.51) | copy-start | bytes 9220
  496.4 29.1 %copy-start.48 = (f32[1536]{0:T(1024)S(1)}, f32[1536]{0:T(1024)}, u32[]{:S(2)}) copy-start(f32[1536]{0:T(1024)} %param.49) | copy-start | bytes 18436
  496.4 58.5 %collective-permute-start.8 = (bf16[3168,768]{1,0:T(8,128)(2,1)}, bf16[3168,768]{1,0:T(8,128)(2,1)}, u32[]{:S(2)}, u32[]{:S(2)}) collective-permute-start(bf16[3168,768]{1,0:T(8,128)(2,1)} %shard_map.530.refs_0_), channel_id=1, source_target_pairs={{0,8},{8,0},{16,24},{24,16},{1,9},{9,1},{17,25},{25,17},{2,10},{10... | collective-permute-start | bytes 14598152 | tf_op jit(solution)/shard_map/ppermute | solution.py:1403
  496.7 26.6 %collective-permute-start.10 = (bf16[720,768]{1,0:T(8,128)(2,1)S(1)}, bf16[720,768]{1,0:T(8,128)(2,1)S(1)}, u32[]{:S(2)}, u32[]{:S(2)}) collective-permute-start(bf16[720,768]{1,0:T(8,128)(2,1)S(1)} %fusion.12), channel_id=1, source_target_pairs={{0,16},{8,24},{16,0},{24,8},{1,17},{9,25},{17,1},{25,9},{2,18},{10... | collective-permute-start | bytes 3317768 | tf_op jit(solution)/shard_map/ppermute | solution.py:1279
  524.6 4.3 collective-permute-start.11
  538.4 29.6 %copy-start.9 = (f32[512,192]{1,0:T(8,128)}, f32[512,192]{1,0:T(8,128)S(1)}, u32[]{:S(2)}) copy-start(f32[512,192]{1,0:T(8,128)S(1)} %get-tuple-element.256.refs_4_.refs_5_) | copy-start | bytes 1179652
  (50 other events, 426.0 us)

commit v3 on v2

--- a/solution.py
+++ b/solution.py
@@ -137,14 +137,21 @@
                 steps.remove(step)
 
 
-def scatter_sum(link, base, n_row, part, from_col, ins, outs, own):
+def scatter_sum(link, base, n_row, part, from_col, ins, outs, own, make=None):
     row, col = link.row, link.col
     (up_in, down_in), (up_out, down_out) = ins, outs
     y_base, up_base, down_base = base, base + n_row, base + 2 * n_row
     order = [at for k in range(n_row // 2) for at in (n_row - 1 - k, k)]
     for at in order:
+        if make is not None:
+            make(1 - col, at)
         link.send(part.at[1 - col, at], from_col.at[at], y_base + at, link.device(col=1 - col))
     yield
+    if make is not None:
+        for k, at in enumerate(order):
+            make(col, at)
+            if k % 2:
+                yield
     waiting = list(order)
 
     def mine(at):
@@ -256,21 +263,81 @@
 N_MATRIX = 4 * 4 + 2
 
 
-def front_kernel(n_row, looked, pos, *refs):
-    shards, (start, own_rows), wholes = refs[:4], refs[4:6], refs[6:10]
-    from_col, up_in, down_in, up_out, down_out, own, own_low, send_sems, recv_sems, local_sems = refs[10:]
+def front_kernel(n_row, ids, table, pos, *refs):
+    shards, (start, low, square), wholes = refs[:4], refs[4:7], refs[7:11]
+    held, staged, row_block_ref, pos_in, looked = refs[11:16]
+    from_col, up_in, down_in, up_out, down_out, own, own_low = refs[16:23]
+    send_sems, recv_sems, local_sems, table_sems, low_sems = refs[23:]
+    limit, width = table.shape
+    block = own.shape[0]
+    piece = limit // table_sems.shape[0]
+    loads = [
+        pltpu.make_async_copy(table.at[pl.ds(at, piece)], held.at[pl.ds(at, piece)], table_sems.at[k])
+        for k, at in enumerate(range(0, limit, piece))
+    ]
+    for load in loads:
+        load.start()
     link = Link(send_sems, recv_sems)
+    row_peers = [(link.row + k) % n_row for k in range(1, n_row)]
     link.greet(
-        link.plane_neighbours(n_row)
+        [(link.device(row=peer), None) for peer in row_peers]
+        + [(link.device(col=1 - link.col), None)]
         + [(link.device(dp=link.beside), None), (link.device(dp=link.sibling), None)]
     )
+    first = (link.col * n_row + link.row) * limit
+    pos_base = 5 * n_row + 4 * N_MATRIX
+
+    def look_up(col, at):
+        token = (col * n_row + at) * block
+
+        def step(k, carry):
+            entry = ids[token + k] - first
+            inside = (entry >= 0) & (entry < limit)
+            row = held[pl.ds(jnp.clip(entry, 0, limit - 1), 1), :]
+            row_block_ref[pl.ds(k, 1), :] = jnp.where(inside, row, 0.0)
+            return carry
+
+        lax.fori_loop(0, block, step, 0, unroll=8)
+        looked[col, at] = row_block_ref[...].astype(BF16)
 
     def tokens():
-        yield from scatter_sum(link, 0, n_row, looked, from_col, (up_in, down_in), (up_out, down_out), own)
-        own_rows[...] = own[...].astype(BF16)
-        own_low[...] = (own[...] + pos[...]).astype(BF16)
+        for peer in row_peers:
+            rows = pos.at[pl.ds(pl.multiple_of(peer * block, 8), block)]
+            link.send(rows, pos_in.at[link.row], pos_base + link.row, link.device(row=peer))
+        pos_in[link.row] = pos[pl.ds(pl.multiple_of(link.row * block, 8), block), :]
+        for load in loads:
+            load.wait()
+        yield from scatter_sum(
+            link, 0, n_row, looked, from_col, (up_in, down_in), (up_out, down_out), own, look_up
+        )
+        for peer in row_peers:
+            link.landed(pos_in.at[peer], pos_base + peer)
+        pos_own = jnp.concatenate([pos_in[k] for k in range(n_row)], 1)
+        own_low[...] = (own[...] + pos_own).astype(BF16)
         start[link.col, link.row] = own_low[...]
         yield from spread(link, 3 * n_row, n_row, own_low, lambda r, c: start.at[c, r])
+
+    def shorten():
+        yield
+        square[...] = jnp.zeros_like(square)
+        count = low.shape[0] // BLOCK
+        stores = []
+        for k in range(count):
+            rows = min(BLOCK, limit - k * BLOCK)
+            if k > 1:
+                stores[k - 2].wait()
+            part = held[k * BLOCK : k * BLOCK + rows, :]
+            square[...] += jnp.sum(part * part, 0, keepdims=True)
+            if rows < BLOCK:
+                staged[k % 2, rows:] = jnp.zeros((BLOCK - rows, width), BF16)
+            staged[k % 2, :rows] = part.astype(BF16)
+            stores.append(
+                pltpu.make_async_copy(staged.at[k % 2], low.at[pl.ds(k * BLOCK, BLOCK)], low_sems.at[k % 2])
+            )
+            stores[k].start()
+            yield
+        for store in stores[-2:]:
+            store.wait()
 
     matrices = [
         spread_matrix(
@@ -278,33 +345,41 @@
         )
         for index in range(4)
     ]
-    run_together(tokens(), *matrices)
+    run_together(*matrices, tokens(), shorten())
     link.finish()
 
 
-def front(looked, pos, shards, n_row):
-    block, width = looked.shape[2:]
+def front(ids, table, pos, shards, n_row):
+    limit, width = table.shape
+    block = ids.shape[0] // (2 * n_row)
+    low = (pl.cdiv(limit, BLOCK) * BLOCK, width)
     wholes = [(n_row, 2, 2) + shard.shape[1:2] + (2 * shard.shape[2],) for shard in shards[:3]]
     wholes.append((2, 2, 2) + shards[3].shape[1:2] + (n_row * shards[3].shape[2],))
     rows = pltpu.VMEM((n_row, block, width), BF16)
     vmem, hbm = pl.BlockSpec(memory_space=pltpu.VMEM), pl.BlockSpec(memory_space=pl.ANY)
+    shape = jax.ShapeDtypeStruct
     return pl.pallas_call(
         functools.partial(front_kernel, n_row),
-        out_shape=[jax.ShapeDtypeStruct(looked.shape, BF16), jax.ShapeDtypeStruct((block, width), BF16)]
-        + [jax.ShapeDtypeStruct(shape, BF16) for shape in wholes],
-        in_specs=[vmem, vmem] + [hbm] * 4,
-        out_specs=[vmem, vmem] + [hbm] * 4,
-        scratch_shapes=[rows] * 5
+        out_shape=[shape((2, n_row, block, width), BF16), shape(low, BF16), shape((1, width), F32)]
+        + [shape(whole, BF16) for whole in wholes],
+        in_specs=[pl.BlockSpec(memory_space=pltpu.SMEM), hbm, vmem] + [hbm] * 4,
+        out_specs=[vmem, hbm, vmem] + [hbm] * 4,
+        scratch_shapes=[pltpu.VMEM(table.shape, F32), pltpu.VMEM((2, BLOCK, width), BF16)]
+        + [pltpu.VMEM((block, width), F32), pltpu.VMEM((n_row, block) + pos.shape[1:], F32)]
+        + [pltpu.VMEM((2, n_row, block, width), BF16)]
+        + [rows] * 5
         + [pltpu.VMEM((block, width), F32), pltpu.VMEM((block, width), BF16)]
         + [
             pltpu.SemaphoreType.DMA((220,)),
-            pltpu.SemaphoreType.DMA((5 * n_row + 4 * N_MATRIX,)),
+            pltpu.SemaphoreType.DMA((6 * n_row + 4 * N_MATRIX,)),
             pltpu.SemaphoreType.DMA((4, 2)),
+            pltpu.SemaphoreType.DMA((6,)),
+            pltpu.SemaphoreType.DMA((2,)),
         ],
         compiler_params=pltpu.CompilerParams(
-            collective_id=1, has_side_effects=True, vmem_limit_bytes=40 * 1024 * 1024
+            collective_id=1, has_side_effects=True, vmem_limit_bytes=56 * 1024 * 1024
         ),
-    )(looked, pos, *shards)
+    )(ids, table, pos, *shards)
 
 
 def total_kernel(n_row, part, total, *refs):
@@ -340,7 +415,8 @@
     )(part)
 
 
-QUERIES = 256
+FORWARD_QUERIES = 512
+BACK_QUERIES = 256
 
 
 def causal(scores):
@@ -349,28 +425,39 @@
     return jnp.where(keys <= queries, scores, -1e30)
 
 
+def lanes_of(head):
+    return slice(head * HEAD, (head + 1) * HEAD)
+
+
 def attend_kernel(q_ref, k_ref, v_ref, o_ref, log_ref):
-    length = q_ref.shape[0]
-    for head in range(2):
-        lanes = slice(head * HEAD, (head + 1) * HEAD)
-        keys, values = k_ref[:, lanes], v_ref[:, lanes].T
-        for at in range(0, length, QUERIES):
-            here = slice(at, at + QUERIES)
-            queries = q_ref[here, lanes] * HEAD ** (-0.5)
-            edge = causal(mm_nt(keys[here], queries))
-            top = jnp.max(edge, 0, keepdims=True)
-            if at:
-                before = mm_nt(keys[:at], queries)
-                top = jnp.maximum(top, jnp.max(before, 0, keepdims=True))
-            edge = jnp.exp(edge - top)
-            count = jnp.sum(edge, 0, keepdims=True)
-            mixed = mm(values[:, here], edge.astype(BF16))
-            if at:
-                before = jnp.exp(before - top)
-                count = count + jnp.sum(before, 0, keepdims=True)
-                mixed = mixed + mm(values[:, :at], before.astype(BF16))
-            o_ref[here, lanes] = (mixed / count).T.astype(BF16)
-            log_ref[0, head : head + 1, here] = top + jnp.log(count)
+    size = FORWARD_QUERIES
+    values = [v_ref[:, lanes_of(head)].T for head in range(2)]
+    steps = [(head, at) for head in range(2) for at in range(0, q_ref.shape[0], size)]
+
+    def scores_of(head, at):
+        queries = q_ref[at : at + size, lanes_of(head)] * HEAD ** (-0.5)
+        return mm_nt(k_ref[: at + size, lanes_of(head)], queries)
+
+    later = scores_of(*steps[0])
+    for k, (head, at) in enumerate(steps):
+        scores = later
+        if k + 1 < len(steps):
+            later = scores_of(*steps[k + 1])
+        here = slice(at, at + size)
+        edge = causal(scores[at:])
+        top = jnp.max(edge, 0, keepdims=True)
+        if at:
+            top = jnp.maximum(top, jnp.max(scores[:at], 0, keepdims=True))
+        exps = jnp.exp(edge - top)
+        count = jnp.sum(exps, 0, keepdims=True)
+        exps = exps.astype(BF16)
+        if at:
+            before = jnp.exp(scores[:at] - top)
+            count = count + jnp.sum(before, 0, keepdims=True)
+            exps = jnp.concatenate([before.astype(BF16), exps], 0)
+        mixed = mm(values[head][:, : at + size], exps)
+        o_ref[here, lanes_of(head)] = (mixed / count).T.astype(BF16)
+        log_ref[0, head : head + 1, here] = top + jnp.log(count)
 
 
 def attend(packed):
@@ -393,29 +480,40 @@
 
 
 def attend_back_kernel(q_ref, k_ref, v_ref, g_ref, log_ref, out_ref, key_sum, value_sum):
-    length = q_ref.shape[0]
-    for head in range(2):
-        lanes = slice(head * HEAD, (head + 1) * HEAD)
-        keys, values = k_ref[:, lanes], v_ref[:, lanes]
-        keys_turned = keys.T
-        key_sum[...] = jnp.zeros_like(key_sum)
-        value_sum[...] = jnp.zeros_like(value_sum)
-        for at in range(0, length, QUERIES):
-            here, seen = slice(at, at + QUERIES), slice(0, at + QUERIES)
-            queries, grads = q_ref[here, lanes] * HEAD ** (-0.5), g_ref[here, lanes]
-            log_norm = log_ref[0, head : head + 1, here]
-            probs = jnp.exp(causal(mm_nt(keys[here], queries)) - log_norm)
-            if at:
-                probs = jnp.concatenate([jnp.exp(mm_nt(keys[:at], queries) - log_norm), probs], 0)
-            prob_grad = mm_nt(values[seen], grads)
-            level = jnp.sum(probs * prob_grad, 0, keepdims=True)
-            score_grad = (probs * (prob_grad - level)).astype(BF16)
-            value_sum[seen] += mm(probs.astype(BF16), grads)
-            key_sum[seen] += mm(score_grad, queries)
-            query_grad = mm(keys_turned[:, seen], score_grad) * HEAD ** (-0.5)
-            out_ref[0, here, lanes] = query_grad.T.astype(BF16)
-        out_ref[1, :, lanes] = key_sum[...].astype(BF16)
-        out_ref[2, :, lanes] = value_sum[...].astype(BF16)
+    length, size = q_ref.shape[0], BACK_QUERIES
+    keys_turned = [k_ref[:, lanes_of(head)].T for head in range(2)]
+    steps = [(head, at) for head in range(2) for at in range(0, length, size)]
+
+    def products_of(head, at):
+        queries = q_ref[at : at + size, lanes_of(head)] * HEAD ** (-0.5)
+        grads = g_ref[at : at + size, lanes_of(head)]
+        scores = mm_nt(k_ref[: at + size, lanes_of(head)], queries)
+        return scores, mm_nt(v_ref[: at + size, lanes_of(head)], grads), queries, grads
+
+    later = products_of(*steps[0])
+    for k, (head, at) in enumerate(steps):
+        scores, prob_grad, queries, grads = later
+        if k + 1 < len(steps):
+            later = products_of(*steps[k + 1])
+        here = slice(at, at + size)
+        log_norm = log_ref[0, head : head + 1, here]
+        probs = jnp.exp(causal(scores[at:]) - log_norm)
+        if at:
+            probs = jnp.concatenate([jnp.exp(scores[:at] - log_norm), probs], 0)
+        level = jnp.sum(probs * prob_grad, 0, keepdims=True)
+        score_grad = (probs * (prob_grad - level)).astype(BF16)
+        value_grad = mm(probs.astype(BF16), grads)
+        key_grad = mm(score_grad, queries)
+        query_grad = mm(keys_turned[head][:, : at + size], score_grad) * HEAD ** (-0.5)
+        out_ref[0, here, lanes_of(head)] = query_grad.T.astype(BF16)
+        if at:
+            value_sum[head, :at] += value_grad[:at]
+            key_sum[head, :at] += key_grad[:at]
+        value_sum[head, here] = value_grad[at:]
+        key_sum[head, here] = key_grad[at:]
+        if at + size == length:
+            out_ref[1, :, lanes_of(head)] = key_sum[head].astype(BF16)
+            out_ref[2, :, lanes_of(head)] = value_sum[head].astype(BF16)
 
 
 def attend_back(packed, mixed_grad, log_norm):
@@ -430,18 +528,20 @@
         in_specs=[column(0), column(pairs), column(2 * pairs), column(0)]
         + [pl.BlockSpec((1, 2, length), lambda i: (i, 0, 0))],
         out_specs=pl.BlockSpec((3, length, lanes), lambda i: (0, 0, i)),
-        scratch_shapes=[pltpu.VMEM((length, HEAD), F32)] * 2,
+        scratch_shapes=[pltpu.VMEM((2, length, HEAD), F32)] * 2,
         cost_estimate=cost(30 * length * length * width, 16 * length * width),
         compiler_params=pltpu.CompilerParams(vmem_limit_bytes=48 * 1024 * 1024),
     )(packed, packed, packed, mixed_grad, log_norm)
 
 
-def meet(link, base, value, slots, me, peers):
-    slots[me] = value[...]
-    for _, device in peers:
-        link.send(value, slots.at[me], base + me, device)
-    for index, _ in peers:
-        link.landed(slots.at[index], base + index)
+def meet(link, *exchanges):
+    for base, value, slots, me, peers in exchanges:
+        slots[me] = value[...]
+        for _, device in peers:
+            link.send(value, slots.at[me], base + me, device)
+    for base, _, slots, _, peers in exchanges:
+        for index, _ in peers:
+            link.landed(slots.at[index], base + index)
 
 
 def added(slots):
@@ -456,9 +556,9 @@
     me, peers = link.plane_peers(n_row)
     examples = link.example_peers()
     link.greet([(device, None) for _, device in peers + examples])
-    meet(link, 0, value, slots, me, peers)
+    meet(link, (0, value, slots, me, peers))
     middle[...] = added(slots)
-    meet(link, 2 * n_row, middle, dp_slots, link.dp, examples)
+    meet(link, (2 * n_row, middle, dp_slots, link.dp, examples))
     total[...] = added(dp_slots)
     link.finish()
 
@@ -485,7 +585,7 @@
     value[0] = top
     value[1] = jnp.sum(sums[...] * jnp.exp(tops[...] - top[None]), 0)
     value[2] = picked[...]
-    meet(link, 0, value, slots, me, peers)
+    meet(link, (0, value, slots, me, peers))
     everyone = range(2 * n_row)
     top, total, pick = slots[0, 0], jnp.zeros_like(top), jnp.zeros_like(top)
     for k in everyone:
@@ -527,33 +627,40 @@
     return pl.cdiv(limit, BLOCK)
 
 
-def entries(shape, first=0):
-    return lax.broadcasted_iota(jnp.int32, shape, 0) + (pl.program_id(0) + first) * BLOCK
-
-
-def head_kernel(limit, table_ref, z_ref, target_ref, low_ref, exp_ref, top_ref, sum_ref, pick_ref, square_ref):
-    table = table_ref[...]
-    table = jnp.where(entries(table.shape) < limit, table, 0.0)
-    low = table.astype(BF16)
-    low_ref[...] = low
-    logits = mm_nt(low, z_ref[...])
-    entry = entries(logits.shape)
-    logits = jnp.where(entry < limit, logits, -1e30)
-    top = jnp.max(logits, 0, keepdims=True)
-    picked = jnp.sum(jnp.where(entry == target_ref[...], logits, 0.0), 0, keepdims=True)
-    exps = jnp.exp(logits - top)
-    exp_ref[...] = exps.astype(BF16)
-    top_ref[0] = top
-    sum_ref[0] = jnp.sum(exps, 0, keepdims=True)
-    square = jnp.sum(table * table, 0, keepdims=True)
-
+def entries(shape, first=0, skip=0):
+    return lax.broadcasted_iota(jnp.int32, shape, 0) + ((pl.program_id(0) + first) * BLOCK + skip)
+
+
+PARTS = 3
+PART = BLOCK // PARTS
+
+
+def parts_of():
+    return [slice(at, at + PART) for at in range(0, BLOCK, PART)]
+
+
+def head_kernel(limit, low_ref, z_ref, target_ref, exp_ref, top_ref, sum_ref, pick_ref):
     @pl.when(pl.program_id(0) == 0)
     def _():
         pick_ref[...] = jnp.zeros_like(pick_ref)
-        square_ref[...] = jnp.zeros_like(square_ref)
-
+
+    picked = jnp.zeros(pick_ref.shape, F32)
+    steps = parts_of()
+    later = mm_nt(low_ref[steps[0]], z_ref[...])
+    for k, rows in enumerate(steps):
+        logits = later
+        if k + 1 < PARTS:
+            later = mm_nt(low_ref[steps[k + 1]], z_ref[...])
+        off = jnp.where(entries((PART, 1), 0, rows.start) < limit, 0.0, -1e30)
+        logits = logits + off
+        top = jnp.max(logits, 0, keepdims=True)
+        hit = lax.broadcasted_iota(jnp.int32, logits.shape, 0) == target_ref[...] - (pl.program_id(0) * BLOCK + rows.start)
+        picked = picked + jnp.sum(jnp.where(hit, logits, 0.0), 0, keepdims=True)
+        exps = jnp.exp(logits - top)
+        exp_ref[rows] = exps.astype(BF16)
+        top_ref[k] = top
+        sum_ref[k] = jnp.sum(exps, 0, keepdims=True)
     pick_ref[...] += picked
-    square_ref[...] += square
 
 
 def whole_block(shape):
@@ -564,41 +671,39 @@
     return pl.BlockSpec((BLOCK, width), lambda i, *_: (i, 0))
 
 
-def line_block(width):
-    return pl.BlockSpec((1, 1, width), lambda i, *_: (i, 0, 0))
-
-
-def head(table, z, target):
-    limit, width = table.shape
-    length, count = z.shape[0], blocks_of(limit)
+def line_block(width, lines=1):
+    return pl.BlockSpec((lines, 1, width), lambda i, *_: (i, 0, 0))
+
+
+def head(low, limit, z, target):
+    length, width = z.shape
+    count = blocks_of(limit)
     shape = jax.ShapeDtypeStruct
+    line = shape((count * PARTS, 1, length), F32)
     return pl.pallas_call(
         functools.partial(head_kernel, limit),
         grid=(count,),
-        out_shape=[
-            shape((count * BLOCK, width), BF16),
-            shape((count * BLOCK, length), BF16),
-            shape((count, 1, length), F32),
-            shape((count, 1, length), F32),
-            shape((1, length), F32),
-            shape((1, width), F32),
-        ],
+        out_shape=[shape((count * BLOCK, length), BF16), line, line, shape((1, length), F32)],
         in_specs=[row_block(width), whole_block((length, width)), whole_block((1, length))],
-        out_specs=[row_block(width), row_block(length), line_block(length), line_block(length)]
-        + [whole_block((1, length)), whole_block((1, width))],
-        cost_estimate=cost(2 * limit * width * length, 6 * limit * width + 2 * limit * length),
+        out_specs=[row_block(length), line_block(length, PARTS), line_block(length, PARTS), whole_block((1, length))],
+        cost_estimate=cost(2 * limit * width * length, 2 * limit * width + 2 * limit * length),
         compiler_params=pltpu.CompilerParams(vmem_limit_bytes=48 * MEGA),
-    )(table, z, target)
-
-
-def head_back_kernel(exp_ref, top_ref, log_ref, target_ref, low_ref, z_ref, grad_ref, table_ref, total):
+    )(low, z, target)
+
+
+def slope_of(exps, rows, target_ref, first=0):
+    entry = lax.broadcasted_iota(jnp.int32, exps.shape, 0)
+    target = target_ref[...] - ((pl.program_id(0) + first) * BLOCK + rows.start)
+    return jnp.where(entry == target, exps - 1.0, exps).astype(BF16)
+
+
+def head_back_kernel(exp_ref, top_ref, log_ref, target_ref, low_ref, z_ref, grad_ref, table_ref, slope, total):
     at = pl.program_id(0)
-    scale = jnp.exp(top_ref[0] - log_ref[...])
-    exps = exp_ref[...].astype(F32)
-    hit = (entries(exps.shape) == target_ref[...]).astype(F32)
-    slope = (exps * scale - hit).astype(BF16)
-    table_ref[...] = mm(slope, z_ref[...]).astype(BF16)
-    part = mm_tn(low_ref[...], slope)
+    for k, rows in enumerate(parts_of()):
+        scale = jnp.exp(top_ref[k] - log_ref[...])
+        slope[rows] = slope_of(exp_ref[rows].astype(F32) * scale, rows, target_ref)
+        table_ref[rows] = mm(slope[rows], z_ref[...]).astype(BF16)
+    part = mm_tn(low_ref[...], slope[...])
 
     @pl.when(at == 0)
     def _():
@@ -619,10 +724,10 @@
         head_back_kernel,
         grid=(low.shape[0] // BLOCK,),
         out_shape=[jax.ShapeDtypeStruct((length, width), BF16), jax.ShapeDtypeStruct(low.shape, BF16)],
-        in_specs=[row_block(length), line_block(length), whole_block((1, length)), whole_block((1, length))]
+        in_specs=[row_block(length), line_block(length, PARTS), whole_block((1, length)), whole_block((1, length))]
         + [row_block(width), whole_block((length, width))],
         out_specs=[whole_block((length, width)), row_block(width)],
-        scratch_shapes=[pltpu.VMEM((width, length), F32)],
+        scratch_shapes=[pltpu.VMEM((BLOCK, length), BF16), pltpu.VMEM((width, length), F32)],
         cost_estimate=cost(4 * low.size * length, 4 * low.size + 2 * exps.size),
         compiler_params=pltpu.CompilerParams(vmem_limit_bytes=48 * MEGA),
     )(exps, tops, log_norm, target, low, z)
@@ -685,9 +790,14 @@
 
 def table_sum_kernel(first, ids_ref, order_ref, bounds_ref, share_ref, *refs):
     low_ref, z_ref, log_ref, target_ref, own_ref, grad_ref, out_ref, total = refs
-    exps = jnp.exp(mm_nt(low_ref[...], z_ref[...]) - log_ref[...])
-    hit = (entries(exps.shape, first) == target_ref[...]).astype(F32)
-    total[...] = mm((exps - hit).astype(BF16), z_ref[...])
+    steps = parts_of()
+    later = mm_nt(low_ref[steps[0]], z_ref[...])
+    for k, rows in enumerate(steps):
+        logits = later
+        if k + 1 < PARTS:
+            later = mm_nt(low_ref[steps[k + 1]], z_ref[...])
+        slope = slope_of(jnp.exp(logits - log_ref[...]), rows, target_ref, first)
+        total[rows] = mm(slope, z_ref[...])
     add_rows(total, ids_ref, order_ref, bounds_ref, grad_ref, first)
     out_ref[...] = (share_ref[0] * own_ref[...].astype(F32) + share_ref[1] * total[...]).astype(BF16)
 
@@ -767,21 +877,47 @@
 SIDE = 256
 
 
-def pack_small(pos_ex, layer_packed, small_ex):
-    tall = pos_ex.shape[0] // 4
-    pos = jnp.pad(pos_ex, ((0, 0), (0, SIDE - pos_ex.shape[1])))
-    pos = [pos[k * tall : (k + 1) * tall] for k in range(4)]
-    blank = jnp.zeros_like(pos[0])
-    pieces = [layer_packed, jnp.concatenate(pos[:3], 1), jnp.concatenate([pos[3], blank, blank], 1)]
-    pieces.append(jnp.pad(small_ex, ((0, 32 - small_ex.shape[0]), (0, 0))))
-    return jnp.concatenate(pieces, 0)
-
-
 def line_of(column):
     return jnp.broadcast_to(column, (column.shape[0], 128)).T[:1]
 
 
 BY_ROW = (False, True, True, True, False)
+
+
+def put_line(ref, at, line):
+    size = line.shape[1]
+    for k in range(0, size, 128):
+        ref[at : at + 1, : min(128, size - k)] = line[:, k : min(k + 128, size)]
+        at += 1
+    return at
+
+
+def get_line(value, at, size):
+    rows = [value[at + k : at + k + 1, : min(128, size - 128 * k)] for k in range(pl.cdiv(size, 128))]
+    return rows[0] if len(rows) == 1 else jnp.concatenate(rows, 1)
+
+
+def line_places(shapes, rows_first):
+    at, places = 0, []
+    for (rows, cols), along in zip(shapes, BY_ROW):
+        places.append(at)
+        at += pl.cdiv(rows if along == rows_first else cols, 128)
+    return places, -at // 8 * -8
+
+
+def join_kernel(one_ref, two_ref, after_ref, out_ref):
+    out_ref[...] = (one_ref[...].astype(F32) + two_ref[...].astype(F32)).astype(BF16)
+
+
+def join(one, two, after):
+    return pl.pallas_call(
+        join_kernel,
+        out_shape=jax.ShapeDtypeStruct(one.shape, BF16),
+        grid=(1,),
+        in_specs=[whole_block(one.shape), whole_block(two.shape), pl.BlockSpec(memory_space=pl.ANY)],
+        out_specs=whole_block(one.shape),
+        cost_estimate=cost(0, 6 * one.size),
+    )(one, two, after)
 
 
 def small_gradients_kernel(divisor, *refs):
@@ -815,15 +951,16 @@
 
     to_col[...] = jnp.zeros_like(to_col)
     to_row[...] = jnp.zeros_like(to_row)
-    lane = lax.broadcasted_iota(jnp.int32, (1, width), 1)
-    weight_sq = jnp.zeros((1, width), F32)
+    shapes = [item.shape for item in weights]
+    col_places, row_places = line_places(shapes, True)[0], line_places(shapes, False)[0]
+    lane = lax.broadcasted_iota(jnp.int32, (1, 128), 1)
+    weight_sq = jnp.zeros((1, 128), F32)
     for index, along in enumerate(BY_ROW):
         squares = grads[index][...] * grads[index][...]
         row_sum = line_of(jnp.sum(squares, 1, keepdims=True))
         col_sum = jnp.sum(squares, 0, keepdims=True)
-        rows_to, cols_to = (to_col, to_row) if along else (to_row, to_col)
-        rows_to[index : index + 1, : row_sum.shape[1]] = row_sum
-        cols_to[index : index + 1, : col_sum.shape[1]] = col_sum
+        put_line(to_col, col_places[index], row_sum if along else col_sum)
+        put_line(to_row, row_places[index], col_sum if along else row_sum)
         total = jnp.sum(jnp.sum(weights[index][...] * weights[index][...], 0, keepdims=True), 1, keepdims=True)
         weight_sq = weight_sq + jnp.where(lane == index, total, 0.0)
     square_ref[...] = weight_sq
@@ -842,10 +979,11 @@
 
 def small_gradients(packed, small, small_second, small_noise, weights, noises, divisor):
     width = small.shape[1]
-    wide = max(item.shape[1] for item in weights)
+    matrix_shapes = [item.shape for item in weights]
+    line_rows = [line_places(matrix_shapes, first)[1] for first in (True, False)]
     shape = lambda dims: jax.ShapeDtypeStruct(dims, F32)
     operands = [packed, small, small_second, small_noise, *weights, *noises]
-    shapes = [item.shape for item in weights] + [small.shape] * 3 + [(8, width), (8, wide), (1, width)]
+    shapes = matrix_shapes + [small.shape] * 3 + [(line_rows[0], 128), (line_rows[1], 128), (1, 128)]
     out = pl.pallas_call(
         functools.partial(small_gradients_kernel, divisor),
         grid=(1,),
@@ -862,7 +1000,7 @@
     table_over, over_cols, over_rows, old_lines = refs[:4]
     grads, (lines_ref, factor_ref), held = refs[4:9], refs[9:11], refs[11:16]
     to_level, both_slots, col_slots, row_slots, level_slots, send_sems, recv_sems, local_sems = refs[16:]
-    n_col, width = 2, table_over.shape[1]
+    n_col, width = 2, factor_ref.shape[1]
     everyone = n_row * n_col
     copies = [pltpu.make_async_copy(grads[k], held[k], local_sems.at[k]) for k in range(5)]
     for copy in copies:
@@ -871,39 +1009,41 @@
     me, peers = link.plane_peers(n_row)
     link.greet([(device, None) for _, device in peers])
     row_peers = [((link.row + k) % n_row, link.device(row=(link.row + k) % n_row)) for k in range(1, n_row)]
-    meet(link, 0, table_over, both_slots, me, peers)
-    meet(link, everyone, over_cols, col_slots, link.col, [(1 - link.col, link.device(col=1 - link.col))])
-    meet(link, everyone + n_col, over_rows, row_slots, link.row, row_peers)
+    meet(
+        link,
+        (0, table_over, both_slots, me, peers),
+        (everyone, over_cols, col_slots, link.col, [(1 - link.col, link.device(col=1 - link.col))]),
+        (everyone + n_col, over_rows, row_slots, link.row, row_peers),
+    )
     both, over_col, over_row = added(both_slots), added(col_slots), added(row_slots)
     for copy in copies:
         copy.wait()
 
     lane = lax.broadcasted_iota(jnp.int32, (1, 128), 1)
-
-    def pick(line, at):
-        return jnp.sum(jnp.where(lane == at, line[:, :128], 0.0), 1, keepdims=True)
-
-    def step_size(weight_sum, level, square_sum, entries_all):
-        size = RATE * jnp.maximum(1e-3, jnp.sqrt(weight_sum / entries_all))
-        size = size / jnp.maximum(1.0, jnp.sqrt(square_sum * level / entries_all))
-        return size * jnp.sqrt(level)
-
     whole = lambda line: jnp.sum(line, 1, keepdims=True)
-    cols_new = DECAY * table_over[5:6] + (1.0 - DECAY) * (both[0:1] / vocab + 1e-30)
-    level = pick(both[2:3], 0) / vocab
-    size = step_size(whole(both[3:4]), level, whole(both[1:2] / cols_new), float(vocab * width))
+    lines = width // 128
+    cols_new = DECAY * old_lines[5:6, :width] + (1.0 - DECAY) * (get_line(both, 0, width) / vocab + 1e-30)
+    weight_sums, table_level = both[2 * lines : 2 * lines + 1], both[2 * lines + 1 : 2 * lines + 2, :1]
+    everywhere = jnp.where(lane == 5, whole(get_line(both, lines, width) / cols_new), 0.0)
+    counts = jnp.full((1, 128), float(vocab * width), F32)
+    for index in range(5):
+        counts = jnp.where(lane == index, float(held[index].shape[0] * held[index].shape[1] * everyone), counts)
     factor_ref[...] = jnp.zeros_like(factor_ref)
     factor_ref[0:1] = cols_new
-    factor_ref[1:2] = size * lax.rsqrt(cols_new)
+    factor_ref[1:2] = lax.rsqrt(cols_new)
 
     lines_ref[...] = jnp.zeros_like(lines_ref)
-    levels = jnp.zeros((1, 128), F32)
+    shapes = [item.shape for item in held]
+    col_places, row_places = line_places(shapes, True)[0], line_places(shapes, False)[0]
+    levels = jnp.where(lane == 5, table_level / (vocab * everyone), 0.0)
+    scaled_sums = jnp.zeros((1, 128), F32)
     for index, along in enumerate(BY_ROW):
         rows, cols = held[index].shape
         parts_rows, parts_cols = (n_row, n_col) if along else (n_col, n_row)
-        rows_from, cols_from = (over_col, over_row) if along else (over_row, over_col)
-        row_mean = rows_from[index : index + 1, :rows] / (cols * parts_cols) + 1e-30
-        col_mean = cols_from[index : index + 1, :cols] / (rows * parts_rows) + 1e-30
+        by_col = get_line(over_col, col_places[index], rows if along else cols)
+        by_line = get_line(over_row, row_places[index], cols if along else rows)
+        row_mean = (by_col if along else by_line) / (cols * parts_cols) + 1e-30
+        col_mean = (by_line if along else by_col) / (rows * parts_rows) + 1e-30
         rows_line = DECAY * old_lines[index : index + 1, :rows] + (1.0 - DECAY) * row_mean
         cols_line = DECAY * old_lines[8 + index : 9 + index, :cols] + (1.0 - DECAY) * col_mean
         lines_ref[index : index + 1, :rows] = rows_line
@@ -911,22 +1051,23 @@
         level = whole(rows_line) / (rows * parts_rows * parts_cols)
         scaled = held[index][...] * held[index][...] * (1.0 / turned(rows_line, 128)[:, :1])
         scaled = whole(jnp.sum(scaled, 0, keepdims=True) / cols_line)
-        levels = levels + jnp.where(lane == 2 * index, level, 0.0) + jnp.where(lane == 2 * index + 1, scaled, 0.0)
+        levels = jnp.where(lane == index, level, levels)
+        scaled_sums = jnp.where(lane == index, scaled, scaled_sums)
     to_level[...] = jnp.zeros_like(to_level)
-    to_level[:1] = levels
-    meet(link, everyone + n_col + n_row, to_level, level_slots, me, peers)
-    levels = added(level_slots)[:1]
-    sizes = jnp.zeros((1, 128), F32)
-    for index in range(5):
-        entries_all = float(held[index].shape[0] * held[index].shape[1] * everyone)
-        size = step_size(pick(both[4:5], index), pick(levels, 2 * index), pick(levels, 2 * index + 1), entries_all)
-        sizes = sizes + jnp.where(lane == index, size, 0.0)
+    to_level[0:1] = levels
+    to_level[1:2] = scaled_sums
+    meet(link, (everyone + n_col + n_row, to_level, level_slots, me, peers))
+    levels = added(level_slots)
+    level, square_sum = levels[0:1], levels[1:2] + everywhere
+    size = RATE * jnp.maximum(1e-3, jnp.sqrt(weight_sums / counts))
+    size = size / jnp.maximum(1.0, jnp.sqrt(square_sum * level / counts))
+    sizes = size * jnp.sqrt(level)
     factor_ref[2:3, :128] = sizes
     link.finish()
 
 
-def statistics(table_over, over_cols, over_rows, old_lines, grads, n_row, vocab, collective_id):
-    width, wide = table_over.shape[1], over_rows.shape[1]
+def statistics(table_over, over_cols, over_rows, old_lines, grads, width, n_row, vocab, collective_id):
+    wide = old_lines.shape[1]
     everyone = 2 * n_row
     vmem, hbm = pl.BlockSpec(memory_space=pltpu.VMEM), pl.BlockSpec(memory_space=pl.ANY)
     return pl.pallas_call(
@@ -935,8 +1076,9 @@
         in_specs=[vmem] * 4 + [hbm] * 5,
         out_specs=[vmem] * 2,
         scratch_shapes=[pltpu.VMEM(item.shape, F32) for item in grads]
-        + [pltpu.VMEM((8, 128), F32), pltpu.VMEM((everyone, 8, width), F32), pltpu.VMEM((2, 8, width), F32)]
-        + [pltpu.VMEM((n_row, 8, wide), F32), pltpu.VMEM((everyone, 8, 128), F32)]
+        + [pltpu.VMEM((8, 128), F32), pltpu.VMEM((everyone,) + table_over.shape, F32)]
+        + [pltpu.VMEM((2,) + over_cols.shape, F32), pltpu.VMEM((n_row,) + over_rows.shape, F32)]
+        + [pltpu.VMEM((everyone, 8, 128), F32)]
         + [pltpu.SemaphoreType.DMA((3 * everyone,)), pltpu.SemaphoreType.DMA((2 * everyone + 2 + n_row,))]
         + [pltpu.SemaphoreType.DMA((5,))],
         compiler_params=pltpu.CompilerParams(
@@ -949,17 +1091,17 @@
     weights, grads, (table_new_ref, table_cols_ref) = refs[:5], refs[5:10], refs[10:12]
     rows_outs, cols_outs, news = refs[12:17], refs[17:22], refs[22:27]
     rows = turned(lax.rsqrt(rows_ref[0]), 128)[:, :1]
-    table_new_ref[...] = table_ref[...] - table_grad_ref[...] * rows * factor_ref[1:2]
+    table_new_ref[...] = table_ref[...] - table_grad_ref[...] * rows * (factor_ref[1:2] * factor_ref[2:3, 5:6])
 
     @pl.when(pl.program_id(0) == 0)
     def _():
-        table_cols_ref[...] = factor_ref[0:1]
+        table_cols_ref[...] = factor_ref[0:1].reshape(table_cols_ref.shape)
         for index in range(5):
             count_rows, count_cols = weights[index].shape
             rows_line = lines_ref[index : index + 1, :count_rows]
             cols_line = lines_ref[8 + index : 9 + index, :count_cols]
-            rows_outs[index][...] = rows_line
-            cols_outs[index][...] = cols_line
+            rows_outs[index][...] = rows_line.reshape(count_rows)
+            cols_outs[index][...] = cols_line.reshape(count_cols)
             rows = turned(lax.rsqrt(rows_line), 128)[:, :1]
             factors = factor_ref[2:3, index : index + 1] * lax.rsqrt(cols_line)
             news[index][...] = weights[index][...] - grads[index][...] * rows * factors
@@ -968,7 +1110,7 @@
 def update(table, table_grad, table_rows, factors, lines, weights, grads):
     limit, width = table.shape
     shape = lambda dims: jax.ShapeDtypeStruct(dims, F32)
-    small_shapes = [(1, width)] + [(1, item.shape[0]) for item in weights] + [(1, item.shape[1]) for item in weights]
+    small_shapes = [(width,)] + [item.shape[:1] for item in weights] + [item.shape[1:] for item in weights]
     small_shapes += [item.shape for item in weights]
     out = pl.pallas_call(
         update_kernel,
@@ -981,8 +1123,7 @@
         compiler_params=pltpu.CompilerParams(vmem_limit_bytes=56 * MEGA),
         cost_estimate=cost(0, 3 * 4 * limit * width),
     )(table, table_grad, table_rows, factors, lines, *weights, *grads)
-    flat = lambda items: [item[0] for item in items]
-    return out[0], out[1][0], flat(out[2:7]), flat(out[7:12]), out[12:]
+    return out[0], out[1], out[2:7], out[7:12], out[12:]
 
 
 HIDDEN = 1024
@@ -1172,7 +1313,8 @@
 
 
 def weight_grads_kernel(place_ref, ones_ref, mixed_ref, low_ref, *refs):
-    packed, (branch_ref, pre_ref, down_ref, act_ref), (out_ref, square_ref, wide) = refs[:3], refs[3:7], refs[7:]
+    packed, (branch_ref, pre_ref, down_ref, act_ref, grad_ref, small_ref) = refs[:3], refs[3:9]
+    out_ref, square_ref, wide = refs[9:]
     width = ones_ref.shape[1]
     tall = width // 4
     start = pl.multiple_of(place_ref[0], 128)
@@ -1193,21 +1335,34 @@
             out_ref[piece * tall : (piece + 1) * tall, side * half : (side + 1) * half] = grad
             square = square + jnp.sum(grad * grad, 0, keepdims=True)
     left = down_ref[...].T
+    first = 4 * tall
     for side in range(2):
         grad = mm(left, act_ref[:, side * half : (side + 1) * half])
-        out_ref[4 * tall :, side * half : (side + 1) * half] = grad
+        out_ref[first : first + half, side * half : (side + 1) * half] = grad
         square = square + jnp.sum(grad * grad, 0, keepdims=True)
     square_ref[...] = square
-
-
-def weight_grads(ln_one, mixed, low, packed_grad, branch, pre, down_grad, act, row_at, col_at):
+    first += half
+    tall = grad_ref.shape[0] // 4
+    lines = out_ref.shape[0] - first
+    out_ref[first:, :] = jnp.zeros((lines, width), F32)
+    for k in range(4):
+        rows = slice(first + tall * (k // 3), first + tall * (k // 3) + tall)
+        part = grad_ref[k * tall : (k + 1) * tall, pl.ds(start, SIDE)]
+        out_ref[rows, SIDE * (k % 3) : SIDE * (k % 3 + 1)] = jnp.where(skip > 0, pltpu.roll(part, SIDE - width // 12, 1), part)
+    first += 2 * tall
+    out_ref[first : first + small_ref.shape[0], :] = small_ref[...]
+
+
+def weight_grads(ln_one, mixed, low, packed_grad, branch, pre, down_grad, act, grad_in, small_ex, row_at, col_at):
     length, width = ln_one.shape
     half, tall = width // 2, width // 4
-    hidden = pre.shape[1] // 2
+    hidden, tokens = pre.shape[1] // 2, length // 2
     shape = jax.ShapeDtypeStruct
     first = row_at * tall
     place = jnp.stack([first // 128 * 128, first % 128, row_at, col_at]).astype(jnp.int32)
     unit = lambda k: pl.BlockSpec((1, length, half), lambda i, at: ((3 * at[3] + k) // 2, 0, (3 * at[3] + k) % 2))
+    by_col = lambda size: pl.BlockSpec((length, size), lambda i, at: (0, at[3]))
+    lines = 4 * tall + half + tokens // 2 + 32
     return pl.pallas_call(
         weight_grads_kernel,
         grid_spec=pltpu.PrefetchScalarGridSpec(
@@ -1215,15 +1370,15 @@
             grid=(1,),
             in_specs=[whole_block((length, width))] * 3
             + [unit(k) for k in range(3)]
-            + [pl.BlockSpec((length, half), lambda i, at: (0, at[3])), pl.BlockSpec((length, hidden), lambda i, at: (0, at[3]))]
-            + [pl.BlockSpec((length, half), lambda i, at: (0, at[3])), pl.BlockSpec((length, width), lambda i, at: (0, at[2]))],
-            out_specs=[whole_block((4 * tall + half, width)), whole_block((1, half))],
+            + [by_col(half), by_col(hidden), by_col(half), pl.BlockSpec((length, width), lambda i, at: (0, at[2]))]
+            + [pl.BlockSpec((tokens, width), lambda i, at: (at[3], 0)), whole_block(small_ex.shape)],
+            out_specs=[whole_block((lines, width)), whole_block((1, half))],
             scratch_shapes=[pltpu.VMEM((SIDE, half), F32)],
         ),
-        out_shape=[shape((4 * tall + half, width), F32), shape((1, half), F32)],
+        out_shape=[shape((lines, width), F32), shape((1, half), F32)],
         cost_estimate=cost(2 * length * width * width * 2, 16 * length * width),
         compiler_params=pltpu.CompilerParams(vmem_limit_bytes=56 * MEGA),
-    )(place, ln_one, mixed, low, packed_grad, packed_grad, packed_grad, branch, pre, down_grad, act)
+    )(place, ln_one, mixed, low, packed_grad, packed_grad, packed_grad, branch, pre, down_grad, act, grad_in, small_ex)
 
 
 def body(
@@ -1285,29 +1440,22 @@
     weights_in = [tok_table, pos_table, qkv_weight, attn_weight, up_weight, down_weight]
     noises = [table_noise, pos_noise, qkv_noise, attn_noise, up_noise, down_noise]
     lows = [item.astype(BF16) for item in weights_in[2:]]
-    local_ids = ids - vocab_start
-    inside = (local_ids >= 0) & (local_ids < vocab_here)
-    safe_ids = jnp.clip(local_ids, 0, vocab_here - 1)
-    looked = jnp.where(inside[:, None], jnp.take(tok_table, safe_ids, axis=0), 0.0).astype(BF16)
     if tuned:
-        pos_blocks = pos_table.reshape(n_row, block, -1)
-        pieces = []
-        for k in range(n_row):
-            piece = lax.dynamic_index_in_dim(pos_blocks, row_at ^ k, 0, False)
-            if k:
-                piece = lax.ppermute(piece, "row", [(at, at ^ k) for at in range(n_row)])
-            pieces.append(piece)
-        pieces = jnp.stack(pieces)
-        pos_own = jnp.concatenate([pieces[row_at ^ at] for at in range(n_row)], 1)
         shards = [item.reshape(n_data, -1, item.shape[1]) for item in lows]
-        start, own_rows, qkv_full, attn_full, up_full, down_full = front(
-            looked.reshape(n_col, n_row, block, width), pos_own, shards, n_row
+        start, table_low, table_sq, qkv_full, attn_full, up_full, down_full = front(
+            ids, tok_table, pos_table, shards, n_row
         )
         stream_in = start.reshape(length, width)
         qkv_full, attn_full, up_full, down_full = (
             item.reshape(width, -1) for item in (qkv_full, attn_full, up_full, down_full)
         )
     else:
+        local_ids = ids - vocab_start
+        inside = (local_ids >= 0) & (local_ids < vocab_here)
+        safe_ids = jnp.clip(local_ids, 0, vocab_here - 1)
+        looked = jnp.where(inside[:, None], jnp.take(tok_table, safe_ids, axis=0), 0.0).astype(BF16)
+        table_sq = jnp.sum(tok_table * tok_table, 0, keepdims=True)
+        table_low = jnp.pad(tok_table.astype(BF16), ((0, blocks_of(vocab_here) * BLOCK - vocab_here), (0, 0)))
         stream_in = (plane_sum(looked).astype(F32) + gather_matrix(pos_table, 1)).astype(BF16)
         qkv_full, attn_full, up_full = (gather_matrix(item, 0) for item in lows[:3])
         down_full = gather_matrix(lows[3], 1)
@@ -1321,7 +1469,7 @@
         stream_in, mixed, attn_full, up_full, up_bias, down_full, small
     )
 
-    table_low, exps, tops, exp_sums, picked, table_sq = head(tok_table, ln_fin, target)
+    exps, tops, exp_sums, picked = head(table_low, vocab_here, ln_fin, target)
     if tuned:
         met_z = beside(ln_fin)
         log_norm, picked = log_total(tops, exp_sums, picked, n_row, 3)
@@ -1343,13 +1491,29 @@
     )
     packed_grad = attend_back(packed, mixed_grad, attn_log)
     grad_in, emb_low, emb_grad, start_rows = start_back(packed_grad, qkv_full, mid_grad, stream_in, small)
+    small_ex = jnp.concatenate(
+        [start_rows[:4], mid_rows[5:6], mid_rows[3:5], pre_sum.reshape(-1, width), mid_rows[2:3], mid_rows[:2]], 0
+    )
     if tuned:
         met_grad = beside(emb_low)
-        layer_packed, layer_sq = weight_grads(
-            ln_one, mixed, ln_two, packed_grad, branch_grad, pre_grad, down_grad, up_act, row_at, col_at
+        packed_ex, layer_sq = weight_grads(
+            ln_one,
+            mixed,
+            ln_two,
+            packed_grad,
+            branch_grad,
+            pre_grad,
+            down_grad,
+            up_act,
+            grad_in,
+            small_ex,
+            row_at,
+            col_at,
         )
         layer_sq = jnp.sum(layer_sq)
     else:
+        tok_here, dim_here = pos_table.shape
+        pos_ex = lax.dynamic_slice(grad_in, (col_at * tok_here, row_at * dim_here), (tok_here, dim_here))
         all_grads = packed_grad.transpose(1, 0, 2).reshape(length, -1)
 
         def columns_of(array, at, parts):
@@ -1366,11 +1530,6 @@
             )
         ]
         layer_sq = sum(jnp.sum(item * item) for item in layer_ex)
-    tok_here, dim_here = pos_table.shape
-    pos_ex = lax.dynamic_slice(grad_in, (col_at * tok_here, row_at * dim_here), (tok_here, dim_here))
-    small_ex = jnp.concatenate(
-        [start_rows[:4], mid_rows[5:6], mid_rows[3:5], pre_sum.reshape(-1, width), mid_rows[2:3], mid_rows[:2]], 0
-    )
     table_ex, own_sq = add_own_rows(table_ex, lists, emb_grad)
 
     own_sq = jnp.sum(own_sq) + layer_sq
@@ -1401,16 +1560,11 @@
     if tuned:
         core = ex_at % 2
         to_core = lambda item: lax.ppermute(item, "dp", [(at, at ^ 1) for at in range(4)])
-        halves = (own_share * pack_small(pos_ex, layer_packed, small_ex)).astype(BF16).reshape(2, -1, width)
+        halves = (own_share * packed_ex).astype(BF16).reshape(2, -1, width)
         half = (halves[core].astype(F32) + to_core(halves[1 - core]).astype(F32)).astype(BF16)
         shares = jnp.stack([own_share, share[ex_at ^ 2]])
         half, shares = lax.optimization_barrier((half, shares))
-        half = (half.astype(F32) + beside(half).astype(F32)).astype(BF16)
-        other_half = to_core(half)
-        packed = jnp.concatenate(
-            [jnp.where(core == 0, half, other_half), jnp.where(core == 0, other_half, half)], 0
-        )
-
+        from_beside = beside(half)
         middle = count // 2
         spans = [(0, middle), (middle, count - middle)]
         met = (met_z, met_log, met_target, met_lists, met_grad.astype(F32), shares)
@@ -1421,19 +1575,25 @@
             into, *more = table_gradient(pair, table_noise, table_old, divisor, *span, into)
             over.append(more)
         table_grad = into
+        half = join(half, from_beside, over[1][1])
+        other_half = to_core(half)
+        packed = jnp.concatenate(
+            [jnp.where(core == 0, half, other_half), jnp.where(core == 0, other_half, half)], 0
+        )
         rows_blocks = jnp.concatenate([item[0] for item in over], 0)
         cols, scaled, level = (over[0][k] + over[1][k] for k in (1, 2, 3))
-        level = jnp.pad(level[:, :1], ((0, 0), (0, width - 1)))
         small_grads, smalls, (over_cols, over_rows, squares) = small_gradients(
             packed, small_params, small_second, small_noise, weights_in[1:], noises[1:], divisor
         )
-        table_over = jnp.concatenate(
-            [cols, scaled, level, table_sq, squares, table_cols[None], jnp.zeros((2, width), F32)], 0
+        scalars = jnp.where(jnp.arange(128) == 5, jnp.sum(table_sq), squares[0])
+        table_over = jnp.concatenate([cols[0], scaled[0], scalars, level[0]]).reshape(-1, 128)
+        table_over = jnp.pad(table_over, ((0, -table_over.shape[0] % 8), (0, 0)))
+        wide = max(item.shape[0] for pair in olds for item in pair)
+        lines = [jnp.pad(item, (0, wide - item.shape[0])) for pair in zip(*olds) for item in pair + (table_cols,) * 3]
+        old_lines = jnp.stack(lines)
+        lines, factors = statistics(
+            table_over, over_cols, over_rows, old_lines, small_grads, width, n_row, vocab, 5
         )
-        wide = over_rows.shape[1]
-        lines = [jnp.pad(item, (0, wide - item.shape[0])) for pair in zip(*olds) for item in pair + (pair[0],) * 3]
-        old_lines = jnp.stack(lines)
-        lines, factors = statistics(table_over, over_cols, over_rows, old_lines, small_grads, n_row, vocab, 5)
         table_new, table_cols_new, rows_new, cols_new, news = update(
             tok_table, table_grad, rows_blocks, factors, lines, weights_in[1:], small_grads
         )

time: 641 us -> 559 us (0.87)
  waiting for transfers between devices: 25.2 us -> 0.02 us
  Pallas kernels: 481 us -> 460 us
  local copies, waits for them, and re-layouts: 49.4 us -> 35.4 us
  other arithmetic: 50.2 us -> 36.6 us
    ppermute x5, waiting for transfers between devices: 25.2 us -> 0.01 us  [body(): lax.ppermute(item, 'dp', [(at, at ^ 2) for at in range(4)])]
    gather x1 -> x0, local copies, waits for them, and re-layouts: 12.1 us -> none  [body(): jnp.take(tok_table, safe_ids, axis=0)]
    convert_element_type x3 -> x1, other arithmetic: 11.4 us -> 3.24 us  [body(): halves = (own_share * packed_ex).astype(BF16).reshape(2, -1, width)]
    pallas_call x6 -> x0, other arithmetic: 7.71 us -> none  [update(): pl.pallas_call(update_kernel, grid=(blocks_of(limit),), out_shape=[shape(...]
    pallas_call x1 -> x2, Pallas kernels: 99.6 us -> 107 us  [the longest x1 104 us: front(): pl.pallas_call(functools.partial(front_kernel, n_row), out_shape=[shape((...]
    pallas_call x1, Pallas kernels: 34.9 us -> 27.7 us  [attend_back(): pl.pallas_call(attend_back_kernel, grid=(pairs,), out_shape=jax.ShapeDtyp...]
    pallas_call x1, Pallas kernels: 22 us -> 14.9 us  [attend(): pl.pallas_call(attend_kernel, grid=(pairs,), out_shape=[jax.ShapeDtypeStr...]
    pallas_call x1, Pallas kernels: 23.6 us -> 17 us  [statistics(): pl.pallas_call(functools.partial(statistics_kernel, n_row, vocab), out_sh...]
  transfers between devices with their start and end apart: 12 -> 9, of which waited for: 1 -> 0; matrix products, arithmetic and copies ran while one was open for 10% -> 8% of each run, Pallas kernels for 41% -> 71%
where the time goes in v3:
time: 559 us; the launch traced here: 553 us
  Pallas kernels  460 us (82%)
  other arithmetic  36.6 us (7%)
  local copies, waits for them, and re-layouts  35.4 us (6%)
  between operations  9.68 us (2%)
  starting transfers between devices  7.56 us (1%)
    pallas_call x1, Pallas kernels, front(): pl.pallas_call(functools.partial(front_kernel, n_row), out_shape=[shape((...  104 us
    pallas_call x1, Pallas kernels, plane_total(): pl.pallas_call(functools.partial(total_kernel, n_row), out_shape=jax.Shap...  50.6 us
    pallas_call x2, Pallas kernels, table_sum(): pl.pallas_call(functools.partial(table_sum_kernel, first), grid_spec=pltp...  33.3 us
    pallas_call x1, Pallas kernels, middle_back(): pl.pallas_call(middle_back_kernel, grid=(hidden // HIDDEN,), out_shape=[s...  33.3 us
    unnamed x135, local copies, waits for them, and re-layouts  30 us
    pallas_call x1, Pallas kernels, head_back(): pl.pallas_call(head_back_kernel, grid=(low.shape[0] // BLOCK,), out_shape...  28.8 us
    pallas_call x1, Pallas kernels, attend_back(): pl.pallas_call(attend_back_kernel, grid=(pairs,), out_shape=jax.ShapeDtyp...  27.7 us
    pallas_call x2, Pallas kernels, table_gradient(): pl.pallas_call(functools.partial(gradient_kernel, limit, len(sums), divis...  25.7 us
  transfers between devices with their start and end apart: 9, of which 0 were waited for; matrix products, arithmetic and copies ran while one was open for 8% of the time, Pallas kernels for 71%

profile of v3, /device:TPU:0, one launch (start us, length us, event | category | flops | bytes accessed | tf_op | source)
XLA Modules:
  0.0 553.3 jit_solution(8895381218492027179)
XLA Ops:
  1.6 3.0 collective-permute-start
  12.8 104.4 %shard_map.517 = (bf16[2,4,128,768]{3,2,1,0:T(8,128)(2,1)}, bf16[6336,768]{1,0:T(8,128)(2,1)}, f32[1,768]{1,0:T(1,128)}, bf16[4,2,2,48,2304]{4,3,2,1,0:T(8,128)(...) custom-call(s32[1024]{0:T(1024)} %bitcast.69, ...), custom_call_target="tpu_custom_call" | custom-call | tf_op jit(solution)/shard_map/pallas_call | solution.py:361
  121.4 4.3 add_convert_fusion.q_ref.k_ref.v_ref
  125.7 14.9 %shard_map.518 = (bf16[1024,768]{1,0:T(8,128)(2,1)S(1)}, f32[6,2,1024]{2,1,0:T(2,128)S(1)}) custom-call(bf16[1024,2304]{1,0:T(8,128)(2,1)S(1)} %add_convert_fusion.q_ref.k_ref.v_ref, bf16[1024,2304]{1,0:T(8,128)(2,1)S(1)} %add_convert_fusion.q_ref.k_ref.v_ref, bf16[1024,2304]{1,0:T(8,128)(2,1)S(1)} %add_convert_fusion.q_ref.k_ref.v_ref), custom_call_target="tpu_custom_call" | custom-call | flops 16106127360 | bytes 6291456 | tf_op jit(solution)/shard_map/pallas_call | solution.py:468
  142.4 20.9 %shard_map.519 = (f32[1024,768]{1,0:T(8,128)}, bf16[1024,768]{1,0:T(8,128)(2,1)}, f32[1024,768]{1,0:T(8,128)}, bf16[1024,768]{1,0:T(8,128)(2,1)}) custom-call(bf16[1024,768]{1,0:T(8,128)(2,1)} %bitcast.51, bf16[1024,768]{1,0:T(8,128)(2,1)} %copy-done.15, bf16[768,768]{1,0:T(8,128)(2,1)} %bitcast.88, bf16[768,3072]{1,0:T(8,128)(2,1)} %bitcast.82, ...), custom_call_target="tpu_custom_call" | custom-call | flops 9663676416 | bytes 12582912 | tf_op jit(solution)/shard_map/pallas_call | solution.py:1196
  166.3 18.8 %shard_map.520 = (bf16[6336,1024]{1,0:T(8,128)(2,1)}, f32[18,1,1024]{2,1,0:T(1,128)S(1)}, f32[18,1,1024]{2,1,0:T(1,128)S(1)}, f32[1,1024]{1,0:T(1,128)S(1)}) custom-call(bf16[6336,768]{1,0:T(8,128)(2,1)} %get-tuple-element.111.low_ref.refs_0_, bf16[1024,768]{1,0:T(8,128)(2,1)S(1)} %copy-done.33, s32[1,1024]{1,0:T(1,128)S(1)} %and_select_fusion.1.target_ref), custom_call_target="tpu_custom_call" | custom-call | flops 9890168832 | bytes 22536192 | tf_op jit(solution)/shard_map/pallas_call | solution.py:683
  187.0 8.7 %shard_map.521 = (f32[8,128]{1,0:T(8,128)}, f32[8,128]{1,0:T(8,128)}) custom-call(f32[18,8,128]{2,1,0:T(8,128)} %bitcast.55, f32[18,8,128]{2,1,0:T(8,128)} %bitcast.56, f32[8,128]{1,0:T(8,128)} %bitcast.57), custom_call_target="tpu_custom_call" | custom-call | tf_op jit(solution)/shard_map/pallas_call | solution.py:606
  197.2 28.8 %shard_map.522 = (bf16[1024,768]{1,0:T(8,128)(2,1)S(1)}, bf16[6336,768]{1,0:T(8,128)(2,1)}) custom-call(bf16[6336,1024]{1,0:T(8,128)(2,1)} %get-tuple-element.119.exp_ref, f32[18,1,1024]{2,1,0:T(1,128)S(1)} %copy-done.23, f32[1,1024]{1,0:T(1,128)S(1)} %bitcast.58, s32[1,1024]{1,0:T(1,128)S(1)} %and_select_fusion.1.target_ref, ...), custom_call_target="tpu_custom_call" | custom-call | flops 19931332608 | bytes 32440320 | tf_op jit(solution)/shard_map/pallas_call | solution.py:723
  226.1 50.6 %shard_map.523 = bf16[2,4,128,768]{3,2,1,0:T(8,128)(2,1)S(1)} custom-call(bf16[2,4,128,768]{3,2,1,0:T(8,128)(2,1)S(1)} %bitcast.54), custom_call_target="tpu_custom_call" | custom-call | tf_op jit(solution)/shard_map/pallas_call | solution.py:404
  277.9 33.3 %shard_map.524 = (bf16[1024,768]{1,0:T(8,128)(2,1)}, bf16[1024,3072]{1,0:T(8,128)(2,1)}, bf16[1024,3072]{1,0:T(8,128)(2,1)}, f32[1,3072]{1,0:T(1,128)}, f32[1024...) custom-call(bf16[1024,768]{1,0:T(8,128)(2,1)} %bitcast.53, ...), custom_call_target="tpu_custom_call" | custom-call | flops 14495514624 | bytes 31457280 | tf_op jit(solution)/shard_map/pallas_call | solution.py:1265
  312.7 27.7 %shard_map.525.packed_ref.refs_0_.refs_1_.refs_2_ = bf16[3,1024,768]{2,1,0:T(8,128)(2,1)} custom-call(bf16[1024,2304]{1,0:T(8,128)(2,1)} %copy-done.36, bf16[1024,2304]{1,0:T(8,128)(2,1)} %copy-done.36, bf16[1024,2304]{1,0:T(8,128)(2,1)} %copy-done.36, bf16[1024,768]{1,0:T(8,128)(2,1)S(1)} %copy-done.37, f32[6,2,1024]{2,1,0:T(2,128)S(1)} %get-tuple-element.130.log_ref), custom_call_target="tpu_custom_call" | custom-call | flops 24159191040 | bytes 12582912 | tf_op jit(solution)/shard_map/pallas_call | solution.py:524
  340.4 9.8 %shard_map.526 = (f32[1024,768]{1,0:T(8,128)S(1)}, bf16[1024,768]{1,0:T(8,128)(2,1)}, f32[1024,768]{1,0:T(8,128)S(1)}, f32[8,768]{1,0:T(8,128)S(1)}) custom-call(bf16[3,1024,768]{2,1,0:T(8,128)(2,1)} %shard_map.525.packed_ref.refs_0_.refs_1_.refs_2_, bf16[768,2304]{1,0:T(8,128)(2,1)} %bitcast.86, f32[1024,768]{1,0:T(8,128)S(1)} %copy-done.35, ...), custom_call_target="tpu_custom_call" | custom-call | flops 3623878656 | bytes 15728640 | tf_op jit(solution)/shard_map/pallas_call | solution.py:1303
  362.8 11.4 %shard_map.528 = (f32[1440,768]{1,0:T(8,128)}, f32[1,384]{1,0:T(1,128)}) custom-call(s32[4]{0:T(128)} %pad_add_fusion.1.place_ref, bf16[1024,768]{1,0:T(8,128)(2,1)} %add_convert_fusion.1.ones_ref, bf16[1024,768]{1,0:T(8,128)(2,1)} %copy-done.15, bf16[1024,768]{1,0:T(8,128)(2,1)} %get-tuple-element.128.refs_3_.low_ref, ...), custom_call_target="tpu_custom_call" | custom-call | flops 2415919104 | bytes 12582912 | tf_op jit(solution)/shard_map/pallas_call | solution.py:1366
  378.9 11.3 %shard_map.527 = (bf16[6336,768]{1,0:T(8,128)(2,1)}, f32[1,768]{1,0:T(1,128)}) custom-call(s32[1024]{0:T(1024)} %broadcast_subtract_fusion.ids_ref, s32[1024]{0:T(1024)} %get-tuple-element.258.order_ref, s32[7]{0:T(128)} %get-tuple-element.262.bounds_ref, bf16[6336,768]{1,0:T(8,128)(2,1)} %get-tuple-element.124.table_ref, f32[1024,768]{1,0:T(8,128)} %copy-done.11), custom_call_target="tpu_custom_call" | custom-call | bytes 19464192 | tf_op jit(solution)/shard_map/pallas_call | solution.py:776
  393.5 11.6 %shard_map.529 = f32[8,128]{1,0:T(8,128)} custom-call(f32[8,128]{1,0:T(8,128)} %fusion.10.value), custom_call_target="tpu_custom_call" | custom-call | tf_op jit(solution)/shard_map/pallas_call | solution.py:568
  407.1 3.2 multiply_convert_fusion
  418.8 16.5 %shard_map.531.refs_0_ = bf16[3168,768]{1,0:T(8,128)(2,1)} custom-call(s32[1024]{0:T(1024)S(1)} %broadcast_subtract_fusion.1.ids_ref, s32[1024]{0:T(1024)S(1)} %get-tuple-element.260.order_ref, s32[7]{0:T(128)S(1)} %get-tuple-element.263.bounds_ref, f32[2]{0:T(128)S(1)} %pad_maximum_fusion.2.share_ref, bf16[6336,768]{1,0:T(8,128)(2,1)} %get-tuple-element.111.low_ref.refs_0_, ...), custom_call_target="tpu_custom_call" | custom-call | flops 9965666304 | bytes 14598144 | tf_op jit(solution)/shard_map/pallas_call | solution.py:808
  435.5 16.9 %shard_map.530.refs_0_ = bf16[3168,768]{1,0:T(8,128)(2,1)} custom-call(s32[1024]{0:T(1024)S(1)} %broadcast_subtract_fusion.1.ids_ref, s32[1024]{0:T(1024)S(1)} %get-tuple-element.260.order_ref, s32[7]{0:T(128)S(1)} %get-tuple-element.263.bounds_ref, f32[2]{0:T(128)S(1)} %pad_maximum_fusion.2.share_ref, bf16[6336,768]{1,0:T(8,128)(2,1)} %get-tuple-element.111.low_ref.refs_0_, ...), custom_call_target="tpu_custom_call" | custom-call | flops 9965666304 | bytes 14598144 | tf_op jit(solution)/shard_map/pallas_call | solution.py:808
  456.4 12.9 %shard_map.532 = (f32[6288,768]{1,0:T(8,128)}, f32[3,1,1056]{2,1,0:T(1,128)S(1)}, f32[1,768]{1,0:T(1,128)S(1)}, f32[1,768]{1,0:T(1,128)S(1)}, f32[1,128]{1,0:T(1,128)S(1)}) custom-call(bf16[3168,768]{1,0:T(8,128)(2,1)S(1)} %copy-done.6, bf16[3168,768]{1,0:T(8,128)(2,1)} %collective-permute-done.6.refs_1_, f32[6288,768]{1,0:T(8,128)} %refs_2_.5, ...), custom_call_target="tpu_custom_call" | custom-call | bytes 29196288 | tf_op jit(solution)/shard_map/pallas_call | solution.py:860
  469.4 12.7 %shard_map.533 = (f32[6288,768]{1,0:T(8,128)}, f32[3,1,1056]{2,1,0:T(1,128)S(1)}, f32[1,768]{1,0:T(1,128)S(1)}, f32[1,768]{1,0:T(1,128)S(1)}, f32[1,128]{1,0:T(1,128)S(1)}) custom-call(bf16[3168,768]{1,0:T(8,128)(2,1)S(1)} %copy-done.5, bf16[3168,768]{1,0:T(8,128)(2,1)} %collective-permute-done.5.refs_1_, ...), custom_call_target="tpu_custom_call", output_to_operand_aliasing={{0}: (4, {})} | custom-call | bytes 29196288 | tf_op jit(solution)/shard_map/pallas_call | solution.py:860
  482.8 2.9 shard_map.534
  495.5 5.2 shard_map.535
  507.0 17.0 %shard_map.536 = (f32[16,1536]{1,0:T(8,128)S(1)}, f32[8,768]{1,0:T(8,128)S(1)}) custom-call(f32[16,128]{1,0:T(8,128)S(1)} %pad.54.refs_0_, f32[16,128]{1,0:T(8,128)S(1)} %get-tuple-element.163.refs_1_, f32[32,128]{1,0:T(8,128)S(1)} %get-tuple-element.164.refs_2_, f32[16,1536]{1,0:T(8,128)S(1)} %stack.80.refs_3_, ...), custom_call_target="tpu_custom_call" | custom-call | tf_op jit(solution)/shard_map/pallas_call | solution.py:1073
  525.2 23.3 %shard_map.537 = (f32[6288,768]{1,0:T(8,128)}, f32[768]{0:T(1024)}, f32[512]{0:T(512)}, f32[192]{0:T(256)}, f32[192]{0:T(256)}, /*index=5*/f32[192]{0:T(256)}, f...) custom-call(f32[6288,768]{1,0:T(8,128)} %table_ref.1, ...), custom_call_target="tpu_custom_call" | custom-call | bytes 57950208 | tf_op jit(solution)/shard_map/pallas_call | solution.py:1115
  (234 shorter events, 73.3 us)
Async XLA Ops:
  1.6 376.6 %collective-permute-start = (s32[2,1024]{1,0:T(2,128)S(1)}, s32[2,1024]{1,0:T(2,128)S(1)}, u32[]{:S(2)}, u32[]{:S(2)}) collective-permute-start(s32[2,1024]{1,0:T(2,128)S(1)} %pad_add_fusion), channel_id=1, source_target_pairs={{0,16},{8,24},{16,0},{24,8},{1,17},{9,25},{17,1},{25,9},{2,18},{10... | collective-permute-start | bytes 24584 | tf_op jit(solution)/shard_map/ppermute | solution.py:1434
  125.7 15.0 %copy-start.36 = (bf16[1024,2304]{1,0:T(8,128)(2,1)}, bf16[1024,2304]{1,0:T(8,128)(2,1)S(1)}, u32[]{:S(2)}) copy-start(bf16[1024,2304]{1,0:T(8,128)(2,1)S(1)} %add_convert_fusion.q_ref.k_ref.v_ref) | copy-start | bytes 14155780
  142.4 22.5 %copy-start.47 = (s32[1,1024]{1,0:T(1,128)S(1)}, s32[1,1024]{1,0:T(1,128)}, u32[]{:S(2)}) copy-start(s32[1,1024]{1,0:T(1,128)} %param.31) | copy-start | bytes 12292
  163.3 255.5 %collective-permute-start.3 = (bf16[1024,768]{1,0:T(8,128)(2,1)}, bf16[1024,768]{1,0:T(8,128)(2,1)S(1)}, u32[]{:S(2)}, u32[]{:S(2)}) collective-permute-start(bf16[1024,768]{1,0:T(8,128)(2,1)} %get-tuple-element.118.z_ref), channel_id=1, source_target_pairs={{0,16},{8,24},{16,0},{24,8},{1,17},{9,25},{17,1},{25,9},{2,18},{10... | collective-permute-start | bytes 4718600 | tf_op jit(solution)/shard_map/ppermute | solution.py:1434
  166.3 29.4 %copy-start.34 = (bf16[1024,768]{1,0:T(8,128)(2,1)S(1)}, bf16[1024,768]{1,0:T(8,128)(2,1)}, u32[]{:S(2)}) copy-start(bf16[1024,768]{1,0:T(8,128)(2,1)} %get-tuple-element.118.z_ref) | copy-start | bytes 4718596
  312.7 27.7 %copy-start = (bf16[2,4,128,768]{3,2,1,0:T(8,128)(2,1)S(1)}, bf16[2,4,128,768]{3,2,1,0:T(8,128)(2,1)}, u32[]{:S(2)}) copy-start(bf16[2,4,128,768]{3,2,1,0:T(8,128)(2,1)} %get-tuple-element.112) | copy-start | bytes 4718596
  312.7 27.7 %copy-start.20 = (f32[14,768]{1,0:T(8,128)S(1)}, f32[14,768]{1,0:T(8,128)}, u32[]{:S(2)}) copy-start(f32[14,768]{1,0:T(8,128)} %refs_1_.2) | copy-start | bytes 129028
  312.7 27.7 %copy-start.35 = (f32[1024,768]{1,0:T(8,128)S(1)}, f32[1024,768]{1,0:T(8,128)}, u32[]{:S(2)}) copy-start(f32[1024,768]{1,0:T(8,128)} %get-tuple-element.131.mid_grad_ref) | copy-start | bytes 9437188
  340.3 13.7 %copy-start.48 = (f32[8,768]{1,0:T(8,128)S(1)}, f32[8,768]{1,0:T(8,128)}, u32[]{:S(2)}) copy-start(f32[8,768]{1,0:T(8,128)} %get-tuple-element.140) | copy-start | bytes 73732
  340.4 13.7 %copy-start.45 = (s32[1,1024]{1,0:T(1,128)S(1)}, s32[1,1024]{1,0:T(1,128)}, u32[]{:S(2)}) copy-start(s32[1,1024]{1,0:T(1,128)} %param.30) | copy-start | bytes 12292
  340.4 17.2 %copy-start.32 = (f32[8,128]{1,0:T(8,128)S(1)}, f32[8,128]{1,0:T(8,128)}, u32[]{:S(2)}) copy-start(f32[8,128]{1,0:T(8,128)} %get-tuple-element.123) | copy-start | bytes 12292
  340.4 17.2 %copy-start.54 = (f32[8,128]{1,0:T(8,128)S(1)}, f32[8,128]{1,0:T(8,128)}, u32[]{:S(2)}) copy-start(f32[8,128]{1,0:T(8,128)} %get-tuple-element.143) | copy-start | bytes 12292
  340.4 18.9 %copy-start.49 = (f32[1,3072]{1,0:T(1,128)S(1)}, f32[1,3072]{1,0:T(1,128)}, u32[]{:S(2)}) copy-start(f32[1,3072]{1,0:T(1,128)} %get-tuple-element.141) | copy-start | bytes 36868
  353.5 40.1 %collective-permute-start.1 = (bf16[1024,768]{1,0:T(8,128)(2,1)}, bf16[1024,768]{1,0:T(8,128)(2,1)}, u32[]{:S(2)}, u32[]{:S(2)}) collective-permute-start(bf16[1024,768]{1,0:T(8,128)(2,1)} %get-tuple-element.144), channel_id=1, source_target_pairs={{0,16},{8,24},{16,0},{24,8},{1,17},{9,25},{17,1},{25,9},{2,18},{10... | collective-permute-start | bytes 4718600 | tf_op jit(solution)/shard_map/ppermute | solution.py:1434
  411.7 5.5 collective-permute-start.2
  411.9 7.0 %collective-permute-start.4 = (f32[1,1024]{1,0:T(1,128)S(1)}, f32[1,1024]{1,0:T(1,128)S(1)}, u32[]{:S(2)}, u32[]{:S(2)}) collective-permute-start(f32[1,1024]{1,0:T(1,128)S(1)} %bitcast.59), channel_id=1, source_target_pairs={{0,16},{8,24},{16,0},{24,8},{1,17},{9,25},{17,1},{25,9},{2,18},{10... | collective-permute-start | bytes 12296 | tf_op jit(solution)/shard_map/ppermute | solution.py:1434
  418.8 33.9 %copy-start.41 = (bf16[720,768]{1,0:T(8,128)(2,1)}, bf16[720,768]{1,0:T(8,128)(2,1)S(1)}, u32[]{:S(2)}) copy-start(bf16[720,768]{1,0:T(8,128)(2,1)S(1)} %fusion.9.one_ref) | copy-start | bytes 3317764
  435.3 18.6 %copy-start.46 = (f32[6288]{0:T(1024)S(1)}, f32[6288]{0:T(1024)}, u32[]{:S(2)}) copy-start(f32[6288]{0:T(1024)} %param.40) | copy-start | bytes 75460
  435.3 18.7 %collective-permute-start.6 = (bf16[3168,768]{1,0:T(8,128)(2,1)}, bf16[3168,768]{1,0:T(8,128)(2,1)}, u32[]{:S(2)}, u32[]{:S(2)}) collective-permute-start(bf16[3168,768]{1,0:T(8,128)(2,1)} %shard_map.531.refs_0_), channel_id=1, source_target_pairs={{0,8},{8,0},{16,24},{24,16},{1,9},{9,1},{17,25},{25,17},{2,10},{10... | collective-permute-start | bytes 14598152 | tf_op jit(solution)/shard_map/ppermute | solution.py:1562
  452.4 17.0 %collective-permute-start.5 = (bf16[3168,768]{1,0:T(8,128)(2,1)}, bf16[3168,768]{1,0:T(8,128)(2,1)}, u32[]{:S(2)}, u32[]{:S(2)}) collective-permute-start(bf16[3168,768]{1,0:T(8,128)(2,1)} %shard_map.530.refs_0_), channel_id=1, source_target_pairs={{0,8},{8,0},{16,24},{24,16},{1,9},{9,1},{17,25},{25,17},{2,10},{10... | collective-permute-start | bytes 14598152 | tf_op jit(solution)/shard_map/ppermute | solution.py:1562
  452.7 30.1 %collective-permute-start.7 = (bf16[720,768]{1,0:T(8,128)(2,1)S(1)}, bf16[720,768]{1,0:T(8,128)(2,1)}, u32[]{:S(2)}, u32[]{:S(2)}) collective-permute-start(bf16[720,768]{1,0:T(8,128)(2,1)S(1)} %fusion.9.one_ref), channel_id=1, source_target_pairs={{0,16},{8,24},{16,0},{24,8},{1,17},{9,25},{17,1},{25,9},{2,18},{10... | collective-permute-start | bytes 3317768 | tf_op jit(solution)/shard_map/ppermute | solution.py:1434
  456.4 12.9 %copy-start.5 = (bf16[3168,768]{1,0:T(8,128)(2,1)S(1)}, bf16[3168,768]{1,0:T(8,128)(2,1)}, u32[]{:S(2)}) copy-start(bf16[3168,768]{1,0:T(8,128)(2,1)} %shard_map.530.refs_0_) | copy-start | bytes 14598148
  485.7 5.4 collective-permute-start.8
  500.7 24.5 %copy-start.7 = (f32[512,192]{1,0:T(8,128)}, f32[512,192]{1,0:T(8,128)S(1)}, u32[]{:S(2)}) copy-start(f32[512,192]{1,0:T(8,128)S(1)} %get-tuple-element.226.refs_4_.refs_5_) | copy-start | bytes 1179652
  (49 other events, 147.7 us)

commit v4 on v3

--- a/solution.py
+++ b/solution.py
@@ -137,7 +137,7 @@
                 steps.remove(step)
 
 
-def scatter_sum(link, base, n_row, part, from_col, ins, outs, own, make=None):
+def scatter_sum(link, base, n_row, part, from_col, ins, outs, own, make=None, span=slice(None)):
     row, col = link.row, link.col
     (up_in, down_in), (up_out, down_out) = ins, outs
     y_base, up_base, down_base = base, base + n_row, base + 2 * n_row
@@ -145,7 +145,7 @@
     for at in order:
         if make is not None:
             make(1 - col, at)
-        link.send(part.at[1 - col, at], from_col.at[at], y_base + at, link.device(col=1 - col))
+        link.send(part.at[1 - col, at, span], from_col.at[at, span], y_base + at, link.device(col=1 - col))
     yield
     if make is not None:
         for k, at in enumerate(order):
@@ -155,13 +155,13 @@
     waiting = list(order)
 
     def mine(at):
-        return part[col, at].astype(F32) + from_col[at].astype(F32)
+        return part[col, at, span].astype(F32) + from_col[at, span].astype(F32)
 
     for k in range(n_row - 1):
         for at in (n_row - 1 - k, k):
             if at in waiting:
                 waiting.remove(at)
-                link.landed(from_col.at[at], y_base + at)
+                link.landed(from_col.at[at, span], y_base + at)
         for at, going, more, source, target, base_at, device in (
             (n_row - 1 - k, row < n_row - 1 - k, row > 0, up_in, up_out, up_base, link.device(row=row + 1)),
             (k, row > k, row < n_row - 1, down_in, down_out, down_base, link.device(row=row - 1)),
@@ -169,23 +169,23 @@
 
             @pl.when(going & more)
             def _():
-                link.landed(source.at[at], base_at + at)
-                target[at] = (mine(at) + source[at].astype(F32)).astype(BF16)
+                link.landed(source.at[at, span], base_at + at)
+                target[at, span] = (mine(at) + source[at, span].astype(F32)).astype(BF16)
 
             @pl.when(going & jnp.logical_not(more))
             def _():
-                target[at] = mine(at).astype(BF16)
-
-            link.send(target.at[at], source.at[at], base_at + at, device, going)
+                target[at, span] = mine(at).astype(BF16)
+
+            link.send(target.at[at, span], source.at[at, span], base_at + at, device, going)
         yield
-    own[...] = mine(row)
+    own[span] = mine(row)
 
     for more, source, base_at in ((row > 0, up_in, up_base), (row < n_row - 1, down_in, down_base)):
 
         @pl.when(more)
         def _():
-            link.landed(source.at[row], base_at + row)
-            own[...] += source[row].astype(F32)
+            link.landed(source.at[row, span], base_at + row)
+            own[span] += source[row, span].astype(F32)
 
 
 def spread(link, base, n_row, own, place, onward=None):
@@ -194,8 +194,17 @@
     here = place(row, col)
     link.send(own, here, base + row, up, row < n_row - 1)
     link.send(own, here, base + row, down, row > 0)
+    if onward is not None:
+        yield
     link.send(own, here, base + n_row + row, side)
     yield
+    def arrive(k):
+        for at, there in [(row - k, row >= k), (row + k, row + k < n_row)][: 2 if k else 1]:
+            block = place(at, 1 - col)
+            pl.when(there)(functools.partial(link.landed, block, base + n_row + at))
+            if onward is not None:
+                onward(at, 1 - col, there)
+
     for k in range(1, n_row):
         for at, there, device, further in (
             (row - k, row >= k, up, row < n_row - 1),
@@ -209,14 +218,12 @@
             if onward is not None:
                 onward(at, col, there)
         yield
-    for k in range(n_row):
-        for at, there in [(row - k, row >= k), (row + k, row + k < n_row)][: 2 if k else 1]:
-            block = place(at, 1 - col)
-            pl.when(there)(functools.partial(link.landed, block, base + n_row + at))
-            if onward is not None:
-                onward(at, 1 - col, there)
-        if k % 2:
+        if k > 1:
+            arrive(k - 2)
             yield
+    for k in range(n_row - 2, n_row):
+        arrive(k)
+        yield
 
 
 def spread_matrix(link, base, n_row, shard, whole, by_row, local_sems):
@@ -237,30 +244,40 @@
     x_base, core_base = base + 2 * n_row, base + 4 * n_row
     beside, sibling = link.device(dp=link.beside), link.device(dp=link.sibling)
 
+    def side_of(at_col, x, core):
+        if not by_row:
+            return whole.at[at_col, x, core]
+        return whole.at[:, x, core, :, pl.ds(pl.multiple_of(at_col * columns, 128), columns)]
+
     def to_x(at_row, at_col, when):
         ref = block(at_row, at_col, at_x, at_core)
         link.send(ref, ref, x_base + at_col * n_row + at_row, beside, when)
 
+    def to_core(at_col, x, index):
+        ref = side_of(at_col, x, at_core)
+        link.send(ref, ref, core_base + index, sibling)
+
     yield from spread(link, base, n_row, shard.at[link.dp], lambda r, c: block(r, c, at_x, at_core), to_x)
     for copy in local:
         copy.wait()
-    ref = whole.at[:, at_x, at_core]
-    link.send(ref, ref, core_base, sibling)
+    to_core(0, at_x, 0)
+    to_core(1, at_x, 1)
     yield
-    for k in range(2 * n_row):
-        at_row, at_col = lax.rem(row + k // 2, n_row), 1 - col if k % 2 else col
-        if k:
-            link.landed(block(at_row, at_col, 1 - at_x, at_core), x_base + at_col * n_row + at_row)
-        if k % 2:
-            yield
-    ref = whole.at[:, 1 - at_x, at_core]
-    link.send(ref, ref, core_base + 1, sibling)
+    for index, at_col in enumerate((col, 1 - col)):
+        for k in range(n_row):
+            at_row = lax.rem(row + k, n_row)
+            if k or index:
+                link.landed(block(at_row, at_col, 1 - at_x, at_core), x_base + at_col * n_row + at_row)
+            if k % 2:
+                yield
+        to_core(at_col, 1 - at_x, 2 + at_col)
     yield
-    link.landed(whole.at[:, at_x, 1 - at_core], core_base)
-    link.landed(whole.at[:, 1 - at_x, 1 - at_core], core_base + 1)
-
-
-N_MATRIX = 4 * 4 + 2
+    for at_col in range(2):
+        link.landed(side_of(at_col, at_x, 1 - at_core), core_base + at_col)
+        link.landed(side_of(at_col, 1 - at_x, 1 - at_core), core_base + 2 + at_col)
+
+
+N_MATRIX = 4 * 4 + 4
 
 
 def front_kernel(n_row, ids, table, pos, *refs):
@@ -302,9 +319,9 @@
 
     def tokens():
         for peer in row_peers:
-            rows = pos.at[pl.ds(pl.multiple_of(peer * block, 8), block)]
+            rows = pos.at[:, pl.ds(pl.multiple_of(peer * block, 128), block)]
             link.send(rows, pos_in.at[link.row], pos_base + link.row, link.device(row=peer))
-        pos_in[link.row] = pos[pl.ds(pl.multiple_of(link.row * block, 8), block), :]
+        pos_in[link.row] = pos[:, pl.ds(pl.multiple_of(link.row * block, 128), block)]
         for load in loads:
             load.wait()
         yield from scatter_sum(
@@ -312,7 +329,7 @@
         )
         for peer in row_peers:
             link.landed(pos_in.at[peer], pos_base + peer)
-        pos_own = jnp.concatenate([pos_in[k] for k in range(n_row)], 1)
+        pos_own = jnp.concatenate([pos_in[k] for k in range(n_row)], 0).T
         own_low[...] = (own[...] + pos_own).astype(BF16)
         start[link.col, link.row] = own_low[...]
         yield from spread(link, 3 * n_row, n_row, own_low, lambda r, c: start.at[c, r])
@@ -365,7 +382,7 @@
         in_specs=[pl.BlockSpec(memory_space=pltpu.SMEM), hbm, vmem] + [hbm] * 4,
         out_specs=[vmem, hbm, vmem] + [hbm] * 4,
         scratch_shapes=[pltpu.VMEM(table.shape, F32), pltpu.VMEM((2, BLOCK, width), BF16)]
-        + [pltpu.VMEM((block, width), F32), pltpu.VMEM((n_row, block) + pos.shape[1:], F32)]
+        + [pltpu.VMEM((block, width), F32), pltpu.VMEM((n_row,) + pos.shape[:1] + (block,), F32)]
         + [pltpu.VMEM((2, n_row, block, width), BF16)]
         + [rows] * 5
         + [pltpu.VMEM((block, width), F32), pltpu.VMEM((block, width), BF16)]
@@ -387,14 +404,21 @@
     link = Link(send_sems, recv_sems)
     link.greet(link.plane_neighbours(n_row))
 
-    def steps():
-        yield from scatter_sum(link, 0, n_row, part, from_col, (up_in, down_in), (up_out, down_out), own)
-        own_low[...] = own[...].astype(BF16)
-        total[link.col, link.row] = own_low[...]
-        yield from spread(link, 3 * n_row, n_row, own_low, lambda r, c: total.at[c, r])
-
-    run_together(steps())
+    def steps(base, span):
+        yield from scatter_sum(
+            link, base, n_row, part, from_col, (up_in, down_in), (up_out, down_out), own, None, span
+        )
+        own_low[span] = own[span].astype(BF16)
+        total[link.col, link.row, span] = own_low[span]
+        place = lambda r, c: total.at[c, r, span]
+        yield from spread(link, base + 3 * n_row, n_row, own_low.at[span], place)
+
+    size = own.shape[0] // SPANS
+    run_together(*(steps(5 * n_row * k, pl.ds(k * size, size)) for k in range(SPANS)))
     link.finish()
+
+
+SPANS = 2
 
 
 def plane_total(part, collective_id):
@@ -408,7 +432,7 @@
         out_specs=vmem,
         scratch_shapes=[rows] * 5
         + [pltpu.VMEM((block, width), F32), pltpu.VMEM((block, width), BF16)]
-        + [pltpu.SemaphoreType.DMA((40,)), pltpu.SemaphoreType.DMA((5 * n_row,))],
+        + [pltpu.SemaphoreType.DMA((40 * SPANS,)), pltpu.SemaphoreType.DMA((5 * n_row * SPANS,))],
         compiler_params=pltpu.CompilerParams(
             collective_id=collective_id, has_side_effects=True, vmem_limit_bytes=40 * 1024 * 1024
         ),
@@ -616,6 +640,7 @@
 
 
 BLOCK = 1056
+ROWS = 528
 MEGA = 1024 * 1024
 
 
@@ -833,7 +858,8 @@
     for item in sums[1:]:
         total = total + item[...].astype(F32)
     grad = (total + NOISE * CLIP * noise_ref[...]) * (1.0 / divisor)
-    inside = entries((BLOCK, 1), first) < limit
+    entry = lax.broadcasted_iota(jnp.int32, (ROWS, 1), 0) + (pl.program_id(0) + first) * ROWS
+    inside = entry < limit
     grad_ref[...] = grad
     squares = jnp.where(inside, grad * grad, 0.0)
     mean = jnp.sum(squares, 1, keepdims=True) / grad.shape[1] + 1e-30
@@ -855,21 +881,22 @@
 def table_gradient(sums, noise, old, divisor, first, count, into=None):
     limit, width = noise.shape
     shape = jax.ShapeDtypeStruct
-    rows = pl.BlockSpec((BLOCK, width), lambda i: (i + first, 0))
-    extra = [] if into is None else [into]
+    rows = pl.BlockSpec((ROWS, width), lambda i: (i + first, 0))
+    extra = [] if into is None else list(into)
+    everything = old.shape[0]
     return pl.pallas_call(
         functools.partial(gradient_kernel, limit, len(sums), divisor, first),
         grid=(count,),
-        out_shape=[shape((limit, width), F32), shape((count, 1, BLOCK), F32)]
+        out_shape=[shape((limit, width), F32), shape((everything, 1, ROWS), F32)]
         + [shape((1, width), F32)] * 2
         + [shape((1, 128), F32)],
-        in_specs=[row_block(width)] * len(sums)
-        + [rows, pl.BlockSpec((1, 1, BLOCK), lambda i: (i + first, 0, 0))]
+        in_specs=[pl.BlockSpec((ROWS, width), lambda i: (i, 0))] * len(sums)
+        + [rows, pl.BlockSpec((1, 1, ROWS), lambda i: (i + first, 0, 0))]
         + [pl.BlockSpec(memory_space=pl.ANY)] * len(extra),
-        out_specs=[rows, line_block(BLOCK), whole_block((1, width)), whole_block((1, width))]
+        out_specs=[rows, pl.BlockSpec((1, 1, ROWS), lambda i: (i + first, 0, 0)), whole_block((1, width)), whole_block((1, width))]
         + [whole_block((1, 128))],
-        input_output_aliases={len(sums) + 2: 0} if extra else {},
-        cost_estimate=cost(0, (8 + 2 * len(sums)) * count * BLOCK * width),
+        input_output_aliases={len(sums) + 2: 0, len(sums) + 3: 1} if extra else {},
+        cost_estimate=cost(0, (8 + 2 * len(sums)) * count * ROWS * width),
         compiler_params=pltpu.CompilerParams(vmem_limit_bytes=48 * MEGA),
     )(*sums, noise, old, *extra)
 
@@ -881,7 +908,7 @@
     return jnp.broadcast_to(column, (column.shape[0], 128)).T[:1]
 
 
-BY_ROW = (False, True, True, True, False)
+BY_ROW = (True, True, True, True, False)
 
 
 def put_line(ref, at, line):
@@ -920,10 +947,13 @@
     )(one, two, after)
 
 
-def small_gradients_kernel(divisor, *refs):
-    packed, small, small_second, small_noise = refs[:4]
-    weights, noises, grads = (refs[4 + 5 * k : 9 + 5 * k] for k in range(3))
-    small_outs, (to_col, to_row, square_ref) = refs[19:22], refs[22:]
+def small_gradients_kernel(divisor, core_ref, *refs):
+    half, other_half, small, small_second, small_noise = refs[:5]
+    weights, noises, grads = (refs[5 + 5 * k : 10 + 5 * k] for k in range(3))
+    small_outs, (to_col, to_row, square_ref, packed) = refs[20:23], refs[23:]
+    lines = half.shape[0]
+    packed[pl.ds(pl.multiple_of(core_ref[0] * lines, 16), lines)] = half[...]
+    packed[pl.ds(pl.multiple_of((1 - core_ref[0]) * lines, 16), lines)] = other_half[...]
     width = small.shape[1]
     scale = 1.0 / divisor
     side = weights[1].shape[0]
@@ -941,13 +971,9 @@
     down = weights[4].shape[0]
     grads[4][...] = (packed[first : first + down, :].astype(F32) + NOISE * CLIP * noises[4][...]) * scale
     first += down
-    tall, wide = weights[0].shape[0] // 4, weights[0].shape[1]
-    for k in range(4):
-        lane, start = SIDE * (k % 3), first + tall * (k // 3)
-        part = packed[start : start + tall, lane : lane + wide].astype(F32)
-        lines = slice(k * tall, (k + 1) * tall)
-        grads[0][lines] = (part + NOISE * CLIP * noises[0][lines]) * scale
-    first += 2 * tall
+    tall, wide = weights[0].shape
+    grads[0][...] = (packed[first : first + tall, :wide].astype(F32) + NOISE * CLIP * noises[0][...]) * scale
+    first += tall
 
     to_col[...] = jnp.zeros_like(to_col)
     to_row[...] = jnp.zeros_like(to_row)
@@ -977,22 +1003,26 @@
     small_outs[2][...] = small[...] - size * update
 
 
-def small_gradients(packed, small, small_second, small_noise, weights, noises, divisor):
+def small_gradients(core, half, other_half, small, small_second, small_noise, weights, noises, divisor):
     width = small.shape[1]
     matrix_shapes = [item.shape for item in weights]
     line_rows = [line_places(matrix_shapes, first)[1] for first in (True, False)]
     shape = lambda dims: jax.ShapeDtypeStruct(dims, F32)
-    operands = [packed, small, small_second, small_noise, *weights, *noises]
+    operands = [half, other_half, small, small_second, small_noise, *weights, *noises]
     shapes = matrix_shapes + [small.shape] * 3 + [(line_rows[0], 128), (line_rows[1], 128), (1, 128)]
     out = pl.pallas_call(
         functools.partial(small_gradients_kernel, divisor),
-        grid=(1,),
+        grid_spec=pltpu.PrefetchScalarGridSpec(
+            num_scalar_prefetch=1,
+            grid=(1,),
+            in_specs=[whole_block(item.shape) for item in operands],
+            out_specs=[whole_block(dims) for dims in shapes],
+            scratch_shapes=[pltpu.VMEM((2 * half.shape[0], width), BF16)],
+        ),
         out_shape=[shape(dims) for dims in shapes],
-        in_specs=[whole_block(item.shape) for item in operands],
-        out_specs=[whole_block(dims) for dims in shapes],
-        compiler_params=pltpu.CompilerParams(vmem_limit_bytes=48 * MEGA),
+        compiler_params=pltpu.CompilerParams(vmem_limit_bytes=56 * MEGA),
         cost_estimate=cost(0, 16 * MEGA),
-    )(*operands)
+    )(core, *operands)
     return out[:5], out[5:8], out[8:]
 
 
@@ -1082,48 +1112,78 @@
         + [pltpu.SemaphoreType.DMA((3 * everyone,)), pltpu.SemaphoreType.DMA((2 * everyone + 2 + n_row,))]
         + [pltpu.SemaphoreType.DMA((5,))],
         compiler_params=pltpu.CompilerParams(
-            collective_id=collective_id, has_side_effects=True, vmem_limit_bytes=32 * MEGA
+            collective_id=collective_id, has_side_effects=True, vmem_limit_bytes=58 * MEGA
         ),
     )(table_over, over_cols, over_rows, old_lines, *grads)
 
 
-def update_kernel(table_ref, table_grad_ref, rows_ref, factor_ref, lines_ref, *refs):
-    weights, grads, (table_new_ref, table_cols_ref) = refs[:5], refs[5:10], refs[10:12]
-    rows_outs, cols_outs, news = refs[12:17], refs[17:22], refs[22:27]
-    rows = turned(lax.rsqrt(rows_ref[0]), 128)[:, :1]
-    table_new_ref[...] = table_ref[...] - table_grad_ref[...] * rows * (factor_ref[1:2] * factor_ref[2:3, 5:6])
-
-    @pl.when(pl.program_id(0) == 0)
+def update_kernel(table_ref, table_grad_ref, rows_ref, all_rows_ref, factor_ref, lines_ref, *refs):
+    weights, grads, (table_new_ref, table_rows_ref, table_cols_ref) = refs[:5], refs[5:10], refs[10:13]
+    rows_outs, cols_outs, news = refs[13:18], refs[18:23], refs[23:28]
+    held_weights, held_grads, (load_sems, store_sems) = refs[28:33], refs[33:38], refs[38:]
+    at, last = pl.program_id(0), pl.num_programs(0) - 1
+    loads = [
+        pltpu.make_async_copy(source, target, load_sems.at[k])
+        for k, (source, target) in enumerate(zip(weights + grads, held_weights + held_grads))
+    ]
+    stores = [pltpu.make_async_copy(held_weights[k], news[k], store_sems.at[k]) for k in range(5)]
+
+    @pl.when(at == 0)
     def _():
+        for load in loads:
+            load.start()
+        limit = table_rows_ref.shape[0]
+        line = jnp.concatenate([all_rows_ref[k] for k in range(all_rows_ref.shape[0])], 1)
+        table_rows_ref[...] = line[:, :limit].reshape(limit)
         table_cols_ref[...] = factor_ref[0:1].reshape(table_cols_ref.shape)
+
+    factors = factor_ref[1:2] * factor_ref[2:3, 5:6]
+    for k in range(BLOCK // ROWS):
+        part = slice(k * ROWS, (k + 1) * ROWS)
+        rows = turned(lax.rsqrt(rows_ref[k]), 128)[:, :1]
+        table_new_ref[part] = table_ref[part] - table_grad_ref[part] * rows * factors
+
+    @pl.when(at == last - 1)
+    def _():
+        for load in loads:
+            load.wait()
         for index in range(5):
-            count_rows, count_cols = weights[index].shape
+            count_rows, count_cols = held_weights[index].shape
             rows_line = lines_ref[index : index + 1, :count_rows]
             cols_line = lines_ref[8 + index : 9 + index, :count_cols]
             rows_outs[index][...] = rows_line.reshape(count_rows)
             cols_outs[index][...] = cols_line.reshape(count_cols)
             rows = turned(lax.rsqrt(rows_line), 128)[:, :1]
             factors = factor_ref[2:3, index : index + 1] * lax.rsqrt(cols_line)
-            news[index][...] = weights[index][...] - grads[index][...] * rows * factors
+            held_weights[index][...] = held_weights[index][...] - held_grads[index][...] * rows * factors
+            stores[index].start()
+
+    @pl.when(at == last)
+    def _():
+        for store in stores:
+            store.wait()
 
 
 def update(table, table_grad, table_rows, factors, lines, weights, grads):
     limit, width = table.shape
     shape = lambda dims: jax.ShapeDtypeStruct(dims, F32)
-    small_shapes = [(width,)] + [item.shape[:1] for item in weights] + [item.shape[1:] for item in weights]
-    small_shapes += [item.shape for item in weights]
+    small_shapes = [(limit,), (width,)] + [item.shape[:1] for item in weights] + [item.shape[1:] for item in weights]
+    matrix_shapes = [item.shape for item in weights]
+    hbm = pl.BlockSpec(memory_space=pl.ANY)
     out = pl.pallas_call(
         update_kernel,
         grid=(blocks_of(limit),),
-        out_shape=[shape(table.shape)] + [shape(dims) for dims in small_shapes],
-        in_specs=[row_block(width), row_block(width), line_block(BLOCK), whole_block(factors.shape)]
-        + [whole_block(lines.shape)]
-        + [whole_block(item.shape) for item in weights] * 2,
-        out_specs=[row_block(width)] + [whole_block(dims) for dims in small_shapes],
-        compiler_params=pltpu.CompilerParams(vmem_limit_bytes=56 * MEGA),
+        out_shape=[shape(table.shape)] + [shape(dims) for dims in small_shapes + matrix_shapes],
+        in_specs=[row_block(width), row_block(width), line_block(ROWS, BLOCK // ROWS), whole_block(table_rows.shape)]
+        + [whole_block(factors.shape), whole_block(lines.shape)]
+        + [hbm] * 10,
+        out_specs=[row_block(width)] + [whole_block(dims) for dims in small_shapes] + [hbm] * 5,
+        scratch_shapes=[pltpu.VMEM(dims, F32) for dims in matrix_shapes * 2]
+        + [pltpu.SemaphoreType.DMA((10,)), pltpu.SemaphoreType.DMA((5,))],
+        compiler_params=pltpu.CompilerParams(vmem_limit_bytes=58 * MEGA),
         cost_estimate=cost(0, 3 * 4 * limit * width),
-    )(table, table_grad, table_rows, factors, lines, *weights, *grads)
-    return out[0], out[1], out[2:7], out[7:12], out[12:]
+    )(table, table_grad, table_rows, table_rows, factors, lines, *weights, *grads)
+    return out[0], out[1], out[2], out[3:8], out[8:13], out[13:]
 
 
 HIDDEN = 1024
@@ -1176,8 +1236,13 @@
             low_ref[rows] = (normed_of(mid)[0] * small_ref[5:6] + small_ref[6:7]).astype(BF16)
             total[rows] = mid + small_ref[11:12]
 
-    for rows in chunks_of(length):
-        hidden = gelu_parts(mm(low_ref[rows], up_ref[...]) + bias_ref[...])[0].astype(BF16)
+    chunks = chunks_of(length)
+    later = mm(low_ref[chunks[0]], up_ref[...])
+    for k, rows in enumerate(chunks):
+        product = later
+        if k + 1 < len(chunks):
+            later = mm(low_ref[chunks[k + 1]], up_ref[...])
+        hidden = gelu_parts(product + bias_ref[...])[0].astype(BF16)
         total[rows] += mm_nt(hidden, down_ref[...])
 
     @pl.when(at == pl.num_programs(0) - 1)
@@ -1308,13 +1373,13 @@
         + [whole_block(small.shape)],
         out_specs=[tokens, tokens, tokens, whole_block((8, width))],
         cost_estimate=cost(6 * length * width * width, 20 * length * width),
-        compiler_params=pltpu.CompilerParams(vmem_limit_bytes=40 * MEGA),
+        compiler_params=pltpu.CompilerParams(vmem_limit_bytes=56 * MEGA),
     )(packed_grad, weight, mid_grad, start, small)
 
 
 def weight_grads_kernel(place_ref, ones_ref, mixed_ref, low_ref, *refs):
     packed, (branch_ref, pre_ref, down_ref, act_ref, grad_ref, small_ref) = refs[:3], refs[3:9]
-    out_ref, square_ref, wide = refs[9:]
+    out_ref, square_ref, wide, turned_grad = refs[9:]
     width = ones_ref.shape[1]
     tall = width // 4
     start = pl.multiple_of(place_ref[0], 128)
@@ -1342,14 +1407,10 @@
         square = square + jnp.sum(grad * grad, 0, keepdims=True)
     square_ref[...] = square
     first += half
-    tall = grad_ref.shape[0] // 4
-    lines = out_ref.shape[0] - first
-    out_ref[first:, :] = jnp.zeros((lines, width), F32)
-    for k in range(4):
-        rows = slice(first + tall * (k // 3), first + tall * (k // 3) + tall)
-        part = grad_ref[k * tall : (k + 1) * tall, pl.ds(start, SIDE)]
-        out_ref[rows, SIDE * (k % 3) : SIDE * (k % 3 + 1)] = jnp.where(skip > 0, pltpu.roll(part, SIDE - width // 12, 1), part)
-    first += 2 * tall
+    turned_grad[...] = grad_ref[:, pl.ds(start, SIDE)].T
+    out_ref[first:, :] = jnp.zeros((out_ref.shape[0] - first, width), F32)
+    out_ref[first : first + tall, : grad_ref.shape[0]] = turned_grad[pl.ds(skip, tall), :]
+    first += tall
     out_ref[first : first + small_ref.shape[0], :] = small_ref[...]
 
 
@@ -1362,7 +1423,7 @@
     place = jnp.stack([first // 128 * 128, first % 128, row_at, col_at]).astype(jnp.int32)
     unit = lambda k: pl.BlockSpec((1, length, half), lambda i, at: ((3 * at[3] + k) // 2, 0, (3 * at[3] + k) % 2))
     by_col = lambda size: pl.BlockSpec((length, size), lambda i, at: (0, at[3]))
-    lines = 4 * tall + half + tokens // 2 + 32
+    lines = 5 * tall + half + 32
     return pl.pallas_call(
         weight_grads_kernel,
         grid_spec=pltpu.PrefetchScalarGridSpec(
@@ -1373,7 +1434,7 @@
             + [by_col(half), by_col(hidden), by_col(half), pl.BlockSpec((length, width), lambda i, at: (0, at[2]))]
             + [pl.BlockSpec((tokens, width), lambda i, at: (at[3], 0)), whole_block(small_ex.shape)],
             out_specs=[whole_block((lines, width)), whole_block((1, half))],
-            scratch_shapes=[pltpu.VMEM((SIDE, half), F32)],
+            scratch_shapes=[pltpu.VMEM((SIDE, half), F32), pltpu.VMEM((SIDE, tokens), F32)],
         ),
         out_shape=[shape((lines, width), F32), shape((1, half), F32)],
         cost_estimate=cost(2 * length * width * width * 2, 16 * length * width),
@@ -1443,7 +1504,7 @@
     if tuned:
         shards = [item.reshape(n_data, -1, item.shape[1]) for item in lows]
         start, table_low, table_sq, qkv_full, attn_full, up_full, down_full = front(
-            ids, tok_table, pos_table, shards, n_row
+            ids, tok_table, pos_table.T, shards, n_row
         )
         stream_in = start.reshape(length, width)
         qkv_full, attn_full, up_full, down_full = (
@@ -1553,7 +1614,8 @@
     divisor = SAMPLE * n_data
     vocab = vocab_here * n_row * n_col
     count = blocks_of(vocab_here)
-    table_old = jnp.pad(table_rows, (0, count * BLOCK - vocab_here), constant_values=1.0).reshape(count, 1, BLOCK)
+    table_old = jnp.pad(table_rows, (0, count * BLOCK - vocab_here), constant_values=1.0).reshape(-1, 1, ROWS)
+    fine = BLOCK // ROWS
     olds = [(pos_rows, pos_cols), (qkv_rows, qkv_cols), (attn_rows, attn_cols), (up_rows, up_cols)]
     olds.append((down_rows, down_cols))
     ends = (token_ids.shape[1] * jnp.sum(taken), example_norm[None])
@@ -1572,18 +1634,19 @@
         pair_sums = [[item, to_core(item)] for item in pair_sums]
         into, over = None, []
         for pair, span in zip(pair_sums, spans):
-            into, *more = table_gradient(pair, table_noise, table_old, divisor, *span, into)
-            over.append(more)
-        table_grad = into
-        half = join(half, from_beside, over[1][1])
+            *into, cols, scaled, level = table_gradient(
+                pair, table_noise, table_old, divisor, span[0] * fine, span[1] * fine, into
+            )
+            over.append((cols, scaled, level))
+        table_grad, rows_blocks = into
+        half = join(half, from_beside, cols)
         other_half = to_core(half)
-        packed = jnp.concatenate(
-            [jnp.where(core == 0, half, other_half), jnp.where(core == 0, other_half, half)], 0
-        )
-        rows_blocks = jnp.concatenate([item[0] for item in over], 0)
-        cols, scaled, level = (over[0][k] + over[1][k] for k in (1, 2, 3))
+        cols, scaled, level = (over[0][k] + over[1][k] for k in range(3))
+        turn = lambda items: [items[1].T] + list(items[2:])
+        matrices, matrix_noises = turn(weights_in), turn(noises)
+        olds[0] = olds[0][::-1]
         small_grads, smalls, (over_cols, over_rows, squares) = small_gradients(
-            packed, small_params, small_second, small_noise, weights_in[1:], noises[1:], divisor
+            core[None], half, other_half, small_params, small_second, small_noise, matrices, matrix_noises, divisor
         )
         scalars = jnp.where(jnp.arange(128) == 5, jnp.sum(table_sq), squares[0])
         table_over = jnp.concatenate([cols[0], scaled[0], scalars, level[0]]).reshape(-1, 128)
@@ -1594,11 +1657,12 @@
         lines, factors = statistics(
             table_over, over_cols, over_rows, old_lines, small_grads, width, n_row, vocab, 5
         )
-        table_new, table_cols_new, rows_new, cols_new, news = update(
-            tok_table, table_grad, rows_blocks, factors, lines, weights_in[1:], small_grads
+        table_new, table_rows_new, table_cols_new, rows_new, cols_new, news = update(
+            tok_table, table_grad, rows_blocks, factors, lines, matrices, small_grads
         )
-        outputs = [table_grad, rows_blocks.reshape(-1)[:vocab_here], table_cols_new, table_new]
-        for group in zip(small_grads, rows_new, cols_new, news):
+        outputs = [table_grad, table_rows_new, table_cols_new, table_new]
+        outputs.extend([small_grads[0].T, cols_new[0], rows_new[0], news[0].T])
+        for group in zip(small_grads[1:], rows_new[1:], cols_new[1:], news[1:]):
             outputs.extend(group)
         return tuple(outputs) + tuple(smalls) + (loss_sum,) + ends
 
@@ -1610,7 +1674,7 @@
     sums = [example_sum(item).astype(F32) for item in others]
     grads = [(sums[index] + NOISE * CLIP * noises[index + 1]) / divisor for index in range(5)]
     table_grad, table_rows_new, *table_over = table_gradient(
-        [table_sum_all], table_noise, table_old, divisor, 0, count
+        [table_sum_all], table_noise, table_old, divisor, 0, pl.cdiv(vocab_here, ROWS)
     )
     table_rows_new = table_rows_new.reshape(-1)[:vocab_here]
     by_row = [False, True, True, True, False]

time: 559 us -> 536 us (0.959)
  Pallas kernels: 460 us -> 447 us
  local copies, waits for them, and re-layouts: 35.4 us -> 23.7 us
    unnamed x135 -> x94, local copies, waits for them, and re-layouts: 30 us -> 16.4 us
    pallas_call x1, Pallas kernels: 104 us -> 91.4 us  [front(): pl.pallas_call(functools.partial(front_kernel, n_row), out_shape=[shape((...]
  transfers between devices with their start and end apart: 9 -> 9, of which waited for: 0 -> 0; matrix products, arithmetic and copies ran while one was open for 8% -> 9% of each run, Pallas kernels for 71% -> 72%
where the time goes in v4:
time: 536 us; the launch traced here: 529 us
  Pallas kernels  447 us (83%)
  other arithmetic  36.1 us (7%)
  local copies, waits for them, and re-layouts  23.7 us (4%)
  between operations  9.5 us (2%)
  starting transfers between devices  7.79 us (1%)
    pallas_call x1, Pallas kernels, front(): pl.pallas_call(functools.partial(front_kernel, n_row), out_shape=[shape((...  91.4 us
    pallas_call x1, Pallas kernels, plane_total(): pl.pallas_call(functools.partial(total_kernel, n_row), out_shape=jax.Shap...  50 us
    pallas_call x2, Pallas kernels, table_sum(): pl.pallas_call(functools.partial(table_sum_kernel, first), grid_spec=pltp...  33.6 us
    pallas_call x1, Pallas kernels, middle_back(): pl.pallas_call(middle_back_kernel, grid=(hidden // HIDDEN,), out_shape=[s...  33.3 us
    pallas_call x1, Pallas kernels, head_back(): pl.pallas_call(head_back_kernel, grid=(low.shape[0] // BLOCK,), out_shape...  29.1 us
    pallas_call x1, Pallas kernels, attend_back(): pl.pallas_call(attend_back_kernel, grid=(pairs,), out_shape=jax.ShapeDtyp...  27.4 us
    pallas_call x2, Pallas kernels, table_gradient(): pl.pallas_call(functools.partial(gradient_kernel, limit, len(sums), divis...  25.5 us
    pallas_call x1, Pallas kernels, update(): pl.pallas_call(update_kernel, grid=(blocks_of(limit),), out_shape=[shape(...  23.8 us
  transfers between devices with their start and end apart: 9, of which 0 were waited for; matrix products, arithmetic and copies ran while one was open for 9% of the time, Pallas kernels for 72%

profile of v4, /device:TPU:0, one launch (start us, length us, event | category | flops | bytes accessed | tf_op | source)
XLA Modules:
  0.0 528.7 jit_solution(12736840618891041885)
XLA Ops:
  1.5 3.0 collective-permute-start
  12.0 91.4 %shard_map.517 = (bf16[2,4,128,768]{3,2,1,0:T(8,128)(2,1)}, bf16[6336,768]{1,0:T(8,128)(2,1)}, f32[1,768]{1,0:T(1,128)}, bf16[4,2,2,48,2304]{4,3,2,1,0:T(8,128)(...) custom-call(s32[1024]{0:T(1024)} %bitcast.80, ...), custom_call_target="tpu_custom_call" | custom-call | tf_op jit(solution)/shard_map/pallas_call | solution.py:378
  107.6 4.3 add_convert_fusion.q_ref.k_ref.v_ref
  111.9 15.0 %shard_map.518 = (bf16[1024,768]{1,0:T(8,128)(2,1)S(1)}, f32[6,2,1024]{2,1,0:T(2,128)S(1)}) custom-call(bf16[1024,2304]{1,0:T(8,128)(2,1)S(1)} %add_convert_fusion.q_ref.k_ref.v_ref, bf16[1024,2304]{1,0:T(8,128)(2,1)S(1)} %add_convert_fusion.q_ref.k_ref.v_ref, bf16[1024,2304]{1,0:T(8,128)(2,1)S(1)} %add_convert_fusion.q_ref.k_ref.v_ref), custom_call_target="tpu_custom_call" | custom-call | flops 16106127360 | bytes 6291456 | tf_op jit(solution)/shard_map/pallas_call | solution.py:492
  128.7 21.1 %shard_map.519 = (f32[1024,768]{1,0:T(8,128)}, bf16[1024,768]{1,0:T(8,128)(2,1)}, f32[1024,768]{1,0:T(8,128)}, bf16[1024,768]{1,0:T(8,128)(2,1)}) custom-call(bf16[1024,768]{1,0:T(8,128)(2,1)} %bitcast.64, bf16[1024,768]{1,0:T(8,128)(2,1)} %copy-done.1, bf16[768,768]{1,0:T(8,128)(2,1)} %bitcast.98, bf16[768,3072]{1,0:T(8,128)(2,1)} %bitcast.92, ...), custom_call_target="tpu_custom_call" | custom-call | flops 9663676416 | bytes 12582912 | tf_op jit(solution)/shard_map/pallas_call | solution.py:1261
  152.6 18.8 %shard_map.520 = (bf16[6336,1024]{1,0:T(8,128)(2,1)}, f32[18,1,1024]{2,1,0:T(1,128)S(1)}, f32[18,1,1024]{2,1,0:T(1,128)S(1)}, f32[1,1024]{1,0:T(1,128)S(1)}) custom-call(bf16[6336,768]{1,0:T(8,128)(2,1)} %get-tuple-element.112.low_ref.refs_0_, bf16[1024,768]{1,0:T(8,128)(2,1)S(1)} %copy-done.12, s32[1,1024]{1,0:T(1,128)S(1)} %and_select_fusion.1.target_ref), custom_call_target="tpu_custom_call" | custom-call | flops 9890168832 | bytes 22536192 | tf_op jit(solution)/shard_map/pallas_call | solution.py:708
  173.3 8.7 %shard_map.521 = (f32[8,128]{1,0:T(8,128)}, f32[8,128]{1,0:T(8,128)}) custom-call(f32[18,8,128]{2,1,0:T(8,128)} %bitcast.59, f32[18,8,128]{2,1,0:T(8,128)} %bitcast.60, f32[8,128]{1,0:T(8,128)} %bitcast.61), custom_call_target="tpu_custom_call" | custom-call | tf_op jit(solution)/shard_map/pallas_call | solution.py:630
  183.6 29.1 %shard_map.522 = (bf16[1024,768]{1,0:T(8,128)(2,1)S(1)}, bf16[6336,768]{1,0:T(8,128)(2,1)}) custom-call(bf16[6336,1024]{1,0:T(8,128)(2,1)} %get-tuple-element.120.exp_ref, f32[18,1,1024]{2,1,0:T(1,128)S(1)} %copy-done.5, f32[1,1024]{1,0:T(1,128)S(1)} %bitcast.62, s32[1,1024]{1,0:T(1,128)S(1)} %and_select_fusion.1.target_ref, ...), custom_call_target="tpu_custom_call" | custom-call | flops 19931332608 | bytes 32440320 | tf_op jit(solution)/shard_map/pallas_call | solution.py:748
  212.7 50.0 %shard_map.523 = bf16[2,4,128,768]{3,2,1,0:T(8,128)(2,1)S(1)} custom-call(bf16[2,4,128,768]{3,2,1,0:T(8,128)(2,1)S(1)} %bitcast.58), custom_call_target="tpu_custom_call" | custom-call | tf_op jit(solution)/shard_map/pallas_call | solution.py:428
  263.9 33.3 %shard_map.524 = (bf16[1024,768]{1,0:T(8,128)(2,1)}, bf16[1024,3072]{1,0:T(8,128)(2,1)}, bf16[1024,3072]{1,0:T(8,128)(2,1)}, f32[1,3072]{1,0:T(1,128)}, f32[1024...) custom-call(bf16[1024,768]{1,0:T(8,128)(2,1)} %bitcast.57, ...), custom_call_target="tpu_custom_call" | custom-call | flops 14495514624 | bytes 31457280 | tf_op jit(solution)/shard_map/pallas_call | solution.py:1330
  298.7 27.4 %shard_map.525.packed_ref.refs_0_.refs_1_.refs_2_ = bf16[3,1024,768]{2,1,0:T(8,128)(2,1)} custom-call(bf16[1024,2304]{1,0:T(8,128)(2,1)} %copy-done.14, bf16[1024,2304]{1,0:T(8,128)(2,1)} %copy-done.14, bf16[1024,2304]{1,0:T(8,128)(2,1)} %copy-done.14, bf16[1024,768]{1,0:T(8,128)(2,1)S(1)} %copy-done.15, f32[6,2,1024]{2,1,0:T(2,128)S(1)} %get-tuple-element.131.log_ref), custom_call_target="tpu_custom_call" | custom-call | flops 24159191040 | bytes 12582912 | tf_op jit(solution)/shard_map/pallas_call | solution.py:548
  326.1 11.6 %shard_map.526 = (f32[1024,768]{1,0:T(8,128)}, bf16[1024,768]{1,0:T(8,128)(2,1)}, f32[1024,768]{1,0:T(8,128)}, f32[8,768]{1,0:T(8,128)}) custom-call(bf16[3,1024,768]{2,1,0:T(8,128)(2,1)} %shard_map.525.packed_ref.refs_0_.refs_1_.refs_2_, bf16[768,2304]{1,0:T(8,128)(2,1)} %bitcast.96, f32[1024,768]{1,0:T(8,128)} %get-tuple-element.132.mid_grad_ref, ...), custom_call_target="tpu_custom_call" | custom-call | flops 3623878656 | bytes 15728640 | tf_op jit(solution)/shard_map/pallas_call | solution.py:1368
  348.4 11.2 %shard_map.528 = (f32[1376,768]{1,0:T(8,128)}, f32[1,384]{1,0:T(1,128)}) custom-call(s32[4]{0:T(128)} %pad_add_fusion.1.place_ref, bf16[1024,768]{1,0:T(8,128)(2,1)} %add_convert_fusion.1.ones_ref, bf16[1024,768]{1,0:T(8,128)(2,1)} %copy-done.1, bf16[1024,768]{1,0:T(8,128)(2,1)} %get-tuple-element.129.refs_3_.low_ref, ...), custom_call_target="tpu_custom_call" | custom-call | flops 2415919104 | bytes 12582912 | tf_op jit(solution)/shard_map/pallas_call | solution.py:1427
  364.3 11.3 %shard_map.527 = (bf16[6336,768]{1,0:T(8,128)(2,1)}, f32[1,768]{1,0:T(1,128)}) custom-call(s32[1024]{0:T(1024)} %broadcast_subtract_fusion.ids_ref, s32[1024]{0:T(1024)} %get-tuple-element.200.order_ref, s32[7]{0:T(128)} %get-tuple-element.204.bounds_ref, bf16[6336,768]{1,0:T(8,128)(2,1)} %get-tuple-element.125.table_ref, ...), custom_call_target="tpu_custom_call" | custom-call | bytes 19464192 | tf_op jit(solution)/shard_map/pallas_call | solution.py:801
  378.9 11.5 %shard_map.529 = f32[8,128]{1,0:T(8,128)} custom-call(f32[8,128]{1,0:T(8,128)} %fusion.10.value), custom_call_target="tpu_custom_call" | custom-call | tf_op jit(solution)/shard_map/pallas_call | solution.py:592
  392.4 3.2 multiply_convert_fusion
  404.1 16.5 %shard_map.531.refs_0_ = bf16[3168,768]{1,0:T(8,128)(2,1)} custom-call(s32[1024]{0:T(1024)S(1)} %broadcast_subtract_fusion.1.ids_ref, s32[1024]{0:T(1024)S(1)} %get-tuple-element.202.order_ref, s32[7]{0:T(128)S(1)} %get-tuple-element.205.bounds_ref, f32[2]{0:T(128)S(1)} %pad_maximum_fusion.1.share_ref, bf16[6336,768]{1,0:T(8,128)(2,1)} %get-tuple-element.112.low_ref.refs_0_, ...), custom_call_target="tpu_custom_call" | custom-call | flops 9965666304 | bytes 14598144 | tf_op jit(solution)/shard_map/pallas_call | solution.py:833
  420.6 17.1 %shard_map.530.refs_0_ = bf16[3168,768]{1,0:T(8,128)(2,1)} custom-call(s32[1024]{0:T(1024)S(1)} %broadcast_subtract_fusion.1.ids_ref, s32[1024]{0:T(1024)S(1)} %get-tuple-element.202.order_ref, s32[7]{0:T(128)S(1)} %get-tuple-element.205.bounds_ref, f32[2]{0:T(128)S(1)} %pad_maximum_fusion.1.share_ref, bf16[6336,768]{1,0:T(8,128)(2,1)} %get-tuple-element.112.low_ref.refs_0_, ...), custom_call_target="tpu_custom_call" | custom-call | flops 9965666304 | bytes 14598144 | tf_op jit(solution)/shard_map/pallas_call | solution.py:833
  442.5 12.9 %shard_map.532 = (f32[6288,768]{1,0:T(8,128)}, f32[12,1,528]{2,1,0:T(1,128)S(1)}, f32[1,768]{1,0:T(1,128)S(1)}, f32[1,768]{1,0:T(1,128)S(1)}, f32[1,128]{1,0:T(1,128)S(1)}) custom-call(bf16[3168,768]{1,0:T(8,128)(2,1)S(1)} %copy-done, bf16[3168,768]{1,0:T(8,128)(2,1)} %collective-permute-done.6.refs_1_, f32[6288,768]{1,0:T(8,128)} %refs_2_.5, ...), custom_call_target="tpu_custom_call" | custom-call | bytes 29196288 | tf_op jit(solution)/shard_map/pallas_call | solution.py:887
  455.4 12.6 %shard_map.533 = (f32[6288,768]{1,0:T(8,128)}, f32[12,1,528]{2,1,0:T(1,128)S(1)}, f32[1,768]{1,0:T(1,128)S(1)}, f32[1,768]{1,0:T(1,128)S(1)}, f32[1,128]{1,0:T(1,128)S(1)}) custom-call(bf16[3168,768]{1,0:T(8,128)(2,1)S(1)} %bitcast.56, bf16[3168,768]{1,0:T(8,128)(2,1)} %collective-permute-done.5.refs_1_, ...), custom_call_target="tpu_custom_call", output_to_operand_aliasing={{0}: (4, {}), {1}: (5, {})} | custom-call | bytes 29196288 | tf_op jit(solution)/shard_map/pallas_call | solution.py:887
  469.7 2.8 shard_map.534.refs_0_
  479.1 6.6 %shard_map.535 = (f32[192,512]{1,0:T(8,128)}, f32[192,1152]{1,0:T(8,128)}, f32[192,384]{1,0:T(8,128)}, f32[192,1536]{1,0:T(8,128)}, f32[384,768]{1,0:T(8,128)}, ...) custom-call(s32[1]{0:T(128)} %bitcast.33.core_ref, ...), custom_call_target="tpu_custom_call" | custom-call | bytes 16777216 | tf_op jit(solution)/shard_map/pallas_call | solution.py:1013
  487.6 14.7 %shard_map.536 = (f32[16,1536]{1,0:T(8,128)}, f32[8,768]{1,0:T(8,128)}) custom-call(f32[16,128]{1,0:T(8,128)} %pad.54.refs_0_, f32[16,128]{1,0:T(8,128)} %get-tuple-element.164.refs_1_, f32[32,128]{1,0:T(8,128)} %get-tuple-element.165.refs_2_, f32[16,1536]{1,0:T(8,128)} %stack.80.refs_3_, f32[192,512]{1,0:T(8,128)} %get-tuple-element.166.refs_4_.refs_5_, ...), custom_call_target="tpu_custom_call" | custom-call | tf_op jit(solution)/shard_map/pallas_call | solution.py:1103
  502.3 23.8 %shard_map.537 = (f32[6288,768]{1,0:T(8,128)}, f32[6288]{0:T(1024)}, f32[768]{0:T(1024)}, f32[192]{0:T(256)}, f32[192]{0:T(256)}, /*index=5*/f32[192]{0:T(256)},...) custom-call(f32[6288,768]{1,0:T(8,128)} %table_ref.1, ...), custom_call_target="tpu_custom_call" | custom-call | bytes 57950208 | tf_op jit(solution)/shard_map/pallas_call | solution.py:1173
  (189 shorter events, 61.5 us)
Async XLA Ops:
  0.7 10.7 %copy-start.21 = (f32[192,384]{1,0:T(8,128)S(1)}, f32[192,384]{1,0:T(8,128)}, u32[]{:S(2)}) copy-start(f32[192,384]{1,0:T(8,128)} %refs_2_.7) | copy-start | bytes 884740
  1.5 362.0 %collective-permute-start = (s32[2,1024]{1,0:T(2,128)S(1)}, s32[2,1024]{1,0:T(2,128)S(1)}, u32[]{:S(2)}, u32[]{:S(2)}) collective-permute-start(s32[2,1024]{1,0:T(2,128)S(1)} %pad_add_fusion), channel_id=1, source_target_pairs={{0,16},{8,24},{16,0},{24,8},{1,17},{9,25},{17,1},{25,9},{2,18},{10... | collective-permute-start | bytes 24584 | tf_op jit(solution)/shard_map/ppermute | solution.py:1495
  111.9 15.0 %copy-start.14 = (bf16[1024,2304]{1,0:T(8,128)(2,1)}, bf16[1024,2304]{1,0:T(8,128)(2,1)S(1)}, u32[]{:S(2)}) copy-start(bf16[1024,2304]{1,0:T(8,128)(2,1)S(1)} %add_convert_fusion.q_ref.k_ref.v_ref) | copy-start | bytes 14155780
  128.7 22.5 %copy-start.27 = (s32[1,1024]{1,0:T(1,128)S(1)}, s32[1,1024]{1,0:T(1,128)}, u32[]{:S(2)}) copy-start(s32[1,1024]{1,0:T(1,128)} %param.31) | copy-start | bytes 12292
  149.7 254.3 %collective-permute-start.3 = (bf16[1024,768]{1,0:T(8,128)(2,1)}, bf16[1024,768]{1,0:T(8,128)(2,1)S(1)}, u32[]{:S(2)}, u32[]{:S(2)}) collective-permute-start(bf16[1024,768]{1,0:T(8,128)(2,1)} %get-tuple-element.119.z_ref), channel_id=1, source_target_pairs={{0,16},{8,24},{16,0},{24,8},{1,17},{9,25},{17,1},{25,9},{2,18},{10... | collective-permute-start | bytes 4718600 | tf_op jit(solution)/shard_map/ppermute | solution.py:1495
  152.6 29.4 %copy-start.13 = (bf16[1024,768]{1,0:T(8,128)(2,1)S(1)}, bf16[1024,768]{1,0:T(8,128)(2,1)}, u32[]{:S(2)}) copy-start(bf16[1024,768]{1,0:T(8,128)(2,1)} %get-tuple-element.119.z_ref) | copy-start | bytes 4718596
  326.1 12.1 %copy-start.28 = (f32[8,768]{1,0:T(8,128)S(1)}, f32[8,768]{1,0:T(8,128)}, u32[]{:S(2)}) copy-start(f32[8,768]{1,0:T(8,128)} %get-tuple-element.141) | copy-start | bytes 73732
  326.1 12.1 %copy-start.25 = (s32[1,1024]{1,0:T(1,128)S(1)}, s32[1,1024]{1,0:T(1,128)}, u32[]{:S(2)}) copy-start(s32[1,1024]{1,0:T(1,128)} %param.30) | copy-start | bytes 12292
  326.1 16.4 %copy-start.11 = (f32[8,128]{1,0:T(8,128)S(1)}, f32[8,128]{1,0:T(8,128)}, u32[]{:S(2)}) copy-start(f32[8,128]{1,0:T(8,128)} %get-tuple-element.124) | copy-start | bytes 12292
  326.1 16.4 %copy-start.34 = (f32[8,128]{1,0:T(8,128)S(1)}, f32[8,128]{1,0:T(8,128)}, u32[]{:S(2)}) copy-start(f32[8,128]{1,0:T(8,128)} %get-tuple-element.144) | copy-start | bytes 12292
  326.1 18.8 %copy-start.29 = (f32[1,3072]{1,0:T(1,128)S(1)}, f32[1,3072]{1,0:T(1,128)}, u32[]{:S(2)}) copy-start(f32[1,3072]{1,0:T(1,128)} %get-tuple-element.142) | copy-start | bytes 36868
  326.1 20.5 %copy-start.16 = (bf16[2,4,128,768]{3,2,1,0:T(8,128)(2,1)S(1)}, bf16[2,4,128,768]{3,2,1,0:T(8,128)(2,1)}, u32[]{:S(2)}) copy-start(bf16[2,4,128,768]{3,2,1,0:T(8,128)(2,1)} %get-tuple-element.113) | copy-start | bytes 4718596
  337.8 41.1 %collective-permute-start.1 = (bf16[1024,768]{1,0:T(8,128)(2,1)}, bf16[1024,768]{1,0:T(8,128)(2,1)}, u32[]{:S(2)}, u32[]{:S(2)}) collective-permute-start(bf16[1024,768]{1,0:T(8,128)(2,1)} %get-tuple-element.145), channel_id=1, source_target_pairs={{0,16},{8,24},{16,0},{24,8},{1,17},{9,25},{17,1},{25,9},{2,18},{10... | collective-permute-start | bytes 4718600 | tf_op jit(solution)/shard_map/ppermute | solution.py:1495
  396.9 5.6 %collective-permute-start.2 = (bf16[688,768]{1,0:T(8,128)(2,1)S(1)}, bf16[688,768]{1,0:T(8,128)(2,1)}, u32[]{:S(2)}, u32[]{:S(2)}) collective-permute-start(bf16[688,768]{1,0:T(8,128)(2,1)S(1)} %dynamic-slice_bitcast_fusion), channel_id=1, source_target_pairs={{0,8},{8,0},{16,24},{24,16},{1,9},{9,1},{17,25},{25,17},{2,10},{10... | collective-permute-start | bytes 3170312 | tf_op jit(solution)/shard_map/ppermute | solution.py:1624
  397.1 7.0 %collective-permute-start.4 = (f32[1,1024]{1,0:T(1,128)S(1)}, f32[1,1024]{1,0:T(1,128)S(1)}, u32[]{:S(2)}, u32[]{:S(2)}) collective-permute-start(f32[1,1024]{1,0:T(1,128)S(1)} %bitcast.63), channel_id=1, source_target_pairs={{0,16},{8,24},{16,0},{24,8},{1,17},{9,25},{17,1},{25,9},{2,18},{10... | collective-permute-start | bytes 12296 | tf_op jit(solution)/shard_map/ppermute | solution.py:1495
  404.0 34.1 %copy-start.20 = (bf16[688,768]{1,0:T(8,128)(2,1)}, bf16[688,768]{1,0:T(8,128)(2,1)S(1)}, u32[]{:S(2)}) copy-start(bf16[688,768]{1,0:T(8,128)(2,1)S(1)} %fusion.9.one_ref) | copy-start | bytes 3170308
  420.6 19.2 %copy-start.26 = (f32[6288]{0:T(1024)S(1)}, f32[6288]{0:T(1024)}, u32[]{:S(2)}) copy-start(f32[6288]{0:T(1024)} %param.40) | copy-start | bytes 75460
  420.6 19.3 %collective-permute-start.6 = (bf16[3168,768]{1,0:T(8,128)(2,1)}, bf16[3168,768]{1,0:T(8,128)(2,1)}, u32[]{:S(2)}, u32[]{:S(2)}) collective-permute-start(bf16[3168,768]{1,0:T(8,128)(2,1)} %shard_map.531.refs_0_), channel_id=1, source_target_pairs={{0,8},{8,0},{16,24},{24,16},{1,9},{9,1},{17,25},{25,17},{2,10},{10... | collective-permute-start | bytes 14598152 | tf_op jit(solution)/shard_map/ppermute | solution.py:1624
  437.7 17.7 %collective-permute-start.5 = (bf16[3168,768]{1,0:T(8,128)(2,1)}, bf16[3168,768]{1,0:T(8,128)(2,1)}, u32[]{:S(2)}, u32[]{:S(2)}) collective-permute-start(bf16[3168,768]{1,0:T(8,128)(2,1)} %shard_map.530.refs_0_), channel_id=1, source_target_pairs={{0,8},{8,0},{16,24},{24,16},{1,9},{9,1},{17,25},{25,17},{2,10},{10... | collective-permute-start | bytes 14598152 | tf_op jit(solution)/shard_map/ppermute | solution.py:1624
  438.2 30.6 %collective-permute-start.7 = (bf16[688,768]{1,0:T(8,128)(2,1)S(1)}, bf16[688,768]{1,0:T(8,128)(2,1)S(1)}, u32[]{:S(2)}, u32[]{:S(2)}) collective-permute-start(bf16[688,768]{1,0:T(8,128)(2,1)S(1)} %fusion.9.one_ref), channel_id=1, source_target_pairs={{0,16},{8,24},{16,0},{24,8},{1,17},{9,25},{17,1},{25,9},{2,18},{10... | collective-permute-start | bytes 3170312 | tf_op jit(solution)/shard_map/ppermute | solution.py:1495
  439.8 15.5 %slice-start = ((s8[4866048]{0:T(1024)(128)(4,1)}), s8[671744]{0:T(1024)(128)(4,1)S(1)}, s32[]{:S(2)}) async-start(s8[4866048]{0:T(1024)(128)(4,1)} %bitcast.55), calls=%async_computation | async-start | bytes 1343488
  439.9 15.4 %slice-start.1 = ((s8[4866048]{0:T(1024)(128)(4,1)}), s8[4194304]{0:T(1024)(128)(4,1)S(1)}, s32[]{:S(2)}) async-start(s8[4866048]{0:T(1024)(128)(4,1)} %bitcast.55), calls=%async_computation.1 | async-start | bytes 8388608
  468.6 17.1 %copy-start.3 = (f32[12,1,528]{2,1,0:T(1,128)}, f32[12,1,528]{2,1,0:T(1,128)S(1)}, u32[]{:S(2)}) copy-start(f32[12,1,528]{2,1,0:T(1,128)S(1)} %get-tuple-element.154.rows_ref.all_rows_ref) | copy-start | bytes 76036
  472.5 5.6 %collective-permute-start.8 = (bf16[688,768]{1,0:T(8,128)(2,1)}, bf16[688,768]{1,0:T(8,128)(2,1)S(1)}, u32[]{:S(2)}, u32[]{:S(2)}) collective-permute-start(bf16[688,768]{1,0:T(8,128)(2,1)} %shard_map.534.refs_0_), channel_id=1, source_target_pairs={{0,8},{8,0},{16,24},{24,16},{1,9},{9,1},{17,25},{25,17},{2,10},{10... | collective-permute-start | bytes 3170312 | tf_op jit(solution)/shard_map/ppermute | solution.py:1624
  (31 other events, 100.0 us)

commit v5 on v4

--- a/solution.py
+++ b/solution.py
@@ -499,7 +499,7 @@
         in_specs=[column(0), column(pairs), column(2 * pairs)],
         out_specs=[column(0), pl.BlockSpec((1, 2, length), lambda i: (i, 0, 0))],
         cost_estimate=cost(20 * length * length * width, 8 * length * width),
-        compiler_params=pltpu.CompilerParams(vmem_limit_bytes=40 * 1024 * 1024),
+        compiler_params=pltpu.CompilerParams(vmem_limit_bytes=40 * MEGA),
     )(packed, packed, packed)
 
 
@@ -897,7 +897,7 @@
         + [whole_block((1, 128))],
         input_output_aliases={len(sums) + 2: 0, len(sums) + 3: 1} if extra else {},
         cost_estimate=cost(0, (8 + 2 * len(sums)) * count * ROWS * width),
-        compiler_params=pltpu.CompilerParams(vmem_limit_bytes=48 * MEGA),
+        compiler_params=pltpu.CompilerParams(vmem_limit_bytes=58 * MEGA),
     )(*sums, noise, old, *extra)
 
 
@@ -1221,6 +1221,32 @@
     half = 0.5 + 0.5 * turn
     inner = GELU_SCALE + (3.0 * GELU_SCALE * 0.044715) * square
     return inputs * half, half + 0.5 * inputs * (1.0 - turn * turn) * inner
+
+
+def first_kernel(start_ref, weight_ref, bias_ref, small_ref, packed_ref, ones_ref):
+    @pl.when(pl.program_id(0) == 0)
+    def _():
+        for rows in chunks_of(start_ref.shape[0]):
+            normed = normed_of(start_ref[rows].astype(F32))[0]
+            ones_ref[rows] = (normed * small_ref[0:1] + small_ref[1:2]).astype(BF16)
+
+    for rows in chunks_of(start_ref.shape[0]):
+        packed_ref[rows] = (mm(ones_ref[rows], weight_ref[...]) + bias_ref[...]).astype(BF16)
+
+
+def first_forward(start, weight, bias, small):
+    length, width = start.shape
+    shape = jax.ShapeDtypeStruct
+    return pl.pallas_call(
+        first_kernel,
+        grid=(weight.shape[1] // width,),
+        out_shape=[shape((length, weight.shape[1]), BF16), shape((length, width), BF16)],
+        in_specs=[whole_block(start.shape), pl.BlockSpec((width, width), lambda i: (0, i))]
+        + [pl.BlockSpec((1, width), lambda i: (0, i)), whole_block(small.shape)],
+        out_specs=[pl.BlockSpec((length, width), lambda i: (0, i)), whole_block((length, width))],
+        cost_estimate=cost(2 * length * width * weight.shape[1], 4 * length * weight.shape[1]),
+        compiler_params=pltpu.CompilerParams(vmem_limit_bytes=40 * MEGA),
+    )(start, weight, bias, small)
 
 
 def middle_kernel(start_ref, mixed_ref, attn_ref, up_ref, bias_ref, down_ref, small_ref, *outs):
@@ -1521,9 +1547,8 @@
         qkv_full, attn_full, up_full = (gather_matrix(item, 0) for item in lows[:3])
         down_full = gather_matrix(lows[3], 1)
 
-    ln_one = (normed_of(stream_in.astype(F32))[0] * small[0] + small[1]).astype(BF16)
-    bias = jnp.concatenate([small[2], jnp.zeros_like(small[2]), small[3]])
-    packed = (mm(ln_one, qkv_full) + bias).astype(BF16)
+    bias = jnp.concatenate([small[2:3], jnp.zeros_like(small[2:3]), small[3:4]], 1)
+    packed, ln_one = first_forward(stream_in, qkv_full, bias, small)
     mixed, attn_log = attend(packed)
     up_bias = small[7:11].reshape(1, -1)
     stream_mid, ln_two, stream_out, ln_fin = middle_forward(

time: 536 us -> 534 us (level)
  Pallas kernels: 447 us -> 454 us
    pallas_call x0 -> x1, Pallas kernels: none -> 6.01 us  [first_forward(): pl.pallas_call(first_kernel, grid=(weight.shape[1] // width,), out_shape=...]
    unnamed x94 -> x92, local copies, waits for them, and re-layouts: 16.4 us -> 16 us
  transfers between devices with their start and end apart: 9 -> 9, of which waited for: 0 -> 0; matrix products, arithmetic and copies ran while one was open for 9% -> 7% of each run, Pallas kernels for 72% -> 74%
where the time goes in v5:
time: 534 us; the launch traced here: 527 us
  Pallas kernels  454 us (85%)
  other arithmetic  30.8 us (6%)
  local copies, waits for them, and re-layouts  24.7 us (5%)
  between operations  9.45 us (2%)
  starting transfers between devices  7.49 us (1%)
    pallas_call x1, Pallas kernels, front(): pl.pallas_call(functools.partial(front_kernel, n_row), out_shape=[shape((...  91.4 us
    pallas_call x1, Pallas kernels, plane_total(): pl.pallas_call(functools.partial(total_kernel, n_row), out_shape=jax.Shap...  50.1 us
    pallas_call x2, Pallas kernels, table_sum(): pl.pallas_call(functools.partial(table_sum_kernel, first), grid_spec=pltp...  33.5 us
    pallas_call x1, Pallas kernels, middle_back(): pl.pallas_call(middle_back_kernel, grid=(hidden // HIDDEN,), out_shape=[s...  33.4 us
    pallas_call x1, Pallas kernels, head_back(): pl.pallas_call(head_back_kernel, grid=(low.shape[0] // BLOCK,), out_shape...  29.1 us
    pallas_call x1, Pallas kernels, attend_back(): pl.pallas_call(attend_back_kernel, grid=(pairs,), out_shape=jax.ShapeDtyp...  27.4 us
    pallas_call x2, Pallas kernels, table_gradient(): pl.pallas_call(functools.partial(gradient_kernel, limit, len(sums), divis...  26.9 us
    pallas_call x1, Pallas kernels, update(): pl.pallas_call(update_kernel, grid=(blocks_of(limit),), out_shape=[shape(...  23.6 us
  transfers between devices with their start and end apart: 9, of which 0 were waited for; matrix products, arithmetic and copies ran while one was open for 7% of the time, Pallas kernels for 74%

profile of v5, /device:TPU:0, one launch (start us, length us, event | category | flops | bytes accessed | tf_op | source)
XLA Modules:
  0.0 526.6 jit_solution(11519832299441979237)
XLA Ops:
  1.5 3.0 collective-permute-start
  12.0 91.4 %shard_map.517 = (bf16[2,4,128,768]{3,2,1,0:T(8,128)(2,1)}, bf16[6336,768]{1,0:T(8,128)(2,1)}, f32[1,768]{1,0:T(1,128)}, bf16[4,2,2,48,2304]{4,3,2,1,0:T(8,128)(...) custom-call(s32[1024]{0:T(1024)} %bitcast.72, ...), custom_call_target="tpu_custom_call" | custom-call | tf_op jit(solution)/shard_map/pallas_call | solution.py:378
  106.7 6.0 %shard_map.518 = (bf16[1024,2304]{1,0:T(8,128)(2,1)S(1)}, bf16[1024,768]{1,0:T(8,128)(2,1)S(1)}) custom-call(bf16[1024,768]{1,0:T(8,128)(2,1)S(1)} %bitcast.60, bf16[768,2304]{1,0:T(8,128)(2,1)S(1)} %bitcast.57, f32[1,2304]{1,0:T(1,128)S(1)} %fusion.5.bias_ref, f32[14,768]{1,0:T(8,128)S(1)} %copy-done.3), custom_call_target="tpu_custom_call" | custom-call | flops 3623878656 | bytes 9437184 | tf_op jit(solution)/shard_map/pallas_call | solution.py:1240
  112.8 14.9 %shard_map.519 = (bf16[1024,768]{1,0:T(8,128)(2,1)S(1)}, f32[6,2,1024]{2,1,0:T(2,128)S(1)}) custom-call(bf16[1024,2304]{1,0:T(8,128)(2,1)S(1)} %get-tuple-element.117.q_ref.k_ref.v_ref, bf16[1024,2304]{1,0:T(8,128)(2,1)S(1)} %get-tuple-element.117.q_ref.k_ref.v_ref, bf16[1024,2304]{1,0:T(8,128)(2,1)S(1)} %get-tuple-element.117.q_ref.k_ref.v_ref), custom_call_target="tpu_custom_call" | custom-call | flops 16106127360 | bytes 6291456 | tf_op jit(solution)/shard_map/pallas_call | solution.py:492
  129.5 20.9 %shard_map.520 = (f32[1024,768]{1,0:T(8,128)}, bf16[1024,768]{1,0:T(8,128)(2,1)}, f32[1024,768]{1,0:T(8,128)}, bf16[1024,768]{1,0:T(8,128)(2,1)}) custom-call(bf16[1024,768]{1,0:T(8,128)(2,1)} %bitcast.58, bf16[1024,768]{1,0:T(8,128)(2,1)} %copy-done.1, bf16[768,768]{1,0:T(8,128)(2,1)} %bitcast.87, bf16[768,3072]{1,0:T(8,128)(2,1)} %bitcast.83, ...), custom_call_target="tpu_custom_call" | custom-call | flops 9663676416 | bytes 12582912 | tf_op jit(solution)/shard_map/pallas_call | solution.py:1287
  153.4 18.8 %shard_map.521 = (bf16[6336,1024]{1,0:T(8,128)(2,1)}, f32[18,1,1024]{2,1,0:T(1,128)S(1)}, f32[18,1,1024]{2,1,0:T(1,128)S(1)}, f32[1,1024]{1,0:T(1,128)S(1)}) custom-call(bf16[6336,768]{1,0:T(8,128)(2,1)} %get-tuple-element.114.low_ref.refs_0_, bf16[1024,768]{1,0:T(8,128)(2,1)S(1)} %copy-done.11, s32[1,1024]{1,0:T(1,128)S(1)} %and_select_fusion.1.target_ref), custom_call_target="tpu_custom_call" | custom-call | flops 9890168832 | bytes 22536192 | tf_op jit(solution)/shard_map/pallas_call | solution.py:708
  174.1 8.7 %shard_map.522 = (f32[8,128]{1,0:T(8,128)}, f32[8,128]{1,0:T(8,128)}) custom-call(f32[18,8,128]{2,1,0:T(8,128)} %bitcast.51, f32[18,8,128]{2,1,0:T(8,128)} %bitcast.52, f32[8,128]{1,0:T(8,128)} %bitcast.53), custom_call_target="tpu_custom_call" | custom-call | tf_op jit(solution)/shard_map/pallas_call | solution.py:630
  184.4 29.1 %shard_map.523 = (bf16[1024,768]{1,0:T(8,128)(2,1)S(1)}, bf16[6336,768]{1,0:T(8,128)(2,1)}) custom-call(bf16[6336,1024]{1,0:T(8,128)(2,1)} %get-tuple-element.123.exp_ref, f32[18,1,1024]{2,1,0:T(1,128)S(1)} %copy-done.5, f32[1,1024]{1,0:T(1,128)S(1)} %bitcast.54, s32[1,1024]{1,0:T(1,128)S(1)} %and_select_fusion.1.target_ref, ...), custom_call_target="tpu_custom_call" | custom-call | flops 19931332608 | bytes 32440320 | tf_op jit(solution)/shard_map/pallas_call | solution.py:748
  213.4 50.1 %shard_map.524 = bf16[2,4,128,768]{3,2,1,0:T(8,128)(2,1)S(1)} custom-call(bf16[2,4,128,768]{3,2,1,0:T(8,128)(2,1)S(1)} %bitcast.50), custom_call_target="tpu_custom_call" | custom-call | tf_op jit(solution)/shard_map/pallas_call | solution.py:428
  264.7 33.4 %shard_map.525 = (bf16[1024,768]{1,0:T(8,128)(2,1)}, bf16[1024,3072]{1,0:T(8,128)(2,1)}, bf16[1024,3072]{1,0:T(8,128)(2,1)}, f32[1,3072]{1,0:T(1,128)}, f32[1024...) custom-call(bf16[1024,768]{1,0:T(8,128)(2,1)} %bitcast.49, ...), custom_call_target="tpu_custom_call" | custom-call | flops 14495514624 | bytes 31457280 | tf_op jit(solution)/shard_map/pallas_call | solution.py:1356
  299.5 27.4 %shard_map.526.packed_ref.refs_0_.refs_1_.refs_2_ = bf16[3,1024,768]{2,1,0:T(8,128)(2,1)} custom-call(bf16[1024,2304]{1,0:T(8,128)(2,1)} %copy-done.14, bf16[1024,2304]{1,0:T(8,128)(2,1)} %copy-done.14, bf16[1024,2304]{1,0:T(8,128)(2,1)} %copy-done.14, bf16[1024,768]{1,0:T(8,128)(2,1)S(1)} %copy-done.15, f32[6,2,1024]{2,1,0:T(2,128)S(1)} %get-tuple-element.134.log_ref), custom_call_target="tpu_custom_call" | custom-call | flops 24159191040 | bytes 12582912 | tf_op jit(solution)/shard_map/pallas_call | solution.py:548
  326.9 11.5 %shard_map.527 = (f32[1024,768]{1,0:T(8,128)}, bf16[1024,768]{1,0:T(8,128)(2,1)}, f32[1024,768]{1,0:T(8,128)}, f32[8,768]{1,0:T(8,128)}) custom-call(bf16[3,1024,768]{2,1,0:T(8,128)(2,1)} %shard_map.526.packed_ref.refs_0_.refs_1_.refs_2_, bf16[768,2304]{1,0:T(8,128)(2,1)} %bitcast.56, f32[1024,768]{1,0:T(8,128)} %get-tuple-element.135.mid_grad_ref, ...), custom_call_target="tpu_custom_call" | custom-call | flops 3623878656 | bytes 15728640 | tf_op jit(solution)/shard_map/pallas_call | solution.py:1394
  347.0 11.2 %shard_map.529 = (f32[1376,768]{1,0:T(8,128)}, f32[1,384]{1,0:T(1,128)}) custom-call(s32[4]{0:T(128)} %pad_add_fusion.1.place_ref, bf16[1024,768]{1,0:T(8,128)(2,1)} %copy-done, bf16[1024,768]{1,0:T(8,128)(2,1)} %copy-done.1, bf16[1024,768]{1,0:T(8,128)(2,1)} %get-tuple-element.132.refs_3_.low_ref, ...), custom_call_target="tpu_custom_call" | custom-call | flops 2415919104 | bytes 12582912 | tf_op jit(solution)/shard_map/pallas_call | solution.py:1453
  362.9 11.4 %shard_map.528 = (bf16[6336,768]{1,0:T(8,128)(2,1)}, f32[1,768]{1,0:T(1,128)}) custom-call(s32[1024]{0:T(1024)} %broadcast_subtract_fusion.ids_ref, s32[1024]{0:T(1024)} %get-tuple-element.198.order_ref, s32[7]{0:T(128)} %get-tuple-element.202.bounds_ref, bf16[6336,768]{1,0:T(8,128)(2,1)} %get-tuple-element.128.table_ref, ...), custom_call_target="tpu_custom_call" | custom-call | bytes 19464192 | tf_op jit(solution)/shard_map/pallas_call | solution.py:801
  377.6 11.1 %shard_map.530 = f32[8,128]{1,0:T(8,128)} custom-call(f32[8,128]{1,0:T(8,128)} %fusion.6.value), custom_call_target="tpu_custom_call" | custom-call | tf_op jit(solution)/shard_map/pallas_call | solution.py:592
  390.6 3.2 multiply_convert_fusion
  400.9 16.6 %shard_map.532.refs_0_ = bf16[3168,768]{1,0:T(8,128)(2,1)} custom-call(s32[1024]{0:T(1024)S(1)} %broadcast_subtract_fusion.1.ids_ref, s32[1024]{0:T(1024)S(1)} %get-tuple-element.200.order_ref, s32[7]{0:T(128)S(1)} %get-tuple-element.203.bounds_ref, f32[2]{0:T(128)S(1)} %pad_maximum_fusion.share_ref, bf16[6336,768]{1,0:T(8,128)(2,1)} %get-tuple-element.114.low_ref.refs_0_, ...), custom_call_target="tpu_custom_call" | custom-call | flops 9965666304 | bytes 14598144 | tf_op jit(solution)/shard_map/pallas_call | solution.py:833
  417.5 16.9 %shard_map.531.refs_0_ = bf16[3168,768]{1,0:T(8,128)(2,1)} custom-call(s32[1024]{0:T(1024)S(1)} %broadcast_subtract_fusion.1.ids_ref, s32[1024]{0:T(1024)S(1)} %get-tuple-element.200.order_ref, s32[7]{0:T(128)S(1)} %get-tuple-element.203.bounds_ref, f32[2]{0:T(128)S(1)} %pad_maximum_fusion.share_ref, bf16[6336,768]{1,0:T(8,128)(2,1)} %get-tuple-element.114.low_ref.refs_0_, ...), custom_call_target="tpu_custom_call" | custom-call | flops 9965666304 | bytes 14598144 | tf_op jit(solution)/shard_map/pallas_call | solution.py:833
  437.2 13.5 %shard_map.533 = (f32[6288,768]{1,0:T(8,128)}, f32[12,1,528]{2,1,0:T(1,128)}, f32[1,768]{1,0:T(1,128)}, f32[1,768]{1,0:T(1,128)}, f32[1,128]{1,0:T(1,128)}) custom-call(bf16[3168,768]{1,0:T(8,128)(2,1)} %shard_map.532.refs_0_, bf16[3168,768]{1,0:T(8,128)(2,1)} %collective-permute-done.6.refs_1_, f32[6288,768]{1,0:T(8,128)} %refs_2_.5, ...), custom_call_target="tpu_custom_call" | custom-call | bytes 29196288 | tf_op jit(solution)/shard_map/pallas_call | solution.py:887
  450.9 13.4 %shard_map.534 = (f32[6288,768]{1,0:T(8,128)}, f32[12,1,528]{2,1,0:T(1,128)}, f32[1,768]{1,0:T(1,128)}, f32[1,768]{1,0:T(1,128)}, f32[1,128]{1,0:T(1,128)}) custom-call(bf16[3168,768]{1,0:T(8,128)(2,1)} %shard_map.531.refs_0_, bf16[3168,768]{1,0:T(8,128)(2,1)} %collective-permute-done.5.refs_1_, ...), custom_call_target="tpu_custom_call", output_to_operand_aliasing={{0}: (4, {}), {1}: (5, {})} | custom-call | bytes 29196288 | tf_op jit(solution)/shard_map/pallas_call | solution.py:887
  465.2 2.8 shard_map.535.refs_0_
  476.6 6.6 %shard_map.536 = (f32[192,512]{1,0:T(8,128)}, f32[192,1152]{1,0:T(8,128)}, f32[192,384]{1,0:T(8,128)}, f32[192,1536]{1,0:T(8,128)}, f32[384,768]{1,0:T(8,128)}, ...) custom-call(s32[1]{0:T(128)} %bitcast.30.core_ref, ...), custom_call_target="tpu_custom_call" | custom-call | bytes 16777216 | tf_op jit(solution)/shard_map/pallas_call | solution.py:1013
  485.1 15.2 %shard_map.537 = (f32[16,1536]{1,0:T(8,128)}, f32[8,768]{1,0:T(8,128)}) custom-call(f32[16,128]{1,0:T(8,128)} %pad.54.refs_0_, f32[16,128]{1,0:T(8,128)} %get-tuple-element.168.refs_1_, f32[32,128]{1,0:T(8,128)} %get-tuple-element.169.refs_2_, f32[16,1536]{1,0:T(8,128)} %stack.80.refs_3_, f32[192,512]{1,0:T(8,128)} %get-tuple-element.170.refs_4_.refs_5_, ...), custom_call_target="tpu_custom_call" | custom-call | tf_op jit(solution)/shard_map/pallas_call | solution.py:1103
  500.4 23.6 %shard_map.538 = (f32[6288,768]{1,0:T(8,128)}, f32[6288]{0:T(1024)}, f32[768]{0:T(1024)}, f32[192]{0:T(256)}, f32[192]{0:T(256)}, /*index=5*/f32[192]{0:T(256)},...) custom-call(f32[6288,768]{1,0:T(8,128)} %table_ref.1, ...), custom_call_target="tpu_custom_call" | custom-call | bytes 57950208 | tf_op jit(solution)/shard_map/pallas_call | solution.py:1173
  (182 shorter events, 56.8 us)
Async XLA Ops:
  1.5 360.7 %collective-permute-start = (s32[2,1024]{1,0:T(2,128)S(1)}, s32[2,1024]{1,0:T(2,128)S(1)}, u32[]{:S(2)}, u32[]{:S(2)}) collective-permute-start(s32[2,1024]{1,0:T(2,128)S(1)} %pad_add_fusion), channel_id=1, source_target_pairs={{0,16},{8,24},{16,0},{24,8},{1,17},{9,25},{17,1},{25,9},{2,18},{10... | collective-permute-start | bytes 24584 | tf_op jit(solution)/shard_map/ppermute | solution.py:1521
  11.9 91.4 %copy-start.3 = (f32[14,768]{1,0:T(8,128)S(1)}, f32[14,768]{1,0:T(8,128)}, u32[]{:S(2)}) copy-start(f32[14,768]{1,0:T(8,128)} %refs_2_.6) | copy-start | bytes 129028
  129.5 22.4 %copy-start.26 = (s32[1,1024]{1,0:T(1,128)S(1)}, s32[1,1024]{1,0:T(1,128)}, u32[]{:S(2)}) copy-start(s32[1,1024]{1,0:T(1,128)} %param.31) | copy-start | bytes 12292
  150.5 250.4 %collective-permute-start.3 = (bf16[1024,768]{1,0:T(8,128)(2,1)}, bf16[1024,768]{1,0:T(8,128)(2,1)S(1)}, u32[]{:S(2)}, u32[]{:S(2)}) collective-permute-start(bf16[1024,768]{1,0:T(8,128)(2,1)} %get-tuple-element.122.z_ref), channel_id=1, source_target_pairs={{0,16},{8,24},{16,0},{24,8},{1,17},{9,25},{17,1},{25,9},{2,18},{10... | collective-permute-start | bytes 4718600 | tf_op jit(solution)/shard_map/ppermute | solution.py:1521
  153.4 29.4 %copy-start.12 = (bf16[1024,768]{1,0:T(8,128)(2,1)S(1)}, bf16[1024,768]{1,0:T(8,128)(2,1)}, u32[]{:S(2)}) copy-start(bf16[1024,768]{1,0:T(8,128)(2,1)} %get-tuple-element.122.z_ref) | copy-start | bytes 4718596
  338.4 39.1 %collective-permute-start.1 = (bf16[1024,768]{1,0:T(8,128)(2,1)}, bf16[1024,768]{1,0:T(8,128)(2,1)S(1)}, u32[]{:S(2)}, u32[]{:S(2)}) collective-permute-start(bf16[1024,768]{1,0:T(8,128)(2,1)} %get-tuple-element.149), channel_id=1, source_target_pairs={{0,16},{8,24},{16,0},{24,8},{1,17},{9,25},{17,1},{25,9},{2,18},{10... | collective-permute-start | bytes 4718600 | tf_op jit(solution)/shard_map/ppermute | solution.py:1521
  395.5 3.9 collective-permute-start.2
  395.6 5.3 %collective-permute-start.4 = (f32[1,1024]{1,0:T(1,128)S(1)}, f32[1,1024]{1,0:T(1,128)S(1)}, u32[]{:S(2)}, u32[]{:S(2)}) collective-permute-start(f32[1,1024]{1,0:T(1,128)S(1)} %bitcast.55), channel_id=1, source_target_pairs={{0,16},{8,24},{16,0},{24,8},{1,17},{9,25},{17,1},{25,9},{2,18},{10... | collective-permute-start | bytes 12296 | tf_op jit(solution)/shard_map/ppermute | solution.py:1521
  400.9 34.1 %copy-start.19 = (bf16[688,768]{1,0:T(8,128)(2,1)}, bf16[688,768]{1,0:T(8,128)(2,1)S(1)}, u32[]{:S(2)}) copy-start(bf16[688,768]{1,0:T(8,128)(2,1)S(1)} %fusion.4.one_ref) | copy-start | bytes 3170308
  417.5 19.0 %copy-start.25 = (f32[6288]{0:T(1024)S(1)}, f32[6288]{0:T(1024)}, u32[]{:S(2)}) copy-start(f32[6288]{0:T(1024)} %param.40) | copy-start | bytes 75460
  417.5 19.7 %collective-permute-start.6 = (bf16[3168,768]{1,0:T(8,128)(2,1)}, bf16[3168,768]{1,0:T(8,128)(2,1)}, u32[]{:S(2)}, u32[]{:S(2)}) collective-permute-start(bf16[3168,768]{1,0:T(8,128)(2,1)} %shard_map.532.refs_0_), channel_id=1, source_target_pairs={{0,8},{8,0},{16,24},{24,16},{1,9},{9,1},{17,25},{25,17},{2,10},{10... | collective-permute-start | bytes 14598152 | tf_op jit(solution)/shard_map/ppermute | solution.py:1649
  434.4 16.3 %collective-permute-start.5 = (bf16[3168,768]{1,0:T(8,128)(2,1)}, bf16[3168,768]{1,0:T(8,128)(2,1)}, u32[]{:S(2)}, u32[]{:S(2)}) collective-permute-start(bf16[3168,768]{1,0:T(8,128)(2,1)} %shard_map.531.refs_0_), channel_id=1, source_target_pairs={{0,8},{8,0},{16,24},{24,16},{1,9},{9,1},{17,25},{25,17},{2,10},{10... | collective-permute-start | bytes 14598152 | tf_op jit(solution)/shard_map/ppermute | solution.py:1649
  435.0 29.3 %collective-permute-start.7 = (bf16[688,768]{1,0:T(8,128)(2,1)S(1)}, bf16[688,768]{1,0:T(8,128)(2,1)S(1)}, u32[]{:S(2)}, u32[]{:S(2)}) collective-permute-start(bf16[688,768]{1,0:T(8,128)(2,1)S(1)} %fusion.4.one_ref), channel_id=1, source_target_pairs={{0,16},{8,24},{16,0},{24,8},{1,17},{9,25},{17,1},{25,9},{2,18},{10... | collective-permute-start | bytes 3170312 | tf_op jit(solution)/shard_map/ppermute | solution.py:1521
  450.7 18.0 %copy-start.37 = (f32[384]{0:T(512)S(1)}, f32[384]{0:T(512)}, u32[]{:S(2)}) copy-start(f32[384]{0:T(512)} %param.50) | copy-start | bytes 4612
  450.7 18.0 %copy-start.31 = (f32[768]{0:T(1024)S(1)}, f32[768]{0:T(1024)}, u32[]{:S(2)}) copy-start(f32[768]{0:T(1024)} %param.41) | copy-start | bytes 9220
  450.8 18.1 %copy-start.38 = (f32[512]{0:T(512)S(1)}, f32[512]{0:T(512)}, u32[]{:S(2)}) copy-start(f32[512]{0:T(512)} %param.42) | copy-start | bytes 6148
  450.8 18.1 %copy-start.30 = (f32[1152]{0:T(1024)S(1)}, f32[1152]{0:T(1024)}, u32[]{:S(2)}) copy-start(f32[1152]{0:T(1024)} %param.45) | copy-start | bytes 13828
  450.8 18.1 %copy-start.39 = (f32[384]{0:T(512)S(1)}, f32[384]{0:T(512)}, u32[]{:S(2)}) copy-start(f32[384]{0:T(512)} %param.47) | copy-start | bytes 4612
  450.8 18.1 %copy-start.32 = (f32[768]{0:T(1024)S(1)}, f32[768]{0:T(1024)}, u32[]{:S(2)}) copy-start(f32[768]{0:T(1024)} %param.51) | copy-start | bytes 9220
  450.8 18.2 %copy-start.29 = (f32[1536]{0:T(1024)S(1)}, f32[1536]{0:T(1024)}, u32[]{:S(2)}) copy-start(f32[1536]{0:T(1024)} %param.49) | copy-start | bytes 18436
  450.8 22.7 %copy-start.36 = (f32[1,768]{1,0:T(1,128)S(1)}, f32[1,768]{1,0:T(1,128)}, u32[]{:S(2)}) copy-start(f32[1,768]{1,0:T(1,128)} %get-tuple-element.159) | copy-start | bytes 9220
  450.8 23.4 %copy-start.35 = (f32[1,768]{1,0:T(1,128)S(1)}, f32[1,768]{1,0:T(1,128)}, u32[]{:S(2)}) copy-start(f32[1,768]{1,0:T(1,128)} %get-tuple-element.161) | copy-start | bytes 9220
  450.8 24.1 %copy-start.44 = (f32[1,128]{1,0:T(1,128)S(1)}, f32[1,128]{1,0:T(1,128)}, u32[]{:S(2)}) copy-start(f32[1,128]{1,0:T(1,128)} %get-tuple-element.166) | copy-start | bytes 1540
  468.0 7.6 %collective-permute-start.8 = (bf16[688,768]{1,0:T(8,128)(2,1)}, bf16[688,768]{1,0:T(8,128)(2,1)S(1)}, u32[]{:S(2)}, u32[]{:S(2)}) collective-permute-start(bf16[688,768]{1,0:T(8,128)(2,1)} %shard_map.535.refs_0_), channel_id=1, source_target_pairs={{0,8},{8,0},{16,24},{24,16},{1,9},{9,1},{17,25},{25,17},{2,10},{10... | collective-permute-start | bytes 3170312 | tf_op jit(solution)/shard_map/ppermute | solution.py:1649
  (30 other events, 229.8 us)
